TPU v7x, 128 devices: a whole 4x4x4 slice. The times are simulated.
128 devices in a mesh: tm: 8 (over z, y_hi), space: 16 (over y_lo, x, core).
Axes of the slice: x: 4, y: 4 (y_hi: 2, y_lo: 2; y = y_hi * 2 + y_lo), z: 4, core: 2. Of those that a mesh axis runs over, the one named last changes fastest.
Arguments:
- right_side: float32 [128, 2048, 128], P('space', 'tm'), may hold values from -3 to 3
- blocks: float32 [128, 7, 128, 128], P('space'), may hold values from -0.1875 to 0.1875
- neighbors: int32 [128, 7], P('space'), may hold values from 0 to 127, as said below
- shift_rates: float32 [4], replicated, may hold values from 5 to 8
Outputs:
- correction: float32 [128, 2048, 128], P('space', 'tm')
Inputs may be any that keep to these rules, and one draw needn't show every extreme that they name: The elements form planes of 8 consecutive elements. neighbors[e, 0] = e. With q the plane of e, column 1 names an element of plane q - 1 and column 2 one of plane q + 1, cyclically over the planes; within a plane, each of these two columns names every element of the neighbouring plane exactly once. Columns 3 to 6 name elements of plane q.
All inputs are finite; a program needn't handle non-finite values.
Results may differ from a plain program's by a relative error of at most 0.0003.
Values sent between devices are 32-bit elements; how exact they have to be, the bound alone decides.
No kernel may reach another device: no remote copies, remote signals or barrier semaphores. Data moves between devices by JAX's collectives and lax.ppermute only.
A program may use at most 128 MiB of HBM per device.

v0:
```python
import math

import jax
import jax.numpy as jnp
from jax import lax
from jax.sharding import PartitionSpec as P

SWEEPS = 4


WRAP_WEIGHT = 0.01
DIAG_WEIGHT = 6.0
BLOCK_WEIGHT = 3.0
STEP_SCALE = 0.1
EXACT_DOTS = lax.Precision.HIGHEST


def extended_2(value, sides, width):
    for axis, dim in sides:
        devices, length = (lax.axis_size(axis), value.shape[dim])
        up = [(i, (i + 1) % devices) for i in range(devices)]
        down = [(j, i) for i, j in up]
        last = lax.slice_in_dim(value, length - width, length, axis=dim)
        initial = lax.slice_in_dim(value, 0, width, axis=dim)
        before = lax.ppermute(last, axis, up)
        after = lax.ppermute(initial, axis, down)
        value = jnp.concatenate([before, value, after], axis=dim)
    return value


def from_partner(block, axis, bit):
    count = lax.axis_size(axis)
    route = []
    for low in range(count):
        high = low | 1 << bit
        if high != low and high < count:
            route += [(low, high), (high, low)]
    return lax.ppermute(block, axis, route)


def reversed_bits(number, tm_bits):
    result = number * 0
    for bit_place in range(tm_bits):
        result = result + number // (1 << bit_place) % 2 * (1 << tm_bits - 1 - bit_place)
    return result


def complex_mul(a_real, a_imag, b_real, b_imag):
    return (a_real * b_real - a_imag * b_imag, a_real * b_imag + a_imag * b_real)


def block_product(gathered, weights):
    return lax.dot_general(
        gathered,
        weights,
        (((1, 4), (1, 3)), ((0,), (0,))),
        precision=EXACT_DOTS,
        preferred_element_type=jnp.float32,
    )


def operate(state, inner_blocks, rim_blocks, inner_index, prev_index, next_index):
    plane_size = state.shape[0]
    extended = extended_2(state, (("space", 0),), plane_size)
    inner = block_product(jnp.take(state, inner_index, axis=0), inner_blocks)
    before = jnp.take(extended[:plane_size], prev_index, axis=0)
    after = jnp.take(extended[2 * plane_size :], next_index, axis=0)
    rim = block_product(jnp.stack([before, after], 1), rim_blocks)
    return STEP_SCALE * (DIAG_WEIGHT * state + BLOCK_WEIGHT * (inner + rim))


def upper_flag(position, half_span):
    return (position // half_span % 2).astype(jnp.float32)


def forward_butterflies(scaled, position, tm_bits):
    top_bit = tm_bits - 1
    half_span = 1 << top_bit
    is_upper = upper_flag(position, half_span)
    partner = from_partner(scaled, "tm", top_bit)
    mixed = partner + (1.0 - 2.0 * is_upper) * scaled
    phases = is_upper * math.pi * (position % half_span).astype(jnp.float32) / half_span
    now_real = mixed * jnp.cos(phases)
    now_imag = -mixed * jnp.sin(phases)
    for bit_place in range(top_bit - 1, -1, -1):
        half_span = 1 << bit_place
        is_upper = upper_flag(position, half_span)
        other_real, other_imag = from_partner((now_real, now_imag), "tm", bit_place)
        sign_factor = 1.0 - 2.0 * is_upper
        mixed_real = other_real + sign_factor * now_real
        mixed_imag = other_imag + sign_factor * now_imag
        phases = is_upper * math.pi * (position % half_span).astype(jnp.float32) / half_span
        now_real, now_imag = complex_mul(mixed_real, mixed_imag, jnp.cos(phases), -jnp.sin(phases))
    return (now_real, now_imag)


def inverse_butterflies(now_real, now_imag, position, tm_bits):
    for bit_place in range(tm_bits):
        half_span = 1 << bit_place
        is_upper = upper_flag(position, half_span)
        other_real, other_imag = from_partner((now_real, now_imag), "tm", bit_place)
        low_real = now_real + is_upper * (other_real - now_real)
        low_imag = now_imag + is_upper * (other_imag - now_imag)
        high_real = other_real + is_upper * (now_real - other_real)
        high_imag = other_imag + is_upper * (now_imag - other_imag)
        phases = math.pi * (position % half_span).astype(jnp.float32) / half_span
        turned_real, turned_imag = complex_mul(
            high_real, high_imag, jnp.cos(phases), jnp.sin(phases)
        )
        sign_factor = 1.0 - 2.0 * is_upper
        now_real = 0.5 * (low_real + sign_factor * turned_real)
        now_imag = 0.5 * (low_imag + sign_factor * turned_imag)
    return now_real


def per_device(right_side, blocks, neighbors, shift_rates):
    plane_size, local_steps, node_count = right_side.shape
    tm_size = lax.axis_size("tm")
    tm_bits = tm_size.bit_length() - 1
    position = lax.axis_index("tm")
    length = local_steps * tm_size
    moments = jnp.arange(local_steps, dtype=jnp.int32)
    global_steps = (position * local_steps + moments).astype(jnp.float32)
    growth = jnp.exp(global_steps * (math.log(WRAP_WEIGHT) / length))
    scaled = right_side * growth[None, :, None]
    zero_flag = jnp.float32(0.0)
    slot_freq = reversed_bits(position, tm_bits) + tm_size * moments
    wave = (slot_freq[:, None] * moments[None, :] % length).astype(jnp.float32) * (
        2.0 * math.pi / length
    )
    cos_part = jnp.cos(wave)
    sin_part = jnp.sin(wave)
    now_real, now_imag = forward_butterflies(scaled, position, tm_bits)
    spec_real = jnp.einsum("km,emn->ekn", cos_part, now_real, precision=EXACT_DOTS) + jnp.einsum(
        "km,emn->ekn", sin_part, now_imag, precision=EXACT_DOTS
    )
    spec_imag = jnp.einsum("km,emn->ekn", cos_part, now_imag, precision=EXACT_DOTS) - jnp.einsum(
        "km,emn->ekn", sin_part, now_real, precision=EXACT_DOTS
    )
    local_index = neighbors % plane_size
    inner_index = jnp.concatenate([local_index[:, :1], local_index[:, 3:]], 1)
    prev_index = local_index[:, 1]
    next_index = local_index[:, 2]
    inner_blocks = jnp.concatenate([blocks[:, :1], blocks[:, 3:]], 1)
    rim_blocks = blocks[:, 1:3]
    decay_root = math.exp(math.log(WRAP_WEIGHT) / length)
    freq_phase = slot_freq.astype(jnp.float32) * (2.0 * math.pi / length)
    shift_rr = (1.0 - decay_root * jnp.cos(freq_phase))[None, :, None]
    shift_ri = shift_rr + zero_flag * (2.0 * decay_root)
    shift_im = (decay_root * jnp.sin(freq_phase))[None, :, None]
    iter_real = jnp.zeros_like(spec_real)
    iter_imag = jnp.zeros_like(spec_real)
    for sweep_index in range(SWEEPS):
        if sweep_index == 0:
            res_real = spec_real
            res_imag = spec_imag
        else:
            state = jnp.stack([iter_real, iter_imag], 1)
            applied = operate(state, inner_blocks, rim_blocks, inner_index, prev_index, next_index)
            res_real = spec_real - (shift_rr * iter_real - shift_im * iter_imag) - applied[:, 0]
            res_imag = spec_imag - (shift_ri * iter_imag + shift_im * iter_real) - applied[:, 1]
        den_first = shift_rr + STEP_SCALE * shift_rates[sweep_index]
        den_second = shift_ri + STEP_SCALE * shift_rates[sweep_index]
        determinant = den_first * den_second + shift_im * shift_im
        iter_real = iter_real + (den_second * res_real + shift_im * res_imag) / determinant
        iter_imag = iter_imag + (den_first * res_imag - shift_im * res_real) / determinant
    back_real = (
        jnp.einsum("km,ekn->emn", cos_part, iter_real, precision=EXACT_DOTS)
        - jnp.einsum("km,ekn->emn", sin_part, iter_imag, precision=EXACT_DOTS)
    ) / local_steps
    back_imag = (
        jnp.einsum("km,ekn->emn", cos_part, iter_imag, precision=EXACT_DOTS)
        + jnp.einsum("km,ekn->emn", sin_part, iter_real, precision=EXACT_DOTS)
    ) / local_steps
    series = inverse_butterflies(back_real, back_imag, position, tm_bits)
    return series / growth[None, :, None]


def solution(mesh):
    return jax.shard_map(
        per_device,
        mesh=mesh,
        in_specs=(P("space", "tm", None), P("space", None, None, None), P("space", None), P()),
        out_specs=P("space", "tm", None),
        check_vma=False,
    )
```

profile of v0, /device:TPU:6, one launch (start us, length us, event | category | flops | bytes accessed | tf_op | source)
XLA Modules:
  0.0 487.0 jit_solution(6856621507247625659)
XLA Ops:
  5.8 23.1 %collective-permute-done = f32[8,256,128]{1,2,0:T(8,128)} collective-permute-done((f32[8,256,128]{1,2,0:T(8,128)S(1)}, f32[8,256,128]{1,2,0:T(8,128)}, u32[]{:S(2)}, u32[]{:S(2)}) %collective-permute-start) | collective-permute-done | bytes 1048608 | tf_op jit(solution)/shard_map/ppermute | solution.py:38
  32.7 23.9 %collective-permute-done.1 = f32[8,256,128]{1,2,0:T(8,128)S(1)} collective-permute-done((f32[8,256,128]{1,2,0:T(8,128)S(1)}, f32[8,256,128]{1,2,0:T(8,128)S(1)}, u32[]{:S(2)}, u32[]{:S(2)}) %collective-permute-start.1) | collective-permute-done | bytes 1048608 | tf_op jit(solution)/shard_map/ppermute | solution.py:38
  57.5 19.9 %collective-permute-done.2 = f32[8,256,128]{1,2,0:T(8,128)} collective-permute-done((f32[8,256,128]{1,2,0:T(8,128)S(1)}, f32[8,256,128]{1,2,0:T(8,128)}, u32[]{:S(2)}, u32[]{:S(2)}) %collective-permute-start.2) | collective-permute-done | bytes 1048608 | tf_op jit(solution)/shard_map/ppermute | solution.py:38
  86.6 21.5 %collective-permute-done.3 = f32[8,256,128]{1,2,0:T(8,128)S(1)} collective-permute-done((f32[8,256,128]{1,2,0:T(8,128)}, f32[8,256,128]{1,2,0:T(8,128)S(1)}, u32[]{:S(2)}, u32[]{:S(2)}) %collective-permute-start.3) | collective-permute-done | bytes 1048608 | tf_op jit(solution)/shard_map/ppermute | solution.py:38
  108.1 19.8 %collective-permute-done.4 = f32[8,256,128]{1,2,0:T(8,128)S(1)} collective-permute-done((f32[8,256,128]{1,2,0:T(8,128)S(1)}, f32[8,256,128]{1,2,0:T(8,128)S(1)}, u32[]{:S(2)}, u32[]{:S(2)}) %collective-permute-start.4) | collective-permute-done | bytes 1048608 | tf_op jit(solution)/shard_map/ppermute | solution.py:38
  144.8 6.9 %gather_fusion = f32[40,2,256,128]{2,3,1,0:T(8,128)} fusion(f32[8,2,256,128]{2,3,0,1:T(8,128)S(1)} %pad_maximum_fusion, s32[1024]{0:T(1024)S(1)} %pad_clamp_fusion.2), kind=kCustom, calls=%fused_computation.clone | custom fusion | bytes 20971680 | tf_op jit(solution)/shard_map/jit(_take)/gather | solution.py:65
  151.7 11.3 %copy.6 = f32[8,5,2,256,128]{4,3,1,2,0:T(8,128)} copy(f32[8,5,2,256,128]{3,4,2,1,0:T(8,128)} %bitcast.141) | data formatting | bytes 20971520 | tf_op jit(solution)/shard_map/jit(_take)/gather | solution.py:65
  178.3 6.1 %fusion.33 = f32[8,2,256,128]{2,3,1,0:T(8,128)} fusion(f32[8,1,2,256,128]{3,4,2,0,1:T(8,128)S(1)} %select_bitcast_fusion.4, f32[8,1,2,256,128]{3,4,2,0,1:T(8,128)} %select_bitcast_fusion.5, f32[8,7,128,128]{3,2,1,0:T(8,128)} %param.9), kind=kOutput, calls=%fused_computation.54 | convolution fusion | flops 1611661312 | bytes 7340032 | tf_op jit(solution)/shard_map/dot_general | solution.py:53
  184.4 14.1 %fusion.26 = f32[8,2,256,128]{2,3,0,1:T(8,128)} fusion(f32[8,2,256,128]{2,3,1,0:T(8,128)} %fusion.33, f32[8,4,128,128]{3,2,1,0:T(8,128)S(1)} %copy-done.3, f32[8,1,128,128]{3,2,1,0:T(8,128)} %slice.59, f32[8,1,256,128]{2,3,0,1:T(8,128)} %copy-done.13, f32[8,1,256,128]{2,3,0,1:T(8,128)} %copy-done.12, f32[8,5,2,256,128]{4,3,1,2,0:T(8,128)S(1)} %copy-done.1, ...), kind=kOutput, calls=%fused_computation.45 | convolution fusion | flops 4032954368 | bytes 19398696 | tf_op jit(solution)/shard_map/dot_general | solution.py:53
  206.3 6.9 %gather_fusion.3 = f32[40,2,256,128]{2,3,1,0:T(8,128)} fusion(f32[8,2,256,128]{2,3,0,1:T(8,128)S(1)} %pad_maximum_fusion.1, s32[1024]{0:T(1024)S(1)} %pad_clamp_fusion.2), kind=kCustom, calls=%fused_computation.2.clone | custom fusion | bytes 20971680 | tf_op jit(solution)/shard_map/jit(_take)/gather | solution.py:65
  213.2 11.3 %copy.10 = f32[8,5,2,256,128]{4,3,1,2,0:T(8,128)} copy(f32[8,5,2,256,128]{3,4,2,1,0:T(8,128)} %bitcast.142) | data formatting | bytes 20971520 | tf_op jit(solution)/shard_map/jit(_take)/gather | solution.py:65
  241.2 6.1 %fusion.30 = f32[8,2,256,128]{2,3,1,0:T(8,128)} fusion(f32[8,1,2,256,128]{3,4,2,0,1:T(8,128)S(1)} %select_bitcast_fusion.2, f32[8,1,2,256,128]{3,4,2,0,1:T(8,128)} %select_bitcast_fusion.3, f32[8,7,128,128]{3,2,1,0:T(8,128)} %param.9), kind=kOutput, calls=%fused_computation.53 | convolution fusion | flops 1611661312 | bytes 7340032 | tf_op jit(solution)/shard_map/dot_general | solution.py:53
  247.3 14.1 %fusion.23 = f32[8,2,256,128]{2,3,0,1:T(8,128)} fusion(f32[8,2,256,128]{2,3,1,0:T(8,128)} %fusion.30, f32[8,4,128,128]{3,2,1,0:T(8,128)S(1)} %copy-done.4, f32[8,1,128,128]{3,2,1,0:T(8,128)} %slice.59, f32[8,1,256,128]{2,3,0,1:T(8,128)} %bitcast.146, f32[8,1,256,128]{2,3,0,1:T(8,128)} %bitcast.144, f32[8,5,2,256,128]{4,3,1,2,0:T(8,128)S(1)} %copy-done.2, ...), kind=kOutput, calls=%fused_computation.41 | convolution fusion | flops 4032954368 | bytes 19398696 | tf_op jit(solution)/shard_map/dot_general | solution.py:53
  268.4 6.9 %gather_fusion.6 = f32[40,2,256,128]{2,3,1,0:T(8,128)} fusion(f32[8,2,256,128]{2,3,0,1:T(8,128)S(1)} %pad_maximum_fusion.2, s32[1024]{0:T(1024)S(1)} %pad_clamp_fusion.2), kind=kCustom, calls=%fused_computation.3.clone | custom fusion | bytes 20971680 | tf_op jit(solution)/shard_map/jit(_take)/gather | solution.py:65
  275.3 11.3 %copy.14 = f32[8,5,2,256,128]{4,3,1,2,0:T(8,128)} copy(f32[8,5,2,256,128]{3,4,2,1,0:T(8,128)} %bitcast.140) | data formatting | bytes 20971520 | tf_op jit(solution)/shard_map/jit(_take)/gather | solution.py:65
  286.6 5.2 %collective-permute-done.9 = f32[8,2,256,128]{2,3,0,1:T(8,128)} collective-permute-done((f32[8,2,256,128]{2,3,0,1:T(8,128)S(1)}, f32[8,2,256,128]{2,3,0,1:T(8,128)}, u32[]{:S(2)}, u32[]{:S(2)}) %collective-permute-start.9) | collective-permute-done | bytes 2097184 | tf_op jit(solution)/shard_map/ppermute | solution.py:25
  304.5 6.1 %fusion.27 = f32[8,2,256,128]{2,3,1,0:T(8,128)} fusion(f32[8,1,2,256,128]{3,4,2,0,1:T(8,128)S(1)} %select_bitcast_fusion, f32[8,1,2,256,128]{3,4,2,0,1:T(8,128)} %select_bitcast_fusion.1, f32[8,7,128,128]{3,2,1,0:T(8,128)} %param.9), kind=kOutput, calls=%fused_computation.52 | convolution fusion | flops 1611661312 | bytes 7340032 | tf_op jit(solution)/shard_map/dot_general | solution.py:53
  310.6 14.3 %fusion.20 = f32[8,2,256,128]{2,3,0,1:T(8,128)} fusion(f32[8,2,256,128]{2,3,1,0:T(8,128)} %fusion.27, f32[8,4,128,128]{3,2,1,0:T(8,128)S(1)} %copy-done.5, f32[8,1,128,128]{3,2,1,0:T(8,128)} %slice.59, f32[8,1,256,128]{2,3,0,1:T(8,128)} %bitcast.150, f32[8,1,256,128]{2,3,0,1:T(8,128)} %bitcast.148, f32[8,5,2,256,128]{4,3,1,2,0:T(8,128)S(1)} %copy-done, ...), kind=kOutput, calls=%fused_computation.37 | convolution fusion | flops 4032954368 | bytes 19398696 | tf_op jit(solution)/shard_map/dot_general | solution.py:53
  340.3 19.5 %collective-permute-done.11 = f32[8,256,128]{1,2,0:T(8,128)S(1)} collective-permute-done((f32[8,256,128]{1,2,0:T(8,128)S(1)}, f32[8,256,128]{1,2,0:T(8,128)S(1)}, u32[]{:S(2)}, u32[]{:S(2)}) %collective-permute-start.11) | collective-permute-done | bytes 1048608 | tf_op jit(solution)/shard_map/ppermute | solution.py:38
  359.8 22.5 %collective-permute-done.12 = f32[8,256,128]{1,2,0:T(8,128)S(1)} collective-permute-done((f32[8,256,128]{1,2,0:T(8,128)S(1)}, f32[8,256,128]{1,2,0:T(8,128)S(1)}, u32[]{:S(2)}, u32[]{:S(2)}) %collective-permute-start.12) | collective-permute-done | bytes 1048608 | tf_op jit(solution)/shard_map/ppermute | solution.py:38
  385.3 22.6 %collective-permute-done.13 = f32[8,256,128]{1,2,0:T(8,128)S(1)} collective-permute-done((f32[8,256,128]{1,2,0:T(8,128)S(1)}, f32[8,256,128]{1,2,0:T(8,128)S(1)}, u32[]{:S(2)}, u32[]{:S(2)}) %collective-permute-start.13) | collective-permute-done | bytes 1048608 | tf_op jit(solution)/shard_map/ppermute | solution.py:38
  409.0 21.6 %collective-permute-done.14 = f32[8,256,128]{1,2,0:T(8,128)} collective-permute-done((f32[8,256,128]{1,2,0:T(8,128)S(1)}, f32[8,256,128]{1,2,0:T(8,128)}, u32[]{:S(2)}, u32[]{:S(2)}) %collective-permute-start.14) | collective-permute-done | bytes 1048608 | tf_op jit(solution)/shard_map/ppermute | solution.py:38
  437.0 23.8 %collective-permute-done.15 = f32[8,256,128]{1,2,0:T(8,128)S(1)} collective-permute-done((f32[8,256,128]{1,2,0:T(8,128)S(1)}, f32[8,256,128]{1,2,0:T(8,128)S(1)}, u32[]{:S(2)}, u32[]{:S(2)}) %collective-permute-start.15) | collective-permute-done | bytes 1048608 | tf_op jit(solution)/shard_map/ppermute | solution.py:38
  461.8 21.6 %collective-permute-done.16 = f32[8,256,128]{1,2,0:T(8,128)} collective-permute-done((f32[8,256,128]{1,2,0:T(8,128)S(1)}, f32[8,256,128]{1,2,0:T(8,128)}, u32[]{:S(2)}, u32[]{:S(2)}) %collective-permute-start.16) | collective-permute-done | bytes 1048608 | tf_op jit(solution)/shard_map/ppermute | solution.py:38
  (121 shorter events, 122.7 us)
Async XLA Ops:
  1.7 27.2 %collective-permute-start = (f32[8,256,128]{1,2,0:T(8,128)S(1)}, f32[8,256,128]{1,2,0:T(8,128)}, u32[]{:S(2)}, u32[]{:S(2)}) collective-permute-start(f32[8,256,128]{1,2,0:T(8,128)S(1)} %broadcast_multiply_fusion.1), channel_id=1, source_target_pairs={{0,64},{64,0},{16,80},{80,16},{32,96},{96,32},{48,112},{112,48},{1... | collective-permute-start | bytes 3145736 | tf_op jit(solution)/shard_map/ppermute | solution.py:38
  30.4 26.2 %collective-permute-start.1 = (f32[8,256,128]{1,2,0:T(8,128)S(1)}, f32[8,256,128]{1,2,0:T(8,128)S(1)}, u32[]{:S(2)}, u32[]{:S(2)}) collective-permute-start(f32[8,256,128]{1,2,0:T(8,128)S(1)} %get-tuple-element.28), channel_id=1, source_target_pairs={{0,32},{32,0},{16,48},{48,16},{64,96},{96,64},{80,112},{112,80},{1... | collective-permute-start | bytes 3145736 | tf_op jit(solution)/shard_map/ppermute | solution.py:38
  31.8 45.6 %collective-permute-start.2 = (f32[8,256,128]{1,2,0:T(8,128)S(1)}, f32[8,256,128]{1,2,0:T(8,128)}, u32[]{:S(2)}, u32[]{:S(2)}) collective-permute-start(f32[8,256,128]{1,2,0:T(8,128)S(1)} %get-tuple-element.27), channel_id=1, source_target_pairs={{0,32},{32,0},{16,48},{48,16},{64,96},{96,64},{80,112},{112,80},{1... | collective-permute-start | bytes 3145736 | tf_op jit(solution)/shard_map/ppermute | solution.py:38
  32.7 51.8 %copy-start.19 = (f32[4]{0:T(128)S(1)}, f32[4]{0:T(128)}, u32[]{:S(2)}) copy-start(f32[4]{0:T(128)} %param.11) | copy-start | bytes 52
  80.3 27.8 %collective-permute-start.3 = (f32[8,256,128]{1,2,0:T(8,128)}, f32[8,256,128]{1,2,0:T(8,128)S(1)}, u32[]{:S(2)}, u32[]{:S(2)}) collective-permute-start(f32[8,256,128]{1,2,0:T(8,128)} %get-tuple-element.24), channel_id=1, source_target_pairs={{0,16},{16,0},{32,48},{48,32},{64,80},{80,64},{96,112},{112,96},{1... | collective-permute-start | bytes 3145736 | tf_op jit(solution)/shard_map/ppermute | solution.py:38
  83.5 44.4 %collective-permute-start.4 = (f32[8,256,128]{1,2,0:T(8,128)S(1)}, f32[8,256,128]{1,2,0:T(8,128)S(1)}, u32[]{:S(2)}, u32[]{:S(2)}) collective-permute-start(f32[8,256,128]{1,2,0:T(8,128)S(1)} %get-tuple-element.23), channel_id=1, source_target_pairs={{0,16},{16,0},{32,48},{48,32},{64,80},{80,64},{96,112},{112,96},{1... | collective-permute-start | bytes 3145736 | tf_op jit(solution)/shard_map/ppermute | solution.py:38
  140.1 25.6 %collective-permute-start.5 = (f32[8,2,256,128]{2,3,0,1:T(8,128)S(1)}, f32[8,2,256,128]{2,3,0,1:T(8,128)}, u32[]{:S(2)}, u32[]{:S(2)}) collective-permute-start(f32[8,2,256,128]{2,3,0,1:T(8,128)S(1)} %pad_maximum_fusion), channel_id=1, source_target_pairs={{0,1},{1,2},{2,3},{3,4},{4,5},{5,6},{6,7},{7,8},{8,9},{9,10},{10,1... | collective-permute-start | bytes 6291464 | tf_op jit(solution)/shard_map/ppermute | solution.py:25
  140.1 32.3 %collective-permute-start.6 = (f32[8,2,256,128]{2,3,0,1:T(8,128)S(1)}, f32[8,2,256,128]{2,3,0,1:T(8,128)}, u32[]{:S(2)}, u32[]{:S(2)}) collective-permute-start(f32[8,2,256,128]{2,3,0,1:T(8,128)S(1)} %pad_maximum_fusion), channel_id=1, source_target_pairs={{1,0},{2,1},{3,2},{4,3},{5,4},{6,5},{7,6},{8,7},{9,8},{10,9},{11,1... | collective-permute-start | bytes 6291464 | tf_op jit(solution)/shard_map/ppermute | solution.py:26
  172.4 12.0 %copy-start.3 = (f32[8,4,128,128]{3,2,1,0:T(8,128)S(1)}, f32[8,4,128,128]{3,2,1,0:T(8,128)}, u32[]{:S(2)}) copy-start(f32[8,4,128,128]{3,2,1,0:T(8,128)} %slice.60) | copy-start | bytes 6291460
  176.2 8.2 %copy-start.1 = (f32[8,5,2,256,128]{4,3,1,2,0:T(8,128)S(1)}, f32[8,5,2,256,128]{4,3,1,2,0:T(8,128)}, u32[]{:S(2)}) copy-start(f32[8,5,2,256,128]{4,3,1,2,0:T(8,128)} %copy.6) | copy-start | bytes 31457284
  203.0 25.6 %collective-permute-start.7 = (f32[8,2,256,128]{2,3,0,1:T(8,128)S(1)}, f32[8,2,256,128]{2,3,0,1:T(8,128)}, u32[]{:S(2)}, u32[]{:S(2)}) collective-permute-start(f32[8,2,256,128]{2,3,0,1:T(8,128)S(1)} %pad_maximum_fusion.1), channel_id=1, source_target_pairs={{0,1},{1,2},{2,3},{3,4},{4,5},{5,6},{6,7},{7,8},{8,9},{9,10},{10,1... | collective-permute-start | bytes 6291464 | tf_op jit(solution)/shard_map/ppermute | solution.py:25
  203.0 32.3 %collective-permute-start.8 = (f32[8,2,256,128]{2,3,0,1:T(8,128)S(1)}, f32[8,2,256,128]{2,3,0,1:T(8,128)}, u32[]{:S(2)}, u32[]{:S(2)}) collective-permute-start(f32[8,2,256,128]{2,3,0,1:T(8,128)S(1)} %pad_maximum_fusion.1), channel_id=1, source_target_pairs={{1,0},{2,1},{3,2},{4,3},{5,4},{6,5},{7,6},{8,7},{9,8},{10,9},{11,1... | collective-permute-start | bytes 6291464 | tf_op jit(solution)/shard_map/ppermute | solution.py:26
  235.3 12.0 %copy-start.4 = (f32[8,4,128,128]{3,2,1,0:T(8,128)S(1)}, f32[8,4,128,128]{3,2,1,0:T(8,128)}, u32[]{:S(2)}) copy-start(f32[8,4,128,128]{3,2,1,0:T(8,128)} %slice.60) | copy-start | bytes 6291460
  239.1 8.2 %copy-start.2 = (f32[8,5,2,256,128]{4,3,1,2,0:T(8,128)S(1)}, f32[8,5,2,256,128]{4,3,1,2,0:T(8,128)}, u32[]{:S(2)}) copy-start(f32[8,5,2,256,128]{4,3,1,2,0:T(8,128)} %copy.10) | copy-start | bytes 31457284
  266.3 25.6 %collective-permute-start.9 = (f32[8,2,256,128]{2,3,0,1:T(8,128)S(1)}, f32[8,2,256,128]{2,3,0,1:T(8,128)}, u32[]{:S(2)}, u32[]{:S(2)}) collective-permute-start(f32[8,2,256,128]{2,3,0,1:T(8,128)S(1)} %pad_maximum_fusion.2), channel_id=1, source_target_pairs={{0,1},{1,2},{2,3},{3,4},{4,5},{5,6},{6,7},{7,8},{8,9},{9,10},{10,1... | collective-permute-start | bytes 6291464 | tf_op jit(solution)/shard_map/ppermute | solution.py:25
  267.4 31.2 %collective-permute-start.10 = (f32[8,2,256,128]{2,3,0,1:T(8,128)S(1)}, f32[8,2,256,128]{2,3,0,1:T(8,128)}, u32[]{:S(2)}, u32[]{:S(2)}) collective-permute-start(f32[8,2,256,128]{2,3,0,1:T(8,128)S(1)} %pad_maximum_fusion.2), channel_id=1, source_target_pairs={{1,0},{2,1},{3,2},{4,3},{5,4},{6,5},{7,6},{8,7},{9,8},{10,9},{11,1... | collective-permute-start | bytes 6291464 | tf_op jit(solution)/shard_map/ppermute | solution.py:26
  298.6 12.0 %copy-start.5 = (f32[8,4,128,128]{3,2,1,0:T(8,128)S(1)}, f32[8,4,128,128]{3,2,1,0:T(8,128)}, u32[]{:S(2)}) copy-start(f32[8,4,128,128]{3,2,1,0:T(8,128)} %slice.60) | copy-start | bytes 6291460
  334.5 25.3 %collective-permute-start.11 = (f32[8,256,128]{1,2,0:T(8,128)S(1)}, f32[8,256,128]{1,2,0:T(8,128)S(1)}, u32[]{:S(2)}, u32[]{:S(2)}) collective-permute-start(f32[8,256,128]{1,2,0:T(8,128)S(1)} %fusion.39), channel_id=1, source_target_pairs={{0,16},{16,0},{32,48},{48,32},{64,80},{80,64},{96,112},{112,96},{1... | collective-permute-start | bytes 3145736 | tf_op jit(solution)/shard_map/ppermute | solution.py:38
  339.9 42.4 %collective-permute-start.12 = (f32[8,256,128]{1,2,0:T(8,128)S(1)}, f32[8,256,128]{1,2,0:T(8,128)S(1)}, u32[]{:S(2)}, u32[]{:S(2)}) collective-permute-start(f32[8,256,128]{1,2,0:T(8,128)S(1)} %fusion.37), channel_id=1, source_target_pairs={{0,16},{16,0},{32,48},{48,32},{64,80},{80,64},{96,112},{112,96},{1... | collective-permute-start | bytes 3145736 | tf_op jit(solution)/shard_map/ppermute | solution.py:38
  383.1 24.9 %copy-start.15 = (f32[8,256,128]{1,2,0:T(8,128)}, f32[8,256,128]{1,2,0:T(8,128)S(1)}, u32[]{:S(2)}) copy-start(f32[8,256,128]{1,2,0:T(8,128)S(1)} %get-tuple-element.20) | copy-start | bytes 3145732
  383.1 24.9 %collective-permute-start.13 = (f32[8,256,128]{1,2,0:T(8,128)S(1)}, f32[8,256,128]{1,2,0:T(8,128)S(1)}, u32[]{:S(2)}, u32[]{:S(2)}) collective-permute-start(f32[8,256,128]{1,2,0:T(8,128)S(1)} %get-tuple-element.19), channel_id=1, source_target_pairs={{0,32},{32,0},{16,48},{48,16},{64,96},{96,64},{80,112},{112,80},{1... | collective-permute-start | bytes 3145736 | tf_op jit(solution)/shard_map/ppermute | solution.py:38
  383.8 46.7 %collective-permute-start.14 = (f32[8,256,128]{1,2,0:T(8,128)S(1)}, f32[8,256,128]{1,2,0:T(8,128)}, u32[]{:S(2)}, u32[]{:S(2)}) collective-permute-start(f32[8,256,128]{1,2,0:T(8,128)S(1)} %get-tuple-element.20), channel_id=1, source_target_pairs={{0,32},{32,0},{16,48},{48,16},{64,96},{96,64},{80,112},{112,80},{1... | collective-permute-start | bytes 3145736 | tf_op jit(solution)/shard_map/ppermute | solution.py:38
  433.3 27.6 %collective-permute-start.15 = (f32[8,256,128]{1,2,0:T(8,128)S(1)}, f32[8,256,128]{1,2,0:T(8,128)S(1)}, u32[]{:S(2)}, u32[]{:S(2)}) collective-permute-start(f32[8,256,128]{1,2,0:T(8,128)S(1)} %get-tuple-element.17), channel_id=1, source_target_pairs={{0,64},{64,0},{16,80},{80,16},{32,96},{96,32},{48,112},{112,48},{1... | collective-permute-start | bytes 3145736 | tf_op jit(solution)/shard_map/ppermute | solution.py:38
  436.0 47.4 %collective-permute-start.16 = (f32[8,256,128]{1,2,0:T(8,128)S(1)}, f32[8,256,128]{1,2,0:T(8,128)}, u32[]{:S(2)}, u32[]{:S(2)}) collective-permute-start(f32[8,256,128]{1,2,0:T(8,128)S(1)} %get-tuple-element.18), channel_id=1, source_target_pairs={{0,64},{64,0},{16,80},{80,16},{32,96},{96,32},{48,112},{112,48},{1... | collective-permute-start | bytes 3145736 | tf_op jit(solution)/shard_map/ppermute | solution.py:38
  (14 other events, 34.3 us)
where the time goes:
time: 492 us; the launch traced here: 487 us
  waiting for transfers between devices  252 us (51%)
  local copies, waits for them, and re-layouts  90.1 us (18%)
  matrix products  77.1 us (16%)
  other arithmetic  38.8 us (8%)
  starting transfers between devices  25.5 us (5%)
    ppermute x11, waiting for transfers between devices, from_partner(): return lax.ppermute(block, axis, route)  240 us
    dot_general x6, matrix products, block_product(): lax.dot_general(gathered, weights, (((1, 4), (1, 3)), ((0,), (0,))), prec...  60.8 us
    gather x6, local copies, waits for them, and re-layouts, operate(): inner = block_product(jnp.take(state, inner_index, axis=0), inner_blocks)  54.6 us
    ppermute x11, starting transfers between devices, from_partner(): return lax.ppermute(block, axis, route)  19.5 us
    another operation x6, other arithmetic, operate(): rim = block_product(jnp.stack([before, after], 1), rim_blocks)  15.7 us
    ppermute x3, waiting for transfers between devices, extended_2(): before = lax.ppermute(last, axis, up)  11.9 us
    gather x3, local copies, waits for them, and re-layouts, operate(): after = jnp.take(extended[2 * plane_size:], next_index, axis=0)  11.5 us
    gather x3, local copies, waits for them, and re-layouts, operate(): before = jnp.take(extended[:plane_size], prev_index, axis=0)  10.7 us
  transfers between devices with their start and end apart: 17, of which 14 were waited for; matrix products, arithmetic and copies ran while one was open for 17% of the time, Pallas kernels for 0%

commit v1 on v0

v1 whole, which is shorter than its diff:
```python
import functools
import math

import jax
import jax.numpy as jnp
import numpy as np
from jax import lax
from jax.experimental import pallas as pl
from jax.experimental.pallas import tpu as pltpu
from jax.sharding import PartitionSpec as P

SWEEPS = 4
LENGTH = 2048
CLASSES = 8
HALF = 128
NODES = 128
PLANE = 8
WRAP_WEIGHT = 0.01
DIAG_WEIGHT = 6.0
BLOCK_WEIGHT = 3.0
STEP_SCALE = 0.1
INNER_SLOTS = (0, 3, 4, 5, 6)
ROOT2 = math.sqrt(0.5)
VMEM_LIMIT = 48 * 1024 * 1024


def slot_frequencies(c):
    j = np.arange(HALF)
    return 8 * j if c == 0 else c + 16 * j


def transform_tables():
    m = np.arange(HALF)
    log_g = math.log(WRAP_WEIGHT) / LENGTH
    forward = np.zeros((CLASSES, 256, 256))
    inverse = np.zeros((CLASSES, 256, 256))
    for c in range(CLASSES):
        k = slot_frequencies(c)
        angle = 2.0 * np.pi * ((k[:, None] * m[None, :]) % LENGTH) / LENGTH
        cos, sin = np.cos(angle), np.sin(angle)
        if c:
            forward[c] = np.block([[cos, sin], [-sin, cos]])
            inverse[c] = np.block([[cos.T, -sin.T], [sin.T, cos.T]]) * (2.0 / LENGTH)
        else:
            even = (np.arange(HALF) % 2 == 0)[:, None]
            sign = np.where(m % 2 == 0, 1.0, -1.0)
            cos_even, cos_odd = cos * even, cos * ~even
            sin_even, sin_odd = sin * even, sin * ~even
            forward[c] = np.block([[cos_even, cos_odd], [-sin_even, -sin_odd]])
            forward[c, HALF, :HALF] = sign
            back = np.block([[cos_even.T, -sin_even.T], [cos_odd.T, -sin_odd.T]]) * (2.0 / LENGTH)
            back[:HALF, 0] = 1.0 / LENGTH
            back[:HALF, HALF] = sign / LENGTH
            inverse[c] = back
    growth = np.exp(log_g * m)
    forward *= np.tile(growth, 2)[None, None, :]
    inverse /= np.tile(growth, 2)[None, :, None]
    return forward, inverse


def shift_table():
    root = math.exp(math.log(WRAP_WEIGHT) / LENGTH)
    table = np.zeros((CLASSES, 3, HALF, NODES))
    for c in range(CLASSES):
        angle = 2.0 * np.pi * slot_frequencies(c) / LENGTH
        real = 1.0 - root * np.cos(angle)
        second = real.copy()
        if c == 0:
            second[0] = 1.0 + root
        table[c, 0] = real[:, None]
        table[c, 1] = second[:, None]
        table[c, 2] = (root * np.sin(angle))[:, None]
    return table.astype(np.float32)


def split_host(matrix):
    high = matrix.astype(jnp.bfloat16)
    low = (matrix - high.astype(np.float64)).astype(jnp.bfloat16)
    return high, low


def split(value):
    high = value.astype(jnp.bfloat16)
    return high, (value - high.astype(jnp.float32)).astype(jnp.bfloat16)


def dot(a, b):
    return jnp.dot(a, b, preferred_element_type=jnp.float32)


BLOCK_GROWTH = [math.exp(math.log(WRAP_WEIGHT) * q / 16.0) for q in range(16)]


def real_dft16(s):
    u = [s[r] + s[r + 8] for r in range(8)]
    w = [s[r] - s[r + 8] for r in range(8)]
    p = [u[r] + u[r + 4] for r in range(4)]
    t = [u[r] - u[r + 4] for r in range(4)]
    out = [None] * 8
    a, b = p[0] + p[2], p[1] + p[3]
    out[0] = (a + b, a - b)
    out[4] = (p[0] - p[2], p[3] - p[1])
    minus, plus = ROOT2 * (t[1] - t[3]), ROOT2 * (t[1] + t[3])
    out[2] = (t[0] + minus, -t[2] - plus)
    out[6] = (t[0] - minus, t[2] - plus)
    lower = [w[r] - w[8 - r] for r in (1, 2, 3)]
    upper = [w[r] + w[8 - r] for r in (1, 2, 3)]
    for c in (1, 3, 5, 7):
        real = w[0]
        imag = -w[4] if c % 4 == 1 else w[4]
        for r in (1, 2, 3):
            real = real + math.cos(math.pi * c * r / 8) * lower[r - 1]
            imag = imag - math.sin(math.pi * c * r / 8) * upper[r - 1]
        out[c] = (real, imag)
    return out


def real_idft16(v):
    (v0, v8), (r2, i2), (r4, i4), (r6, i6) = v[0], v[2], v[4], v[6]
    a, b = v0 + v8, v0 - v8
    ee = [a + r4, b - i4, a - r4, b + i4]
    x, y = r2 - r6, i2 + i6
    eo = [r2 + r6, ROOT2 * (x - y), i6 - i2, -ROOT2 * (x + y)]
    even = [ee[q] + eo[q] for q in range(4)] + [ee[q] - eo[q] for q in range(4)]
    odd = [None] * 8
    odd[0] = (v[1][0] + v[3][0]) + (v[5][0] + v[7][0])
    odd[4] = (v[3][1] - v[1][1]) + (v[7][1] - v[5][1])
    for q in (1, 2, 3):
        real = sum(math.cos(math.pi * c * q / 8) * v[c][0] for c in (1, 3, 5, 7))
        imag = sum(math.sin(math.pi * c * q / 8) * v[c][1] for c in (1, 3, 5, 7))
        odd[q] = real - imag
        odd[8 - q] = -real - imag
    return [even[q] + odd[q] for q in range(8)] + [even[q] - odd[q] for q in range(8)]


CHUNK = 16


def forward_kernel(x_ref, high_ref, low_ref, out_ref, z_ref):
    @pl.loop(0, HALF // CHUNK)
    def _(step):
        row = pl.multiple_of(step * CHUNK, CHUNK)
        series = [
            x_ref[q // 2, pl.ds(q % 2 * HALF + row, CHUNK), :] * BLOCK_GROWTH[q] for q in range(16)
        ]
        for c, pair in enumerate(real_dft16(series)):
            for part in range(2):
                high, low = split(pair[part])
                z_ref[c, pl.ds(part * HALF + row, CHUNK), :NODES] = high
                z_ref[c, pl.ds(part * HALF + row, CHUNK), NODES:] = low

    for c in range(CLASSES):
        both = dot(high_ref[c], z_ref[c])
        out_ref[c] = both[:, :NODES] + both[:, NODES:] + dot(low_ref[c], z_ref[c, :, :NODES])


def inverse_kernel(y_ref, high_ref, low_ref, out_ref, v_ref):
    for c in range(CLASSES):
        high, low = split(y_ref[c])
        both = dot(high_ref[c], jnp.concatenate([high, low], 1))
        v_ref[c] = both[:, :NODES] + both[:, NODES:] + dot(low_ref[c], high)

    @pl.loop(0, HALF // CHUNK)
    def _(step):
        row = pl.multiple_of(step * CHUNK, CHUNK)
        pairs = [
            (v_ref[c, pl.ds(row, CHUNK), :], v_ref[c, pl.ds(HALF + row, CHUNK), :])
            for c in range(CLASSES)
        ]
        for q, value in enumerate(real_idft16(pairs)):
            out_ref[q // 2, pl.ds(q % 2 * HALF + row, CHUNK), :] = value * (1.0 / BLOCK_GROWTH[q])


def weights_kernel(blocks_ref, inner_ref, rim_ref):
    for e in range(PLANE):
        for target, slots in ((inner_ref, INNER_SLOTS), (rim_ref, (1, 2))):
            for place, s in enumerate(slots):
                high, low = split(blocks_ref[e, s].T)
                target[e, place * NODES : (place + 1) * NODES, :NODES] = high
                target[e, place * NODES : (place + 1) * NODES, NODES:] = low


def solved(shift_ref, shift):
    first = shift_ref[0] + shift
    second = shift_ref[1] + shift
    imaginary = shift_ref[2]
    scale = 1.0 / (first * second + imaginary * imaginary)
    a, b, c = second * scale, imaginary * scale, first * scale
    return lambda real, imag: (a * real + b * imag, c * imag - b * real)


def first_kernel(rates_ref, spec_ref, shift_ref, out_ref):
    apply = solved(shift_ref, STEP_SCALE * rates_ref[0])

    @pl.loop(0, PLANE)
    def _(e):
        real, imag = apply(spec_ref[e, :HALF], spec_ref[e, HALF:])
        out_ref[e, :HALF] = real
        out_ref[e, HALF:] = imag


def inner_kernel(nb_ref, y_ref, weights_ref, out_ref, high_ref, low_ref):
    @pl.loop(0, PLANE)
    def _(e):
        high_ref[e], low_ref[e] = split(y_ref[e])

    @pl.loop(0, PLANE)
    def _(e):
        picked = [nb_ref[e, s] % PLANE for s in INNER_SLOTS]
        high = jnp.concatenate([high_ref[i] for i in picked], 1)
        low = jnp.concatenate([low_ref[i] for i in picked], 1)
        both = dot(high, weights_ref[e])
        out_ref[e] = both[:, :NODES] + both[:, NODES:] + dot(low, weights_ref[e, :, :NODES])


def rim_kernel(
    sweep, rates_ref, nb_ref, y_ref, inner_ref, before_ref, after_ref, spec_ref, shift_ref, weights_ref, out_ref
):
    shift = STEP_SCALE * rates_ref[sweep]
    apply = solved(shift_ref, shift)

    @pl.loop(0, PLANE)
    def _(e):
        before = before_ref[nb_ref[e, 1] % PLANE]
        after = after_ref[nb_ref[e, 2] % PLANE]
        high, low = split(jnp.concatenate([before, after], 1))
        both = dot(high, weights_ref[e])
        rim = both[:, :NODES] + both[:, NODES:] + dot(low, weights_ref[e, :, :NODES])
        right = (
            spec_ref[e]
            + (shift - STEP_SCALE * DIAG_WEIGHT) * y_ref[e]
            - (STEP_SCALE * BLOCK_WEIGHT) * (inner_ref[e] + rim)
        )
        real, imag = apply(right[:HALF], right[HALF:])
        out_ref[e, :HALF] = real
        out_ref[e, HALF:] = imag


def whole(count):
    return [pl.BlockSpec(memory_space=pltpu.VMEM)] * count


def scalars(count):
    return [pl.BlockSpec(memory_space=pltpu.SMEM)] * count


def call(kernel, outs, specs, flops, moved, scratch=()):
    return pl.pallas_call(
        kernel,
        out_shape=outs,
        in_specs=specs,
        out_specs=jax.tree.map(lambda _: pl.BlockSpec(memory_space=pltpu.VMEM), outs),
        scratch_shapes=scratch,
        compiler_params=pltpu.CompilerParams(vmem_limit_bytes=VMEM_LIMIT),
        cost_estimate=pl.CostEstimate(flops=flops, bytes_accessed=moved, transcendentals=0),
    )


STATE = jax.ShapeDtypeStruct((PLANE, 2 * HALF, NODES), jnp.float32)
MIB = 1 << 20


def per_device(right_side, blocks, neighbors, shift_rates):
    forward, inverse = transform_tables()
    forward_high, forward_low = (jnp.asarray(part) for part in split_host(forward))
    inverse_high, inverse_low = (jnp.asarray(part) for part in split_host(inverse))
    shifts = lax.dynamic_index_in_dim(
        jnp.asarray(shift_table()), lax.axis_index("tm"), 0, keepdims=False
    )
    ring = lax.axis_size("space")
    up = [(i, (i + 1) % ring) for i in range(ring)]
    down = [(j, i) for i, j in up]

    def exchange(value):
        return lax.all_to_all(value, "tm", 0, 0, tiled=True)

    inner_weights, rim_weights = call(
        weights_kernel,
        (
            jax.ShapeDtypeStruct((PLANE, 5 * NODES, 2 * NODES), jnp.bfloat16),
            jax.ShapeDtypeStruct((PLANE, 2 * NODES, 2 * NODES), jnp.bfloat16),
        ),
        whole(1),
        0,
        8 * MIB,
    )(blocks)
    steps = exchange(right_side)
    spectrum = call(
        forward_kernel,
        STATE,
        whole(3),
        10**9,
        4 * MIB,
        [pltpu.VMEM((CLASSES, 256, 256), jnp.bfloat16)],
    )(steps, forward_high, forward_low)
    spectrum = exchange(spectrum)
    state = call(first_kernel, STATE, scalars(1) + whole(2), 0, 2 * MIB)(
        shift_rates, spectrum, shifts
    )
    for sweep in range(1, SWEEPS):
        before = lax.ppermute(state, "space", up)
        after = lax.ppermute(state, "space", down)
        inner = call(
            inner_kernel,
            STATE,
            scalars(1) + whole(2),
            2 * 10**9,
            5 * MIB,
            [pltpu.VMEM((PLANE, 2 * HALF, NODES), jnp.bfloat16)] * 2,
        )(neighbors, state, inner_weights)
        state = call(
            functools.partial(rim_kernel, sweep),
            STATE,
            scalars(2) + whole(7),
            10**9,
            7 * MIB,
        )(shift_rates, neighbors, state, inner, before, after, spectrum, shifts, rim_weights)
    steps = call(
        inverse_kernel,
        STATE,
        whole(3),
        10**9,
        4 * MIB,
        [pltpu.VMEM((CLASSES, 256, 128), jnp.float32)],
    )(exchange(state), inverse_high, inverse_low)
    return exchange(steps)


def solution(mesh):
    return jax.shard_map(
        per_device,
        mesh=mesh,
        in_specs=(P("space", "tm", None), P("space", None, None, None), P("space", None), P()),
        out_specs=P("space", "tm", None),
        check_vma=False,
    )
```

time: 492 us -> 146 us (0.30)
  the two profiles are of different devices: /device:TPU:6 before, /device:TPU:0 now
where the time goes in v1:
time: 146 us
  blocking collectives  58.6 us (40%)
  waiting for transfers between devices  48.4 us (33%)
  Pallas kernels  28 us (19%)
  local copies, waits for them, and re-layouts  5.36 us (4%)
  starting transfers between devices  5.27 us (4%)
    all_to_all x3, blocking collectives, exchange(): return lax.all_to_all(value, 'tm', 0, 0, tiled=True)  58.6 us
    ppermute x3, waiting for transfers between devices, per_device(): after = lax.ppermute(state, 'space', down)  20.9 us
    all_to_all x1, waiting for transfers between devices, exchange(): return lax.all_to_all(value, 'tm', 0, 0, tiled=True)  15.3 us
    ppermute x3, waiting for transfers between devices, per_device(): before = lax.ppermute(state, 'space', up)  12.3 us
    pallas_call x3, Pallas kernels, per_device(): call(functools.partial(rim_kernel, sweep), STATE, scalars(2) + whole(7),...  10.7 us
    pallas_call x3, Pallas kernels, per_device(): call(inner_kernel, STATE, scalars(1) + whole(2), 2 * 10 ** 9, 5 * MIB, [p...  10.4 us
    unnamed x17, local copies, waits for them, and re-layouts  4.41 us
    all_to_all x1, starting transfers between devices, exchange(): return lax.all_to_all(value, 'tm', 0, 0, tiled=True)  3.56 us
  transfers between devices with their start and end apart: 7, of which 7 were waited for; matrix products, arithmetic and copies ran while one was open for 1% of the time, Pallas kernels for 9%

profile of v1, /device:TPU:0, one launch (start us, length us, event | category | flops | bytes accessed | tf_op | source)
XLA Modules:
  0.0 145.8 jit_solution(11518571220700758478)
XLA Ops:
  0.0 25.2 %all_to_all.20.x_ref = f32[8,256,128]{2,1,0:T(8,128)S(1)} all-to-all(f32[8,256,128]{2,1,0:T(8,128)} %param.9), channel_id=1, replica_groups=mesh['tm'=8,'space'=16] {'tm'}, dimensions={0} | all-to-all | bytes 2097152 | tf_op jit(solution)/shard_map/all_to_all | solution.py:275
  25.2 1.2 copy-done.4
  26.5 1.2 copy-done.5
  27.7 2.1 %shard_map.91 = f32[8,256,128]{2,1,0:T(8,128)} custom-call(f32[8,256,128]{2,1,0:T(8,128)S(1)} %all_to_all.20.x_ref, bf16[8,256,256]{2,1,0:T(8,128)(2,1)S(1)} %copy-done.5, bf16[8,256,256]{2,1,0:T(8,128)(2,1)S(1)} %copy-done.4), custom_call_target="tpu_custom_call" | custom-call | flops 1000000000 | bytes 4194304 | tf_op jit(solution)/shard_map/pallas_call | solution.py:288
  29.8 3.6 %all-to-all-start.1 = ((f32[8,256,128]{2,1,0:T(8,128)}), f32[8,256,128]{2,1,0:T(8,128)S(1)}, u32[]{:S(2)}, u32[]{:S(2)}) async-start(f32[8,256,128]{2,1,0:T(8,128)} %shard_map.91), calls=%async_computation.1 | async-start | bytes 2097152 | tf_op jit(solution)/shard_map/all_to_all | solution.py:275
  34.3 15.3 %all-to-all-done.1.spec_ref = f32[8,256,128]{2,1,0:T(8,128)S(1)} async-done(((f32[8,256,128]{2,1,0:T(8,128)}), f32[8,256,128]{2,1,0:T(8,128)S(1)}, u32[]{:S(2)}, u32[]{:S(2)}) %all-to-all-start.1) | async-done | bytes 1048608 | tf_op jit(solution)/shard_map/all_to_all | solution.py:275
  50.9 3.0 %shard_map.93 = (bf16[8,640,256]{2,1,0:T(8,128)(2,1)S(1)}, bf16[8,256,256]{2,1,0:T(8,128)(2,1)S(1)}) custom-call(f32[8,7,128,128]{3,2,1,0:T(8,128)} %blocks_ref.1), custom_call_target="tpu_custom_call" | custom-call | bytes 8388608 | tf_op jit(solution)/shard_map/pallas_call | solution.py:277
  53.9 1.0 copy-done.1
  54.9 3.5 %shard_map.94.inner_ref = f32[8,256,128]{2,1,0:T(8,128)S(1)} custom-call(s32[8,7]{1,0:T(8,128)S(1)} %copy-done.6, f32[8,256,128]{2,1,0:T(8,128)S(1)} %shard_map.92.y_ref, bf16[8,640,256]{2,1,0:T(8,128)(2,1)S(1)} %get-tuple-element.7.weights_ref), custom_call_target="tpu_custom_call" | custom-call | flops 2000000000 | bytes 5242880 | tf_op jit(solution)/shard_map/pallas_call | solution.py:303
  58.4 4.3 %collective-permute-done.1.after_ref = f32[8,256,128]{2,1,0:T(8,128)S(1)} collective-permute-done((f32[8,256,128]{2,1,0:T(8,128)S(1)}, f32[8,256,128]{2,1,0:T(8,128)S(1)}, u32[]{:S(2)}, u32[]{:S(2)}) %collective-permute-start.1) | collective-permute-done | bytes 1048608 | tf_op jit(solution)/shard_map/ppermute | solution.py:302
  62.7 4.1 %collective-permute-done.before_ref = f32[8,256,128]{2,1,0:T(8,128)S(1)} collective-permute-done((f32[8,256,128]{2,1,0:T(8,128)S(1)}, f32[8,256,128]{2,1,0:T(8,128)S(1)}, u32[]{:S(2)}, u32[]{:S(2)}) %collective-permute-start) | collective-permute-done | bytes 1048608 | tf_op jit(solution)/shard_map/ppermute | solution.py:301
  66.8 3.6 %shard_map.95.y_ref = f32[8,256,128]{2,1,0:T(8,128)S(1)} custom-call(f32[4]{0:T(128)S(1)} %copy-done.7, s32[8,7]{1,0:T(8,128)S(1)} %copy-done.6, f32[8,256,128]{2,1,0:T(8,128)S(1)} %shard_map.92.y_ref, f32[8,256,128]{2,1,0:T(8,128)S(1)} %shard_map.94.inner_ref, f32[8,256,128]{2,1,0:T(8,128)S(1)} %collective-permute-done.before_ref, ...), custom_call_target="tpu_custom_call" | custom-call | flops 1000000000 | bytes 7340032 | tf_op jit(solution)/shard_map/pallas_call | solution.py:311
  70.9 3.5 %shard_map.96.inner_ref = f32[8,256,128]{2,1,0:T(8,128)S(1)} custom-call(s32[8,7]{1,0:T(8,128)S(1)} %copy-done.6, f32[8,256,128]{2,1,0:T(8,128)S(1)} %shard_map.95.y_ref, bf16[8,640,256]{2,1,0:T(8,128)(2,1)S(1)} %get-tuple-element.7.weights_ref), custom_call_target="tpu_custom_call" | custom-call | flops 2000000000 | bytes 5242880 | tf_op jit(solution)/shard_map/pallas_call | solution.py:303
  74.4 8.3 %collective-permute-done.3.after_ref = f32[8,256,128]{2,1,0:T(8,128)S(1)} collective-permute-done((f32[8,256,128]{2,1,0:T(8,128)S(1)}, f32[8,256,128]{2,1,0:T(8,128)S(1)}, u32[]{:S(2)}, u32[]{:S(2)}) %collective-permute-start.3) | collective-permute-done | bytes 1048608 | tf_op jit(solution)/shard_map/ppermute | solution.py:302
  82.7 4.1 %collective-permute-done.2.before_ref = f32[8,256,128]{2,1,0:T(8,128)S(1)} collective-permute-done((f32[8,256,128]{2,1,0:T(8,128)S(1)}, f32[8,256,128]{2,1,0:T(8,128)S(1)}, u32[]{:S(2)}, u32[]{:S(2)}) %collective-permute-start.2) | collective-permute-done | bytes 1048608 | tf_op jit(solution)/shard_map/ppermute | solution.py:301
  86.8 3.6 %shard_map.97.y_ref = f32[8,256,128]{2,1,0:T(8,128)S(1)} custom-call(f32[4]{0:T(128)S(1)} %copy-done.7, s32[8,7]{1,0:T(8,128)S(1)} %copy-done.6, f32[8,256,128]{2,1,0:T(8,128)S(1)} %shard_map.95.y_ref, f32[8,256,128]{2,1,0:T(8,128)S(1)} %shard_map.96.inner_ref, f32[8,256,128]{2,1,0:T(8,128)S(1)} %collective-permute-done.2.before_ref, ...), custom_call_target="tpu_custom_call" | custom-call | flops 1000000000 | bytes 7340032 | tf_op jit(solution)/shard_map/pallas_call | solution.py:311
  91.0 3.5 %shard_map.98.inner_ref = f32[8,256,128]{2,1,0:T(8,128)S(1)} custom-call(s32[8,7]{1,0:T(8,128)S(1)} %copy-done.6, f32[8,256,128]{2,1,0:T(8,128)S(1)} %shard_map.97.y_ref, bf16[8,640,256]{2,1,0:T(8,128)(2,1)S(1)} %get-tuple-element.7.weights_ref), custom_call_target="tpu_custom_call" | custom-call | flops 2000000000 | bytes 5242880 | tf_op jit(solution)/shard_map/pallas_call | solution.py:303
  94.5 8.3 %collective-permute-done.5.after_ref = f32[8,256,128]{2,1,0:T(8,128)S(1)} collective-permute-done((f32[8,256,128]{2,1,0:T(8,128)S(1)}, f32[8,256,128]{2,1,0:T(8,128)S(1)}, u32[]{:S(2)}, u32[]{:S(2)}) %collective-permute-start.5) | collective-permute-done | bytes 1048608 | tf_op jit(solution)/shard_map/ppermute | solution.py:302
  102.8 4.1 %collective-permute-done.4.before_ref = f32[8,256,128]{2,1,0:T(8,128)S(1)} collective-permute-done((f32[8,256,128]{2,1,0:T(8,128)S(1)}, f32[8,256,128]{2,1,0:T(8,128)S(1)}, u32[]{:S(2)}, u32[]{:S(2)}) %collective-permute-start.4) | collective-permute-done | bytes 1048608 | tf_op jit(solution)/shard_map/ppermute | solution.py:301
  106.9 3.6 %shard_map.99 = f32[8,256,128]{2,1,0:T(8,128)S(1)} custom-call(f32[4]{0:T(128)S(1)} %copy-done.7, s32[8,7]{1,0:T(8,128)S(1)} %copy-done.6, f32[8,256,128]{2,1,0:T(8,128)S(1)} %shard_map.97.y_ref, f32[8,256,128]{2,1,0:T(8,128)S(1)} %shard_map.98.inner_ref, f32[8,256,128]{2,1,0:T(8,128)S(1)} %collective-permute-done.4.before_ref, ...), custom_call_target="tpu_custom_call" | custom-call | flops 1000000000 | bytes 7340032 | tf_op jit(solution)/shard_map/pallas_call | solution.py:311
  110.4 17.8 %all_to_all.21.y_ref = f32[8,256,128]{2,1,0:T(8,128)S(1)} all-to-all(f32[8,256,128]{2,1,0:T(8,128)S(1)} %shard_map.99), channel_id=1, replica_groups=mesh['tm'=8,'space'=16] {'tm'}, dimensions={0} | all-to-all | bytes 2097152 | tf_op jit(solution)/shard_map/all_to_all | solution.py:275
  128.2 1.0 shard_map.100
  129.3 15.5 %all_to_all.22 = f32[8,256,128]{2,1,0:T(8,128)S(1)} all-to-all(f32[8,256,128]{2,1,0:T(8,128)S(1)} %shard_map.100), channel_id=1, replica_groups=mesh['tm'=8,'space'=16] {'tm'}, dimensions={0} | all-to-all | bytes 2097152 | tf_op jit(solution)/shard_map/all_to_all | solution.py:275
  144.8 1.0 copy.11
  (21 shorter events, 3.4 us)
Async XLA Ops:
  25.2 1.2 copy-start.4
  26.5 1.2 copy-start.5
  27.7 21.9 %copy-start.7 = (f32[4]{0:T(128)S(1)}, f32[4]{0:T(128)}, u32[]{:S(2)}) copy-start(f32[4]{0:T(128)} %rates_ref.7) | copy-start | bytes 52
  29.8 19.8 %all-to-all-start.1 = ((f32[8,256,128]{2,1,0:T(8,128)}), f32[8,256,128]{2,1,0:T(8,128)S(1)}, u32[]{:S(2)}, u32[]{:S(2)}) async-start(f32[8,256,128]{2,1,0:T(8,128)} %shard_map.91), calls=%async_computation.1 | async-start | bytes 2097152 | tf_op jit(solution)/shard_map/all_to_all | solution.py:275
  34.3 20.6 %copy-start.6 = (s32[8,7]{1,0:T(8,128)S(1)}, s32[8,7]{1,0:T(8,128)}, u32[]{:S(2)}) copy-start(s32[8,7]{1,0:T(8,128)} %nb_ref.11) | copy-start | bytes 676
  49.6 4.4 %copy-start = (f32[8,256,128]{2,1,0:T(8,128)}, f32[8,256,128]{2,1,0:T(8,128)S(1)}, u32[]{:S(2)}) copy-start(f32[8,256,128]{2,1,0:T(8,128)S(1)} %all-to-all-done.1.spec_ref) | copy-start | bytes 3145732
  50.3 12.4 %collective-permute-start.1 = (f32[8,256,128]{2,1,0:T(8,128)S(1)}, f32[8,256,128]{2,1,0:T(8,128)S(1)}, u32[]{:S(2)}, u32[]{:S(2)}) collective-permute-start(f32[8,256,128]{2,1,0:T(8,128)S(1)} %shard_map.92.y_ref), channel_id=1, source_target_pairs={{1,0},{2,1},{3,2},{4,3},{5,4},{6,5},{7,6},{8,7},{9,8},{10,9},{11,1... | collective-permute-start | bytes 3145736 | tf_op jit(solution)/shard_map/ppermute | solution.py:302
  50.4 16.4 %collective-permute-start = (f32[8,256,128]{2,1,0:T(8,128)S(1)}, f32[8,256,128]{2,1,0:T(8,128)S(1)}, u32[]{:S(2)}, u32[]{:S(2)}) collective-permute-start(f32[8,256,128]{2,1,0:T(8,128)S(1)} %shard_map.92.y_ref), channel_id=1, source_target_pairs={{0,1},{1,2},{2,3},{3,4},{4,5},{5,6},{6,7},{7,8},{8,9},{9,10},{10,1... | collective-permute-start | bytes 3145736 | tf_op jit(solution)/shard_map/ppermute | solution.py:301
  53.9 1.0 copy-start.1
  70.3 12.4 %collective-permute-start.3 = (f32[8,256,128]{2,1,0:T(8,128)S(1)}, f32[8,256,128]{2,1,0:T(8,128)S(1)}, u32[]{:S(2)}, u32[]{:S(2)}) collective-permute-start(f32[8,256,128]{2,1,0:T(8,128)S(1)} %shard_map.95.y_ref), channel_id=1, source_target_pairs={{1,0},{2,1},{3,2},{4,3},{5,4},{6,5},{7,6},{8,7},{9,8},{10,9},{11,1... | collective-permute-start | bytes 3145736 | tf_op jit(solution)/shard_map/ppermute | solution.py:302
  70.4 16.4 %collective-permute-start.2 = (f32[8,256,128]{2,1,0:T(8,128)S(1)}, f32[8,256,128]{2,1,0:T(8,128)S(1)}, u32[]{:S(2)}, u32[]{:S(2)}) collective-permute-start(f32[8,256,128]{2,1,0:T(8,128)S(1)} %shard_map.95.y_ref), channel_id=1, source_target_pairs={{0,1},{1,2},{2,3},{3,4},{4,5},{5,6},{6,7},{7,8},{8,9},{9,10},{10,1... | collective-permute-start | bytes 3145736 | tf_op jit(solution)/shard_map/ppermute | solution.py:301
  90.4 12.4 %collective-permute-start.5 = (f32[8,256,128]{2,1,0:T(8,128)S(1)}, f32[8,256,128]{2,1,0:T(8,128)S(1)}, u32[]{:S(2)}, u32[]{:S(2)}) collective-permute-start(f32[8,256,128]{2,1,0:T(8,128)S(1)} %shard_map.97.y_ref), channel_id=1, source_target_pairs={{1,0},{2,1},{3,2},{4,3},{5,4},{6,5},{7,6},{8,7},{9,8},{10,9},{11,1... | collective-permute-start | bytes 3145736 | tf_op jit(solution)/shard_map/ppermute | solution.py:302
  90.5 16.4 %collective-permute-start.4 = (f32[8,256,128]{2,1,0:T(8,128)S(1)}, f32[8,256,128]{2,1,0:T(8,128)S(1)}, u32[]{:S(2)}, u32[]{:S(2)}) collective-permute-start(f32[8,256,128]{2,1,0:T(8,128)S(1)} %shard_map.97.y_ref), channel_id=1, source_target_pairs={{0,1},{1,2},{2,3},{3,4},{4,5},{5,6},{6,7},{7,8},{8,9},{9,10},{10,1... | collective-permute-start | bytes 3145736 | tf_op jit(solution)/shard_map/ppermute | solution.py:301
  94.5 33.8 %copy-start.2 = (bf16[8,256,256]{2,1,0:T(8,128)(2,1)S(1)}, bf16[8,256,256]{2,1,0:T(8,128)(2,1)}, u32[]{:S(2)}) copy-start(bf16[8,256,256]{2,1,0:T(8,128)(2,1)} %constant.25.clone.low_ref) | copy-start | bytes 3145732
  94.5 33.8 %copy-start.3 = (bf16[8,256,256]{2,1,0:T(8,128)(2,1)S(1)}, bf16[8,256,256]{2,1,0:T(8,128)(2,1)}, u32[]{:S(2)}) copy-start(bf16[8,256,256]{2,1,0:T(8,128)(2,1)} %constant.24.clone.high_ref) | copy-start | bytes 3145732

commit v2 on v1

--- a/solution.py
+++ b/solution.py
@@ -13,6 +13,9 @@
 LENGTH = 2048
 CLASSES = 8
 HALF = 128
+PARTS = 2
+SLOTS = HALF // PARTS
+ROWS = 2 * SLOTS
 NODES = 128
 PLANE = 8
 WRAP_WEIGHT = 0.01
@@ -55,7 +58,8 @@
     growth = np.exp(log_g * m)
     forward *= np.tile(growth, 2)[None, None, :]
     inverse /= np.tile(growth, 2)[None, :, None]
-    return forward, inverse
+    order = np.arange(256).reshape(2, PARTS, SLOTS).transpose(1, 0, 2).reshape(256)
+    return forward[:, order], inverse[:, :, order]
 
 
 def shift_table():
@@ -70,6 +74,7 @@
         table[c, 0] = real[:, None]
         table[c, 1] = second[:, None]
         table[c, 2] = (root * np.sin(angle))[:, None]
+    table = table.reshape(CLASSES, 3, PARTS, SLOTS, NODES).transpose(0, 2, 1, 3, 4)
     return table.astype(np.float32)
 
 
@@ -136,7 +141,9 @@
 CHUNK = 16
 
 
-def forward_kernel(x_ref, high_ref, low_ref, out_ref, z_ref):
+def forward_kernel(x_ref, high_ref, low_ref, *rest):
+    out_refs, z_ref = rest[:PARTS], rest[PARTS]
+
     @pl.loop(0, HALF // CHUNK)
     def _(step):
         row = pl.multiple_of(step * CHUNK, CHUNK)
@@ -151,12 +158,16 @@
 
     for c in range(CLASSES):
         both = dot(high_ref[c], z_ref[c])
-        out_ref[c] = both[:, :NODES] + both[:, NODES:] + dot(low_ref[c], z_ref[c, :, :NODES])
-
-
-def inverse_kernel(y_ref, high_ref, low_ref, out_ref, v_ref):
+        result = both[:, :NODES] + both[:, NODES:] + dot(low_ref[c], z_ref[c, :, :NODES])
+        for part in range(PARTS):
+            out_refs[part][c] = result[part * ROWS : (part + 1) * ROWS]
+
+
+def inverse_kernel(*refs):
+    y_refs = refs[:PARTS]
+    high_ref, low_ref, out_ref, v_ref = refs[PARTS:]
     for c in range(CLASSES):
-        high, low = split(y_ref[c])
+        high, low = split(jnp.concatenate([y_ref[c] for y_ref in y_refs], 0))
         both = dot(high_ref[c], jnp.concatenate([high, low], 1))
         v_ref[c] = both[:, :NODES] + both[:, NODES:] + dot(low_ref[c], high)
 
@@ -180,28 +191,27 @@
                 target[e, place * NODES : (place + 1) * NODES, NODES:] = low
 
 
-def solved(shift_ref, shift):
-    first = shift_ref[0] + shift
-    second = shift_ref[1] + shift
-    imaginary = shift_ref[2]
+def solved(shift_ref, part, shift):
+    first = shift_ref[part, 0] + shift
+    second = shift_ref[part, 1] + shift
+    imaginary = shift_ref[part, 2]
     scale = 1.0 / (first * second + imaginary * imaginary)
     a, b, c = second * scale, imaginary * scale, first * scale
     return lambda real, imag: (a * real + b * imag, c * imag - b * real)
 
 
-def first_kernel(rates_ref, spec_ref, shift_ref, out_ref):
-    apply = solved(shift_ref, STEP_SCALE * rates_ref[0])
+def first_kernel(part, rates_ref, spec_ref, shift_ref, out_ref):
+    apply = solved(shift_ref, part, STEP_SCALE * rates_ref[0])
 
     @pl.loop(0, PLANE)
     def _(e):
-        real, imag = apply(spec_ref[e, :HALF], spec_ref[e, HALF:])
-        out_ref[e, :HALF] = real
-        out_ref[e, HALF:] = imag
+        real, imag = apply(spec_ref[e, :SLOTS], spec_ref[e, SLOTS:])
+        out_ref[e, :SLOTS] = real
+        out_ref[e, SLOTS:] = imag
 
 
 def inner_kernel(nb_ref, y_ref, weights_ref, out_ref, high_ref, low_ref):
-    @pl.loop(0, PLANE)
-    def _(e):
+    for e in range(PLANE):
         high_ref[e], low_ref[e] = split(y_ref[e])
 
     @pl.loop(0, PLANE)
@@ -214,10 +224,21 @@
 
 
 def rim_kernel(
-    sweep, rates_ref, nb_ref, y_ref, inner_ref, before_ref, after_ref, spec_ref, shift_ref, weights_ref, out_ref
+    part,
+    sweep,
+    rates_ref,
+    nb_ref,
+    y_ref,
+    inner_ref,
+    before_ref,
+    after_ref,
+    spec_ref,
+    shift_ref,
+    weights_ref,
+    out_ref,
 ):
     shift = STEP_SCALE * rates_ref[sweep]
-    apply = solved(shift_ref, shift)
+    apply = solved(shift_ref, part, shift)
 
     @pl.loop(0, PLANE)
     def _(e):
@@ -231,9 +252,9 @@
             + (shift - STEP_SCALE * DIAG_WEIGHT) * y_ref[e]
             - (STEP_SCALE * BLOCK_WEIGHT) * (inner_ref[e] + rim)
         )
-        real, imag = apply(right[:HALF], right[HALF:])
-        out_ref[e, :HALF] = real
-        out_ref[e, HALF:] = imag
+        real, imag = apply(right[:SLOTS], right[SLOTS:])
+        out_ref[e, :SLOTS] = real
+        out_ref[e, SLOTS:] = imag
 
 
 def whole(count):
@@ -256,7 +277,8 @@
     )
 
 
-STATE = jax.ShapeDtypeStruct((PLANE, 2 * HALF, NODES), jnp.float32)
+STEPS = jax.ShapeDtypeStruct((PLANE, 2 * HALF, NODES), jnp.float32)
+STATE = jax.ShapeDtypeStruct((PLANE, ROWS, NODES), jnp.float32)
 MIB = 1 << 20
 
 
@@ -285,44 +307,62 @@
         8 * MIB,
     )(blocks)
     steps = exchange(right_side)
+    steps, inner_weights, rim_weights, shifts = lax.optimization_barrier(
+        (steps, inner_weights, rim_weights, shifts)
+    )
     spectrum = call(
         forward_kernel,
-        STATE,
+        (STATE,) * PARTS,
         whole(3),
         10**9,
         4 * MIB,
         [pltpu.VMEM((CLASSES, 256, 256), jnp.bfloat16)],
     )(steps, forward_high, forward_low)
-    spectrum = exchange(spectrum)
-    state = call(first_kernel, STATE, scalars(1) + whole(2), 0, 2 * MIB)(
-        shift_rates, spectrum, shifts
-    )
+    spectrum = [exchange(part) for part in spectrum]
+    states = [
+        call(functools.partial(first_kernel, part), STATE, scalars(1) + whole(2), 0, 2 * MIB // PARTS)(
+            shift_rates, spectrum[part], shifts
+        )
+        for part in range(PARTS)
+    ]
     for sweep in range(1, SWEEPS):
-        before = lax.ppermute(state, "space", up)
-        after = lax.ppermute(state, "space", down)
-        inner = call(
-            inner_kernel,
-            STATE,
-            scalars(1) + whole(2),
-            2 * 10**9,
-            5 * MIB,
-            [pltpu.VMEM((PLANE, 2 * HALF, NODES), jnp.bfloat16)] * 2,
-        )(neighbors, state, inner_weights)
-        state = call(
-            functools.partial(rim_kernel, sweep),
-            STATE,
-            scalars(2) + whole(7),
-            10**9,
-            7 * MIB,
-        )(shift_rates, neighbors, state, inner, before, after, spectrum, shifts, rim_weights)
+        for part in range(PARTS):
+            state = states[part]
+            before = lax.ppermute(state, "space", up)
+            after = lax.ppermute(state, "space", down)
+            inner = call(
+                inner_kernel,
+                STATE,
+                scalars(1) + whole(2),
+                2 * 10**9 // PARTS,
+                5 * MIB // PARTS,
+                [pltpu.VMEM((PLANE, ROWS, NODES), jnp.bfloat16)] * 2,
+            )(neighbors, state, inner_weights)
+            states[part] = call(
+                functools.partial(rim_kernel, part, sweep),
+                STATE,
+                scalars(2) + whole(7),
+                10**9 // PARTS,
+                7 * MIB // PARTS,
+            )(
+                shift_rates,
+                neighbors,
+                state,
+                inner,
+                before,
+                after,
+                spectrum[part],
+                shifts,
+                rim_weights,
+            )
     steps = call(
         inverse_kernel,
-        STATE,
-        whole(3),
+        STEPS,
+        whole(PARTS + 2),
         10**9,
         4 * MIB,
         [pltpu.VMEM((CLASSES, 256, 128), jnp.float32)],
-    )(exchange(state), inverse_high, inverse_low)
+    )(*[exchange(state) for state in states], inverse_high, inverse_low)
     return exchange(steps)
 
 

time: 146 us -> 158 us (1.082)
  the two profiles are of different devices: /device:TPU:0 before, /device:TPU:6 now
where the time goes in v2:
time: 158 us; the launch traced here: 156 us
  blocking collectives  49.2 us (31%)
  Pallas kernels  38 us (24%)
  starting transfers between devices  35.1 us (22%)
  waiting for transfers between devices  23 us (15%)
  local copies, waits for them, and re-layouts  10.6 us (7%)
    all_to_all x3, blocking collectives, exchange(): return lax.all_to_all(value, 'tm', 0, 0, tiled=True)  49.2 us
    all_to_all x3, waiting for transfers between devices, exchange(): return lax.all_to_all(value, 'tm', 0, 0, tiled=True)  23 us
    ppermute x6, starting transfers between devices, per_device(): before = lax.ppermute(state, 'space', up)  16.6 us
    pallas_call x6, Pallas kernels, per_device(): call(inner_kernel, STATE, scalars(1) + whole(2), 2 * 10 ** 9 // PARTS, 5...  15.8 us
    all_to_all x3, starting transfers between devices, exchange(): return lax.all_to_all(value, 'tm', 0, 0, tiled=True)  15.1 us
    pallas_call x6, Pallas kernels, per_device(): call(functools.partial(rim_kernel, part, sweep), STATE, scalars(2) + whol...  15 us
    unnamed x19, local copies, waits for them, and re-layouts  9.63 us
    ppermute x6, starting transfers between devices, per_device(): after = lax.ppermute(state, 'space', down)  3.48 us
  transfers between devices with their start and end apart: 15, of which 3 were waited for; matrix products, arithmetic and copies ran while one was open for 1% of the time, Pallas kernels for 22%

profile of v2, /device:TPU:6, one launch (start us, length us, event | category | flops | bytes accessed | tf_op | source)
XLA Modules:
  0.0 156.2 jit_solution(5288575139097846674)
XLA Ops:
  0.0 8.1 %all-to-all-start = ((f32[8,256,128]{2,1,0:T(8,128)}), f32[8,256,128]{2,1,0:T(8,128)S(1)}, u32[]{:S(2)}, u32[]{:S(2)}) async-start(f32[8,256,128]{2,1,0:T(8,128)} %param.9), calls=%async_computation | async-start | bytes 2097152 | tf_op jit(solution)/shard_map/all_to_all | solution.py:297
  8.1 3.0 %shard_map.91 = (bf16[8,640,256]{2,1,0:T(8,128)(2,1)S(1)}, bf16[8,256,256]{2,1,0:T(8,128)(2,1)S(1)}) custom-call(f32[8,7,128,128]{3,2,1,0:T(8,128)} %blocks_ref.1), custom_call_target="tpu_custom_call" | custom-call | bytes 8388608 | tf_op jit(solution)/shard_map/pallas_call | solution.py:299
  13.6 11.7 %all-to-all-done.x_ref = f32[8,256,128]{2,1,0:T(8,128)S(1)} async-done(((f32[8,256,128]{2,1,0:T(8,128)}), f32[8,256,128]{2,1,0:T(8,128)S(1)}, u32[]{:S(2)}, u32[]{:S(2)}) %all-to-all-start) | async-done | bytes 1048608 | tf_op jit(solution)/shard_map/all_to_all | solution.py:297
  28.4 14.4 %all_to_all.30.spec_ref = f32[8,128,128]{2,1,0:T(8,128)S(1)} all-to-all(f32[8,128,128]{2,1,0:T(8,128)S(1)} %get-tuple-element.20), channel_id=1, replica_groups=mesh['tm'=8,'space'=16] {'tm'}, dimensions={0} | all-to-all | bytes 1048576 | tf_op jit(solution)/shard_map/all_to_all | solution.py:297
  42.8 3.5 %all-to-all-start.1 = ((f32[8,128,128]{2,1,0:T(8,128)}), f32[8,128,128]{2,1,0:T(8,128)S(1)}, u32[]{:S(2)}, u32[]{:S(2)}) async-start(f32[8,128,128]{2,1,0:T(8,128)} %get-tuple-element.16), calls=%async_computation.1 | async-start | bytes 1048576 | tf_op jit(solution)/shard_map/all_to_all | solution.py:297
  48.8 8.1 %all-to-all-done.1.spec_ref = f32[8,128,128]{2,1,0:T(8,128)S(1)} async-done(((f32[8,128,128]{2,1,0:T(8,128)}), f32[8,128,128]{2,1,0:T(8,128)S(1)}, u32[]{:S(2)}, u32[]{:S(2)}) %all-to-all-start.1) | async-done | bytes 524320 | tf_op jit(solution)/shard_map/all_to_all | solution.py:297
  61.1 2.6 %shard_map.101.inner_ref = f32[8,128,128]{2,1,0:T(8,128)S(1)} custom-call(s32[8,7]{1,0:T(8,128)S(1)} %copy-done.2, f32[8,128,128]{2,1,0:T(8,128)S(1)} %shard_map.100.y_ref, bf16[8,640,256]{2,1,0:T(8,128)(2,1)S(1)} %copy-done.5), custom_call_target="tpu_custom_call" | custom-call | flops 1000000000 | bytes 2621440 | tf_op jit(solution)/shard_map/pallas_call | solution.py:333
  63.7 2.6 %shard_map.102.y_ref = f32[8,128,128]{2,1,0:T(8,128)S(1)} custom-call(f32[4]{0:T(128)S(1)} %copy-done.3, s32[8,7]{1,0:T(8,128)S(1)} %copy-done.2, f32[8,128,128]{2,1,0:T(8,128)S(1)} %shard_map.100.y_ref, f32[8,128,128]{2,1,0:T(8,128)S(1)} %shard_map.101.inner_ref, f32[8,128,128]{2,1,0:T(8,128)S(1)} %collective-permute-done.6.before_ref, ...), custom_call_target="tpu_custom_call" | custom-call | flops 500000000 | bytes 3670016 | tf_op jit(solution)/shard_map/pallas_call | solution.py:341
  66.4 4.6 %collective-permute-start.8 = (f32[8,128,128]{2,1,0:T(8,128)S(1)}, f32[8,128,128]{2,1,0:T(8,128)S(1)}, u32[]{:S(2)}, u32[]{:S(2)}) collective-permute-start(f32[8,128,128]{2,1,0:T(8,128)S(1)} %shard_map.102.y_ref), channel_id=1, source_target_pairs={{0,1},{1,2},{2,3},{3,4},{4,5},{5,6},{6,7},{7,8},{8,9},{9,10},{10,1... | collective-permute-start | bytes 1572872 | tf_op jit(solution)/shard_map/ppermute | solution.py:331
  71.0 2.6 %shard_map.94.inner_ref = f32[8,128,128]{2,1,0:T(8,128)S(1)} custom-call(s32[8,7]{1,0:T(8,128)S(1)} %copy-done.2, f32[8,128,128]{2,1,0:T(8,128)S(1)} %shard_map.93.y_ref, bf16[8,640,256]{2,1,0:T(8,128)(2,1)S(1)} %copy-done.5), custom_call_target="tpu_custom_call" | custom-call | flops 1000000000 | bytes 2621440 | tf_op jit(solution)/shard_map/pallas_call | solution.py:333
  73.7 2.2 %shard_map.95.y_ref = f32[8,128,128]{2,1,0:T(8,128)S(1)} custom-call(f32[4]{0:T(128)S(1)} %copy-done.3, s32[8,7]{1,0:T(8,128)S(1)} %copy-done.2, f32[8,128,128]{2,1,0:T(8,128)S(1)} %shard_map.93.y_ref, f32[8,128,128]{2,1,0:T(8,128)S(1)} %shard_map.94.inner_ref, f32[8,128,128]{2,1,0:T(8,128)S(1)} %collective-permute-done.before_ref, ...), custom_call_target="tpu_custom_call" | custom-call | flops 500000000 | bytes 3670016 | tf_op jit(solution)/shard_map/pallas_call | solution.py:341
  75.9 3.9 %collective-permute-start.2 = (f32[8,128,128]{2,1,0:T(8,128)S(1)}, f32[8,128,128]{2,1,0:T(8,128)S(1)}, u32[]{:S(2)}, u32[]{:S(2)}) collective-permute-start(f32[8,128,128]{2,1,0:T(8,128)S(1)} %shard_map.95.y_ref), channel_id=1, source_target_pairs={{0,1},{1,2},{2,3},{3,4},{4,5},{5,6},{6,7},{7,8},{8,9},{9,10},{10,1... | collective-permute-start | bytes 1572872 | tf_op jit(solution)/shard_map/ppermute | solution.py:331
  79.8 2.6 %shard_map.103.inner_ref = f32[8,128,128]{2,1,0:T(8,128)S(1)} custom-call(s32[8,7]{1,0:T(8,128)S(1)} %copy-done.2, f32[8,128,128]{2,1,0:T(8,128)S(1)} %shard_map.102.y_ref, bf16[8,640,256]{2,1,0:T(8,128)(2,1)S(1)} %copy-done.5), custom_call_target="tpu_custom_call" | custom-call | flops 1000000000 | bytes 2621440 | tf_op jit(solution)/shard_map/pallas_call | solution.py:333
  84.7 3.9 %collective-permute-start.10 = (f32[8,128,128]{2,1,0:T(8,128)S(1)}, f32[8,128,128]{2,1,0:T(8,128)S(1)}, u32[]{:S(2)}, u32[]{:S(2)}) collective-permute-start(f32[8,128,128]{2,1,0:T(8,128)S(1)} %shard_map.104.y_ref), channel_id=1, source_target_pairs={{0,1},{1,2},{2,3},{3,4},{4,5},{5,6},{6,7},{7,8},{8,9},{9,10},{10,1... | collective-permute-start | bytes 1572872 | tf_op jit(solution)/shard_map/ppermute | solution.py:331
  88.6 2.6 %shard_map.96.inner_ref = f32[8,128,128]{2,1,0:T(8,128)S(1)} custom-call(s32[8,7]{1,0:T(8,128)S(1)} %copy-done.2, f32[8,128,128]{2,1,0:T(8,128)S(1)} %shard_map.95.y_ref, bf16[8,640,256]{2,1,0:T(8,128)(2,1)S(1)} %copy-done.5), custom_call_target="tpu_custom_call" | custom-call | flops 1000000000 | bytes 2621440 | tf_op jit(solution)/shard_map/pallas_call | solution.py:333
  93.4 3.9 %collective-permute-start.4 = (f32[8,128,128]{2,1,0:T(8,128)S(1)}, f32[8,128,128]{2,1,0:T(8,128)}, u32[]{:S(2)}, u32[]{:S(2)}) collective-permute-start(f32[8,128,128]{2,1,0:T(8,128)S(1)} %shard_map.97.y_ref), channel_id=1, source_target_pairs={{0,1},{1,2},{2,3},{3,4},{4,5},{5,6},{6,7},{7,8},{8,9},{9,10},{10,1... | collective-permute-start | bytes 1572872 | tf_op jit(solution)/shard_map/ppermute | solution.py:331
  97.4 2.6 %shard_map.105.inner_ref = f32[8,128,128]{2,1,0:T(8,128)S(1)} custom-call(s32[8,7]{1,0:T(8,128)S(1)} %copy-done.2, f32[8,128,128]{2,1,0:T(8,128)S(1)} %shard_map.104.y_ref, bf16[8,640,256]{2,1,0:T(8,128)(2,1)S(1)} %copy-done.5), custom_call_target="tpu_custom_call" | custom-call | flops 1000000000 | bytes 2621440 | tf_op jit(solution)/shard_map/pallas_call | solution.py:333
  100.0 3.0 %shard_map.106 = f32[8,128,128]{2,1,0:T(8,128)} custom-call(f32[4]{0:T(128)S(1)} %copy-done.3, s32[8,7]{1,0:T(8,128)S(1)} %copy-done.2, f32[8,128,128]{2,1,0:T(8,128)S(1)} %shard_map.104.y_ref, f32[8,128,128]{2,1,0:T(8,128)S(1)} %shard_map.105.inner_ref, f32[8,128,128]{2,1,0:T(8,128)S(1)} %collective-permute-done.10.before_ref, ...), custom_call_target="tpu_custom_call" | custom-call | flops 500000000 | bytes 3670016 | tf_op jit(solution)/shard_map/pallas_call | solution.py:341
  103.0 3.5 %all-to-all-start.4 = ((f32[8,128,128]{2,1,0:T(8,128)}), f32[8,128,128]{2,1,0:T(8,128)S(1)}, u32[]{:S(2)}, u32[]{:S(2)}) async-start(f32[8,128,128]{2,1,0:T(8,128)} %shard_map.106), calls=%async_computation.4 | async-start | bytes 1048576 | tf_op jit(solution)/shard_map/all_to_all | solution.py:297
  108.3 2.6 %shard_map.98.inner_ref = f32[8,128,128]{2,1,0:T(8,128)S(1)} custom-call(s32[8,7]{1,0:T(8,128)S(1)} %copy-done.2, f32[8,128,128]{2,1,0:T(8,128)S(1)} %shard_map.97.y_ref, bf16[8,640,256]{2,1,0:T(8,128)(2,1)S(1)} %copy-done.6), custom_call_target="tpu_custom_call" | custom-call | flops 1000000000 | bytes 2621440 | tf_op jit(solution)/shard_map/pallas_call | solution.py:333
  110.9 2.8 %shard_map.99 = f32[8,128,128]{2,1,0:T(8,128)S(1)} custom-call(f32[4]{0:T(128)S(1)} %copy-done.3, s32[8,7]{1,0:T(8,128)S(1)} %copy-done.2, f32[8,128,128]{2,1,0:T(8,128)S(1)} %shard_map.97.y_ref, f32[8,128,128]{2,1,0:T(8,128)S(1)} %shard_map.98.inner_ref, f32[8,128,128]{2,1,0:T(8,128)} %collective-permute-done.4.before_ref, ...), custom_call_target="tpu_custom_call" | custom-call | flops 500000000 | bytes 3670016 | tf_op jit(solution)/shard_map/pallas_call | solution.py:341
  113.7 3.2 %all-to-all-done.4.refs_1_ = f32[8,128,128]{2,1,0:T(8,128)S(1)} async-done(((f32[8,128,128]{2,1,0:T(8,128)}), f32[8,128,128]{2,1,0:T(8,128)S(1)}, u32[]{:S(2)}, u32[]{:S(2)}) %all-to-all-start.4) | async-done | bytes 524320 | tf_op jit(solution)/shard_map/all_to_all | solution.py:297
  117.0 14.3 %all_to_all.31.refs_0_ = f32[8,128,128]{2,1,0:T(8,128)S(1)} all-to-all(f32[8,128,128]{2,1,0:T(8,128)S(1)} %shard_map.99), channel_id=1, replica_groups=mesh['tm'=8,'space'=16] {'tm'}, dimensions={0} | all-to-all | bytes 1048576 | tf_op jit(solution)/shard_map/all_to_all | solution.py:297
  134.7 20.5 %all_to_all.32 = f32[8,256,128]{2,1,0:T(8,128)S(1)} all-to-all(f32[8,256,128]{2,1,0:T(8,128)S(1)} %shard_map.107), channel_id=1, replica_groups=mesh['tm'=8,'space'=16] {'tm'}, dimensions={0} | all-to-all | bytes 2097152 | tf_op jit(solution)/shard_map/all_to_all | solution.py:297
  (46 shorter events, 22.7 us)
Async XLA Ops:
  0.0 25.3 %copy-start.7 = (bf16[8,256,256]{2,1,0:T(8,128)(2,1)S(1)}, bf16[8,256,256]{2,1,0:T(8,128)(2,1)}, u32[]{:S(2)}) copy-start(bf16[8,256,256]{2,1,0:T(8,128)(2,1)} %constant.22.clone.high_ref) | copy-start | bytes 3145732
  0.0 25.3 %all-to-all-start = ((f32[8,256,128]{2,1,0:T(8,128)}), f32[8,256,128]{2,1,0:T(8,128)S(1)}, u32[]{:S(2)}, u32[]{:S(2)}) async-start(f32[8,256,128]{2,1,0:T(8,128)} %param.9), calls=%async_computation | async-start | bytes 2097152 | tf_op jit(solution)/shard_map/all_to_all | solution.py:297
  11.1 1.5 copy-start.4
  25.3 1.2 copy-start.8
  26.5 19.8 %copy-start.3 = (f32[4]{0:T(128)S(1)}, f32[4]{0:T(128)}, u32[]{:S(2)}) copy-start(f32[4]{0:T(128)} %rates_ref.15) | copy-start | bytes 52
  28.4 30.9 %copy-start.2 = (s32[8,7]{1,0:T(8,128)S(1)}, s32[8,7]{1,0:T(8,128)}, u32[]{:S(2)}) copy-start(s32[8,7]{1,0:T(8,128)} %nb_ref.23) | copy-start | bytes 676
  42.8 14.0 %all-to-all-start.1 = ((f32[8,128,128]{2,1,0:T(8,128)}), f32[8,128,128]{2,1,0:T(8,128)S(1)}, u32[]{:S(2)}, u32[]{:S(2)}) async-start(f32[8,128,128]{2,1,0:T(8,128)} %get-tuple-element.16), calls=%async_computation.1 | async-start | bytes 1048576 | tf_op jit(solution)/shard_map/all_to_all | solution.py:297
  47.0 16.7 %collective-permute-start.6 = (f32[8,128,128]{2,1,0:T(8,128)S(1)}, f32[8,128,128]{2,1,0:T(8,128)S(1)}, u32[]{:S(2)}, u32[]{:S(2)}) collective-permute-start(f32[8,128,128]{2,1,0:T(8,128)S(1)} %shard_map.100.y_ref), channel_id=1, source_target_pairs={{0,1},{1,2},{2,3},{3,4},{4,5},{5,6},{6,7},{7,8},{8,9},{9,10},{10,1... | collective-permute-start | bytes 1572872 | tf_op jit(solution)/shard_map/ppermute | solution.py:331
  47.1 16.7 %collective-permute-start.7 = (f32[8,128,128]{2,1,0:T(8,128)S(1)}, f32[8,128,128]{2,1,0:T(8,128)}, u32[]{:S(2)}, u32[]{:S(2)}) collective-permute-start(f32[8,128,128]{2,1,0:T(8,128)S(1)} %shard_map.100.y_ref), channel_id=1, source_target_pairs={{1,0},{2,1},{3,2},{4,3},{5,4},{6,5},{7,6},{8,7},{9,8},{10,9},{11,1... | collective-permute-start | bytes 1572872 | tf_op jit(solution)/shard_map/ppermute | solution.py:332
  57.5 16.2 %collective-permute-start = (f32[8,128,128]{2,1,0:T(8,128)S(1)}, f32[8,128,128]{2,1,0:T(8,128)S(1)}, u32[]{:S(2)}, u32[]{:S(2)}) collective-permute-start(f32[8,128,128]{2,1,0:T(8,128)S(1)} %shard_map.93.y_ref), channel_id=1, source_target_pairs={{0,1},{1,2},{2,3},{3,4},{4,5},{5,6},{6,7},{7,8},{8,9},{9,10},{10,1... | collective-permute-start | bytes 1572872 | tf_op jit(solution)/shard_map/ppermute | solution.py:331
  57.6 16.1 %collective-permute-start.1 = (f32[8,128,128]{2,1,0:T(8,128)S(1)}, f32[8,128,128]{2,1,0:T(8,128)S(1)}, u32[]{:S(2)}, u32[]{:S(2)}) collective-permute-start(f32[8,128,128]{2,1,0:T(8,128)S(1)} %shard_map.93.y_ref), channel_id=1, source_target_pairs={{1,0},{2,1},{3,2},{4,3},{5,4},{6,5},{7,6},{8,7},{9,8},{10,9},{11,1... | collective-permute-start | bytes 1572872 | tf_op jit(solution)/shard_map/ppermute | solution.py:332
  59.3 1.7 %copy-start.5 = (bf16[8,640,256]{2,1,0:T(8,128)(2,1)S(1)}, bf16[8,640,256]{2,1,0:T(8,128)(2,1)}, u32[]{:S(2)}) copy-start(bf16[8,640,256]{2,1,0:T(8,128)(2,1)} %copy-done.4) | copy-start | bytes 7864324
  66.4 16.1 %collective-permute-start.8 = (f32[8,128,128]{2,1,0:T(8,128)S(1)}, f32[8,128,128]{2,1,0:T(8,128)S(1)}, u32[]{:S(2)}, u32[]{:S(2)}) collective-permute-start(f32[8,128,128]{2,1,0:T(8,128)S(1)} %shard_map.102.y_ref), channel_id=1, source_target_pairs={{0,1},{1,2},{2,3},{3,4},{4,5},{5,6},{6,7},{7,8},{8,9},{9,10},{10,1... | collective-permute-start | bytes 1572872 | tf_op jit(solution)/shard_map/ppermute | solution.py:331
  71.0 11.4 %collective-permute-start.9 = (f32[8,128,128]{2,1,0:T(8,128)S(1)}, f32[8,128,128]{2,1,0:T(8,128)S(1)}, u32[]{:S(2)}, u32[]{:S(2)}) collective-permute-start(f32[8,128,128]{2,1,0:T(8,128)S(1)} %shard_map.102.y_ref), channel_id=1, source_target_pairs={{1,0},{2,1},{3,2},{4,3},{5,4},{6,5},{7,6},{8,7},{9,8},{10,9},{11,1... | collective-permute-start | bytes 1572872 | tf_op jit(solution)/shard_map/ppermute | solution.py:332
  75.9 15.4 %collective-permute-start.2 = (f32[8,128,128]{2,1,0:T(8,128)S(1)}, f32[8,128,128]{2,1,0:T(8,128)S(1)}, u32[]{:S(2)}, u32[]{:S(2)}) collective-permute-start(f32[8,128,128]{2,1,0:T(8,128)S(1)} %shard_map.95.y_ref), channel_id=1, source_target_pairs={{0,1},{1,2},{2,3},{3,4},{4,5},{5,6},{6,7},{7,8},{8,9},{9,10},{10,1... | collective-permute-start | bytes 1572872 | tf_op jit(solution)/shard_map/ppermute | solution.py:331
  79.8 11.4 %collective-permute-start.3 = (f32[8,128,128]{2,1,0:T(8,128)S(1)}, f32[8,128,128]{2,1,0:T(8,128)S(1)}, u32[]{:S(2)}, u32[]{:S(2)}) collective-permute-start(f32[8,128,128]{2,1,0:T(8,128)S(1)} %shard_map.95.y_ref), channel_id=1, source_target_pairs={{1,0},{2,1},{3,2},{4,3},{5,4},{6,5},{7,6},{8,7},{9,8},{10,9},{11,1... | collective-permute-start | bytes 1572872 | tf_op jit(solution)/shard_map/ppermute | solution.py:332
  84.7 15.3 %collective-permute-start.10 = (f32[8,128,128]{2,1,0:T(8,128)S(1)}, f32[8,128,128]{2,1,0:T(8,128)S(1)}, u32[]{:S(2)}, u32[]{:S(2)}) collective-permute-start(f32[8,128,128]{2,1,0:T(8,128)S(1)} %shard_map.104.y_ref), channel_id=1, source_target_pairs={{0,1},{1,2},{2,3},{3,4},{4,5},{5,6},{6,7},{7,8},{8,9},{9,10},{10,1... | collective-permute-start | bytes 1572872 | tf_op jit(solution)/shard_map/ppermute | solution.py:331
  88.6 11.4 %collective-permute-start.11 = (f32[8,128,128]{2,1,0:T(8,128)S(1)}, f32[8,128,128]{2,1,0:T(8,128)S(1)}, u32[]{:S(2)}, u32[]{:S(2)}) collective-permute-start(f32[8,128,128]{2,1,0:T(8,128)S(1)} %shard_map.104.y_ref), channel_id=1, source_target_pairs={{1,0},{2,1},{3,2},{4,3},{5,4},{6,5},{7,6},{8,7},{9,8},{10,9},{11,1... | collective-permute-start | bytes 1572872 | tf_op jit(solution)/shard_map/ppermute | solution.py:332
  93.4 17.5 %collective-permute-start.4 = (f32[8,128,128]{2,1,0:T(8,128)S(1)}, f32[8,128,128]{2,1,0:T(8,128)}, u32[]{:S(2)}, u32[]{:S(2)}) collective-permute-start(f32[8,128,128]{2,1,0:T(8,128)S(1)} %shard_map.97.y_ref), channel_id=1, source_target_pairs={{0,1},{1,2},{2,3},{3,4},{4,5},{5,6},{6,7},{7,8},{8,9},{9,10},{10,1... | collective-permute-start | bytes 1572872 | tf_op jit(solution)/shard_map/ppermute | solution.py:331
  97.4 13.6 %collective-permute-start.5 = (f32[8,128,128]{2,1,0:T(8,128)S(1)}, f32[8,128,128]{2,1,0:T(8,128)}, u32[]{:S(2)}, u32[]{:S(2)}) collective-permute-start(f32[8,128,128]{2,1,0:T(8,128)S(1)} %shard_map.97.y_ref), channel_id=1, source_target_pairs={{1,0},{2,1},{3,2},{4,3},{5,4},{6,5},{7,6},{8,7},{9,8},{10,9},{11,1... | collective-permute-start | bytes 1572872 | tf_op jit(solution)/shard_map/ppermute | solution.py:332
  103.0 14.0 %all-to-all-start.4 = ((f32[8,128,128]{2,1,0:T(8,128)}), f32[8,128,128]{2,1,0:T(8,128)S(1)}, u32[]{:S(2)}, u32[]{:S(2)}) async-start(f32[8,128,128]{2,1,0:T(8,128)} %shard_map.106), calls=%async_computation.4 | async-start | bytes 1048576 | tf_op jit(solution)/shard_map/all_to_all | solution.py:297
  106.5 1.7 %copy-start.6 = (bf16[8,640,256]{2,1,0:T(8,128)(2,1)S(1)}, bf16[8,640,256]{2,1,0:T(8,128)(2,1)}, u32[]{:S(2)}) copy-start(bf16[8,640,256]{2,1,0:T(8,128)(2,1)} %copy-done.4) | copy-start | bytes 7864324
  131.3 1.2 copy-start
  132.5 1.2 copy-start.1

commit v3 on v2

--- a/solution.py
+++ b/solution.py
@@ -22,9 +22,9 @@
 DIAG_WEIGHT = 6.0
 BLOCK_WEIGHT = 3.0
 STEP_SCALE = 0.1
-INNER_SLOTS = (0, 3, 4, 5, 6)
+OWN_SLOTS = (0, 3, 4, 5, 6)
 ROOT2 = math.sqrt(0.5)
-VMEM_LIMIT = 48 * 1024 * 1024
+VMEM_LIMIT = 16 * 1024 * 1024
 
 
 def slot_frequencies(c):
@@ -141,9 +141,7 @@
 CHUNK = 16
 
 
-def forward_kernel(x_ref, high_ref, low_ref, *rest):
-    out_refs, z_ref = rest[:PARTS], rest[PARTS]
-
+def forward_kernel(x_ref, high_ref, low_ref, out_ref, z_ref):
     @pl.loop(0, HALF // CHUNK)
     def _(step):
         row = pl.multiple_of(step * CHUNK, CHUNK)
@@ -158,16 +156,12 @@
 
     for c in range(CLASSES):
         both = dot(high_ref[c], z_ref[c])
-        result = both[:, :NODES] + both[:, NODES:] + dot(low_ref[c], z_ref[c, :, :NODES])
-        for part in range(PARTS):
-            out_refs[part][c] = result[part * ROWS : (part + 1) * ROWS]
-
-
-def inverse_kernel(*refs):
-    y_refs = refs[:PARTS]
-    high_ref, low_ref, out_ref, v_ref = refs[PARTS:]
+        out_ref[c] = both[:, :NODES] + both[:, NODES:] + dot(low_ref[c], z_ref[c, :, :NODES])
+
+
+def inverse_kernel(y_ref, high_ref, low_ref, out_ref, v_ref):
     for c in range(CLASSES):
-        high, low = split(jnp.concatenate([y_ref[c] for y_ref in y_refs], 0))
+        high, low = split(y_ref[c])
         both = dot(high_ref[c], jnp.concatenate([high, low], 1))
         v_ref[c] = both[:, :NODES] + both[:, NODES:] + dot(low_ref[c], high)
 
@@ -182,13 +176,16 @@
             out_ref[q // 2, pl.ds(q % 2 * HALF + row, CHUNK), :] = value * (1.0 / BLOCK_GROWTH[q])
 
 
-def weights_kernel(blocks_ref, inner_ref, rim_ref):
+def weights_kernel(core_ref, blocks_ref, near_ref, far_ref):
+    core = core_ref[0]
     for e in range(PLANE):
-        for target, slots in ((inner_ref, INNER_SLOTS), (rim_ref, (1, 2))):
-            for place, s in enumerate(slots):
-                high, low = split(blocks_ref[e, s].T)
-                target[e, place * NODES : (place + 1) * NODES, :NODES] = high
-                target[e, place * NODES : (place + 1) * NODES, NODES:] = low
+        for place, s in enumerate(OWN_SLOTS + (2 - core,)):
+            high, low = split(blocks_ref[e, s].T)
+            near_ref[e, place * NODES : (place + 1) * NODES, :NODES] = high
+            near_ref[e, place * NODES : (place + 1) * NODES, NODES:] = low
+        high, low = split(blocks_ref[e, 1 + core].T)
+        far_ref[e, :, :NODES] = high
+        far_ref[e, :, NODES:] = low
 
 
 def solved(shift_ref, part, shift):
@@ -197,64 +194,65 @@
     imaginary = shift_ref[part, 2]
     scale = 1.0 / (first * second + imaginary * imaginary)
     a, b, c = second * scale, imaginary * scale, first * scale
-    return lambda real, imag: (a * real + b * imag, c * imag - b * real)
+
+    def apply(value):
+        real, imag = value[:SLOTS], value[SLOTS:]
+        return jnp.concatenate([a * real + b * imag, c * imag - b * real], 0)
+
+    return apply
+
+
+def rows_of(part):
+    return slice(part * ROWS, (part + 1) * ROWS)
 
 
 def first_kernel(part, rates_ref, spec_ref, shift_ref, out_ref):
     apply = solved(shift_ref, part, STEP_SCALE * rates_ref[0])
-
-    @pl.loop(0, PLANE)
-    def _(e):
-        real, imag = apply(spec_ref[e, :SLOTS], spec_ref[e, SLOTS:])
-        out_ref[e, :SLOTS] = real
-        out_ref[e, SLOTS:] = imag
-
-
-def inner_kernel(nb_ref, y_ref, weights_ref, out_ref, high_ref, low_ref):
     for e in range(PLANE):
-        high_ref[e], low_ref[e] = split(y_ref[e])
-
-    @pl.loop(0, PLANE)
-    def _(e):
-        picked = [nb_ref[e, s] % PLANE for s in INNER_SLOTS]
-        high = jnp.concatenate([high_ref[i] for i in picked], 1)
-        low = jnp.concatenate([low_ref[i] for i in picked], 1)
-        both = dot(high, weights_ref[e])
-        out_ref[e] = both[:, :NODES] + both[:, NODES:] + dot(low, weights_ref[e, :, :NODES])
-
-
-def rim_kernel(
-    part,
-    sweep,
-    rates_ref,
-    nb_ref,
-    y_ref,
-    inner_ref,
-    before_ref,
-    after_ref,
-    spec_ref,
-    shift_ref,
-    weights_ref,
-    out_ref,
+        out_ref[e] = apply(spec_ref[e, rows_of(part)])
+
+
+def folded(product):
+    return (product[:ROWS, :NODES] + product[:ROWS, NODES:]) + (
+        product[ROWS:, :NODES] + product[ROWS:, NODES:]
+    )
+
+
+def near_kernel(
+    part, sweep, rates_ref, core_ref, nb_ref, y_ref, pair_ref, spec_ref, weights_ref, out_ref, split_ref
 ):
-    shift = STEP_SCALE * rates_ref[sweep]
-    apply = solved(shift_ref, part, shift)
-
-    @pl.loop(0, PLANE)
-    def _(e):
-        before = before_ref[nb_ref[e, 1] % PLANE]
-        after = after_ref[nb_ref[e, 2] % PLANE]
-        high, low = split(jnp.concatenate([before, after], 1))
-        both = dot(high, weights_ref[e])
-        rim = both[:, :NODES] + both[:, NODES:] + dot(low, weights_ref[e, :, :NODES])
-        right = (
-            spec_ref[e]
-            + (shift - STEP_SCALE * DIAG_WEIGHT) * y_ref[e]
-            - (STEP_SCALE * BLOCK_WEIGHT) * (inner_ref[e] + rim)
+    core = core_ref[0]
+    keep = STEP_SCALE * rates_ref[sweep] - STEP_SCALE * DIAG_WEIGHT
+    for place, ref in enumerate((y_ref, pair_ref)):
+        for e in range(PLANE):
+            high, low = split(ref[e])
+            split_ref[place * PLANE + e, :ROWS] = high
+            split_ref[place * PLANE + e, ROWS:] = low
+    for e in range(PLANE):
+        picked = [nb_ref[e, s] % PLANE for s in OWN_SLOTS] + [PLANE + nb_ref[e, 2 - core] % PLANE]
+        product = dot(jnp.concatenate([split_ref[i] for i in picked], 1), weights_ref[e])
+        out_ref[e] = (
+            spec_ref[e, rows_of(part)]
+            + keep * y_ref[e]
+            - (STEP_SCALE * BLOCK_WEIGHT) * folded(product)
         )
-        real, imag = apply(right[:SLOTS], right[SLOTS:])
-        out_ref[e, :SLOTS] = real
-        out_ref[e, SLOTS:] = imag
+
+
+def far_kernel(part, sweep, rates_ref, core_ref, nb_ref, base_ref, far_ref, shift_ref, weights_ref, *rest):
+    core = core_ref[0]
+    apply = solved(shift_ref, part, STEP_SCALE * rates_ref[sweep])
+    out_ref = rest[-1]
+    for e in range(PLANE):
+        product = dot(
+            jnp.concatenate(split(far_ref[nb_ref[e, 1 + core] % PLANE]), 0), weights_ref[e]
+        )
+        result = apply(base_ref[e] - (STEP_SCALE * BLOCK_WEIGHT) * folded(product))
+        if len(rest) == 1:
+            out_ref[e] = result
+        else:
+            for other in range(PARTS - 1):
+                out_ref[e, rows_of(other)] = rest[other][e]
+            out_ref[e, rows_of(part)] = result
 
 
 def whole(count):
@@ -289,80 +287,73 @@
     shifts = lax.dynamic_index_in_dim(
         jnp.asarray(shift_table()), lax.axis_index("tm"), 0, keepdims=False
     )
+    core = (lax.axis_index("space") % 2).astype(jnp.int32).reshape(1)
     ring = lax.axis_size("space")
-    up = [(i, (i + 1) % ring) for i in range(ring)]
-    down = [(j, i) for i, j in up]
+    on_chip = [(i, i ^ 1) for i in range(ring)]
+    off_chip = [(i, (i + 1 if i % 2 else i - 1) % ring) for i in range(ring)]
 
     def exchange(value):
         return lax.all_to_all(value, "tm", 0, 0, tiled=True)
 
-    inner_weights, rim_weights = call(
+    near_weights, far_weights = call(
         weights_kernel,
         (
-            jax.ShapeDtypeStruct((PLANE, 5 * NODES, 2 * NODES), jnp.bfloat16),
-            jax.ShapeDtypeStruct((PLANE, 2 * NODES, 2 * NODES), jnp.bfloat16),
+            jax.ShapeDtypeStruct((PLANE, 6 * NODES, 2 * NODES), jnp.bfloat16),
+            jax.ShapeDtypeStruct((PLANE, NODES, 2 * NODES), jnp.bfloat16),
         ),
-        whole(1),
+        scalars(1) + whole(1),
         0,
         8 * MIB,
-    )(blocks)
+    )(core, blocks)
     steps = exchange(right_side)
-    steps, inner_weights, rim_weights, shifts = lax.optimization_barrier(
-        (steps, inner_weights, rim_weights, shifts)
+    steps, near_weights, far_weights, shifts = lax.optimization_barrier(
+        (steps, near_weights, far_weights, shifts)
     )
     spectrum = call(
         forward_kernel,
-        (STATE,) * PARTS,
+        STEPS,
         whole(3),
         10**9,
         4 * MIB,
         [pltpu.VMEM((CLASSES, 256, 256), jnp.bfloat16)],
     )(steps, forward_high, forward_low)
-    spectrum = [exchange(part) for part in spectrum]
+    spectrum = exchange(spectrum)
     states = [
         call(functools.partial(first_kernel, part), STATE, scalars(1) + whole(2), 0, 2 * MIB // PARTS)(
-            shift_rates, spectrum[part], shifts
+            shift_rates, spectrum, shifts
         )
         for part in range(PARTS)
     ]
     for sweep in range(1, SWEEPS):
         for part in range(PARTS):
             state = states[part]
-            before = lax.ppermute(state, "space", up)
-            after = lax.ppermute(state, "space", down)
-            inner = call(
-                inner_kernel,
+            pair = lax.ppermute(state, "space", on_chip)
+            far = lax.ppermute(state, "space", off_chip)
+            base = call(
+                functools.partial(near_kernel, part, sweep),
                 STATE,
-                scalars(1) + whole(2),
+                scalars(3) + whole(4),
                 2 * 10**9 // PARTS,
                 5 * MIB // PARTS,
-                [pltpu.VMEM((PLANE, ROWS, NODES), jnp.bfloat16)] * 2,
-            )(neighbors, state, inner_weights)
+                [pltpu.VMEM((2 * PLANE, 2 * ROWS, NODES), jnp.bfloat16)],
+            )(shift_rates, core, neighbors, state, pair, spectrum, near_weights)
+            last = sweep == SWEEPS - 1 and part == PARTS - 1
+            others = states[: PARTS - 1] if last else []
             states[part] = call(
-                functools.partial(rim_kernel, part, sweep),
-                STATE,
-                scalars(2) + whole(7),
+                functools.partial(far_kernel, part, sweep),
+                STEPS if last else STATE,
+                scalars(3) + whole(4 + len(others)),
                 10**9 // PARTS,
-                7 * MIB // PARTS,
-            )(
-                shift_rates,
-                neighbors,
-                state,
-                inner,
-                before,
-                after,
-                spectrum[part],
-                shifts,
-                rim_weights,
-            )
+                3 * MIB // PARTS,
+            )(shift_rates, core, neighbors, base, far, shifts, far_weights, *others)
     steps = call(
         inverse_kernel,
         STEPS,
-        whole(PARTS + 2),
+        whole(3),
         10**9,
         4 * MIB,
         [pltpu.VMEM((CLASSES, 256, 128), jnp.float32)],
-    )(*[exchange(state) for state in states], inverse_high, inverse_low)
+    )(exchange(states[-1]), inverse_high, inverse_low)
     return exchange(steps)
 
 

time: 158 us -> 134 us (0.85)
  Pallas kernels: 38 us -> 22.3 us
  starting transfers between devices: 35.1 us -> 19.8 us
  blocking collectives: 49.2 us -> 61 us
  local copies, waits for them, and re-layouts: 10.6 us -> 7.21 us
    pallas_call x15, Pallas kernels: 36.7 us -> 21.1 us  [the longest x6 10.4 us: per_device(): call(functools.partial(near_kernel, part, sweep), STATE, scalars(3) + who...]
    all_to_all x3, blocking collectives: 49.2 us -> 61 us  [exchange(): return lax.all_to_all(value, 'tm', 0, 0, tiled=True)]
    all_to_all x3 -> x1, waiting for transfers between devices: 23 us -> 12.5 us  [exchange(): return lax.all_to_all(value, 'tm', 0, 0, tiled=True)]
    ppermute x12, waiting for transfers between devices: 0.03 us -> 10.3 us  [the longest x6 10.3 us: per_device(): far = lax.ppermute(state, 'space', off_chip)]
    ppermute x12, starting transfers between devices: 20 us -> 11.8 us  [the longest x6 9.93 us: per_device(): pair = lax.ppermute(state, 'space', on_chip)]
    all_to_all x3 -> x1, starting transfers between devices: 15.1 us -> 7.94 us  [exchange(): return lax.all_to_all(value, 'tm', 0, 0, tiled=True)]
    unnamed x19, local copies, waits for them, and re-layouts: 9.63 us -> 6.27 us
  transfers between devices with their start and end apart: 15 -> 13, of which waited for: 3 -> 7; matrix products, arithmetic and copies ran while one was open for 1% -> 1% of each run, Pallas kernels for 22% -> 13%
where the time goes in v3:
time: 134 us; the launch traced here: 133 us
  blocking collectives  61 us (46%)
  waiting for transfers between devices  22.9 us (17%)
  Pallas kernels  22.3 us (17%)
  starting transfers between devices  19.8 us (15%)
  local copies, waits for them, and re-layouts  7.21 us (5%)
    all_to_all x3, blocking collectives, exchange(): return lax.all_to_all(value, 'tm', 0, 0, tiled=True)  61 us
    all_to_all x1, waiting for transfers between devices, exchange(): return lax.all_to_all(value, 'tm', 0, 0, tiled=True)  12.5 us
    pallas_call x6, Pallas kernels, per_device(): call(functools.partial(near_kernel, part, sweep), STATE, scalars(3) + who...  10.4 us
    ppermute x6, waiting for transfers between devices, per_device(): far = lax.ppermute(state, 'space', off_chip)  10.3 us
    ppermute x6, starting transfers between devices, per_device(): pair = lax.ppermute(state, 'space', on_chip)  9.93 us
    all_to_all x1, starting transfers between devices, exchange(): return lax.all_to_all(value, 'tm', 0, 0, tiled=True)  7.94 us
    pallas_call x6, Pallas kernels, per_device(): call(functools.partial(far_kernel, part, sweep), STEPS if last else STATE...  6.29 us
    unnamed x19, local copies, waits for them, and re-layouts  6.27 us
  transfers between devices with their start and end apart: 13, of which 7 were waited for; matrix products, arithmetic and copies ran while one was open for 1% of the time, Pallas kernels for 13%

profile of v3, /device:TPU:6, one launch (start us, length us, event | category | flops | bytes accessed | tf_op | source)
XLA Modules:
  0.0 133.3 jit_solution(493574151880751835)
XLA Ops:
  0.0 7.9 %all-to-all-start = ((f32[8,256,128]{2,1,0:T(8,128)}), f32[8,256,128]{2,1,0:T(8,128)}, u32[]{:S(2)}, u32[]{:S(2)}) async-start(f32[8,256,128]{2,1,0:T(8,128)} %param.9), calls=%async_computation | async-start | bytes 2097152 | tf_op jit(solution)/shard_map/all_to_all | solution.py:296
  8.0 2.0 %copy-done.2 = f32[8,7,128,128]{3,2,1,0:T(8,128)S(1)} copy-done((f32[8,7,128,128]{3,2,1,0:T(8,128)S(1)}, f32[8,7,128,128]{3,2,1,0:T(8,128)}, u32[]{:S(2)}) %copy-start.2) | copy-done | bytes 3670040
  12.7 12.5 %all-to-all-done.x_ref = f32[8,256,128]{2,1,0:T(8,128)} async-done(((f32[8,256,128]{2,1,0:T(8,128)}), f32[8,256,128]{2,1,0:T(8,128)}, u32[]{:S(2)}, u32[]{:S(2)}) %all-to-all-start) | async-done | bytes 1048608 | tf_op jit(solution)/shard_map/all_to_all | solution.py:296
  25.3 1.2 copy-done.5
  26.5 1.2 copy-done.6
  27.7 2.3 %shard_map.92 = f32[8,256,128]{2,1,0:T(8,128)S(1)} custom-call(f32[8,256,128]{2,1,0:T(8,128)} %all-to-all-done.x_ref, bf16[8,256,256]{2,1,0:T(8,128)(2,1)S(1)} %copy-done.5, bf16[8,256,256]{2,1,0:T(8,128)(2,1)S(1)} %copy-done.6), custom_call_target="tpu_custom_call" | custom-call | flops 1000000000 | bytes 4194304 | tf_op jit(solution)/shard_map/pallas_call | solution.py:312
  30.1 19.9 %all_to_all.20.spec_ref = f32[8,256,128]{2,1,0:T(8,128)S(1)} all-to-all(f32[8,256,128]{2,1,0:T(8,128)S(1)} %shard_map.92), channel_id=1, replica_groups=mesh['tm'=8,'space'=16] {'tm'}, dimensions={0} | all-to-all | bytes 2097152 | tf_op jit(solution)/shard_map/all_to_all | solution.py:296
  53.3 1.7 %shard_map.100.base_ref = f32[8,128,128]{2,1,0:T(8,128)S(1)} custom-call(f32[4]{0:T(128)S(1)} %copy-done.8, s32[1]{0:T(128)} %bitcast.core_ref, s32[8,7]{1,0:T(8,128)S(1)} %copy-done.7, f32[8,128,128]{2,1,0:T(8,128)S(1)} %shard_map.99.y_ref, f32[8,128,128]{2,1,0:T(8,128)S(1)} %collective-permute-done.6.pair_ref, f32[8,256,128]{2,1,0:T(8,128)S(1)} %all_to_all.20.spec_ref, ...), custom_call_target="tpu_custom_call" | custom-call | flops 1000000000 | bytes 2621440 | tf_op jit(solution)/shard_map/pallas_call | solution.py:332
  55.1 4.3 %collective-permute-done.7.far_ref = f32[8,128,128]{2,1,0:T(8,128)S(1)} collective-permute-done((f32[8,128,128]{2,1,0:T(8,128)S(1)}, f32[8,128,128]{2,1,0:T(8,128)S(1)}, u32[]{:S(2)}, u32[]{:S(2)}) %collective-permute-start.7) | collective-permute-done | bytes 524320 | tf_op jit(solution)/shard_map/ppermute | solution.py:331
  59.4 1.1 shard_map.101.y_ref
  60.5 2.6 %collective-permute-start.8 = (f32[8,128,128]{2,1,0:T(8,128)S(1)}, f32[8,128,128]{2,1,0:T(8,128)S(1)}, u32[]{:S(2)}, u32[]{:S(2)}) collective-permute-start(f32[8,128,128]{2,1,0:T(8,128)S(1)} %shard_map.101.y_ref), channel_id=1, source_target_pairs={{0,1},{1,0},{2,3},{3,2},{4,5},{5,4},{6,7},{7,6},{8,9},{9,8},{10,11... | collective-permute-start | bytes 1572872 | tf_op jit(solution)/shard_map/ppermute | solution.py:330
  63.1 1.7 %shard_map.94.base_ref = f32[8,128,128]{2,1,0:T(8,128)S(1)} custom-call(f32[4]{0:T(128)S(1)} %copy-done.8, s32[1]{0:T(128)} %bitcast.core_ref, s32[8,7]{1,0:T(8,128)S(1)} %copy-done.7, f32[8,128,128]{2,1,0:T(8,128)S(1)} %shard_map.93.y_ref, f32[8,128,128]{2,1,0:T(8,128)S(1)} %collective-permute-done.pair_ref, f32[8,256,128]{2,1,0:T(8,128)S(1)} %all_to_all.20.spec_ref, ...), custom_call_target="tpu_custom_call" | custom-call | flops 1000000000 | bytes 2621440 | tf_op jit(solution)/shard_map/pallas_call | solution.py:332
  66.1 2.6 %collective-permute-start.2 = (f32[8,128,128]{2,1,0:T(8,128)S(1)}, f32[8,128,128]{2,1,0:T(8,128)S(1)}, u32[]{:S(2)}, u32[]{:S(2)}) collective-permute-start(f32[8,128,128]{2,1,0:T(8,128)S(1)} %shard_map.95.y_ref), channel_id=1, source_target_pairs={{0,1},{1,0},{2,3},{3,2},{4,5},{5,4},{6,7},{7,6},{8,9},{9,8},{10,11... | collective-permute-start | bytes 1572872 | tf_op jit(solution)/shard_map/ppermute | solution.py:330
  68.7 1.7 %shard_map.102.base_ref = f32[8,128,128]{2,1,0:T(8,128)S(1)} custom-call(f32[4]{0:T(128)S(1)} %copy-done.8, s32[1]{0:T(128)} %bitcast.core_ref, s32[8,7]{1,0:T(8,128)S(1)} %copy-done.7, f32[8,128,128]{2,1,0:T(8,128)S(1)} %shard_map.101.y_ref, f32[8,128,128]{2,1,0:T(8,128)S(1)} %collective-permute-done.8.pair_ref, f32[8,256,128]{2,1,0:T(8,128)S(1)} %all_to_all.20.spec_ref, ...), custom_call_target="tpu_custom_call" | custom-call | flops 1000000000 | bytes 2621440 | tf_op jit(solution)/shard_map/pallas_call | solution.py:332
  70.4 1.2 collective-permute-done.9.far_ref
  72.7 2.3 %collective-permute-start.10 = (f32[8,128,128]{2,1,0:T(8,128)S(1)}, f32[8,128,128]{2,1,0:T(8,128)S(1)}, u32[]{:S(2)}, u32[]{:S(2)}) collective-permute-start(f32[8,128,128]{2,1,0:T(8,128)S(1)} %shard_map.103.y_ref), channel_id=1, source_target_pairs={{0,1},{1,0},{2,3},{3,2},{4,5},{5,4},{6,7},{7,6},{8,9},{9,8},{10,11... | collective-permute-start | bytes 1572872 | tf_op jit(solution)/shard_map/ppermute | solution.py:330
  75.0 1.7 %shard_map.96.base_ref = f32[8,128,128]{2,1,0:T(8,128)S(1)} custom-call(f32[4]{0:T(128)S(1)} %copy-done.8, s32[1]{0:T(128)} %bitcast.core_ref, s32[8,7]{1,0:T(8,128)S(1)} %copy-done.7, f32[8,128,128]{2,1,0:T(8,128)S(1)} %shard_map.95.y_ref, f32[8,128,128]{2,1,0:T(8,128)S(1)} %collective-permute-done.2.pair_ref, f32[8,256,128]{2,1,0:T(8,128)S(1)} %all_to_all.20.spec_ref, ...), custom_call_target="tpu_custom_call" | custom-call | flops 1000000000 | bytes 2621440 | tf_op jit(solution)/shard_map/pallas_call | solution.py:332
  78.3 2.3 %collective-permute-start.4 = (f32[8,128,128]{2,1,0:T(8,128)S(1)}, f32[8,128,128]{2,1,0:T(8,128)S(1)}, u32[]{:S(2)}, u32[]{:S(2)}) collective-permute-start(f32[8,128,128]{2,1,0:T(8,128)S(1)} %shard_map.97.y_ref), channel_id=1, source_target_pairs={{0,1},{1,0},{2,3},{3,2},{4,5},{5,4},{6,7},{7,6},{8,9},{9,8},{10,11... | collective-permute-start | bytes 1572872 | tf_op jit(solution)/shard_map/ppermute | solution.py:330
  80.6 1.7 %shard_map.104.base_ref = f32[8,128,128]{2,1,0:T(8,128)S(1)} custom-call(f32[4]{0:T(128)S(1)} %copy-done.8, s32[1]{0:T(128)} %bitcast.core_ref, s32[8,7]{1,0:T(8,128)S(1)} %copy-done.7, f32[8,128,128]{2,1,0:T(8,128)S(1)} %shard_map.103.y_ref, f32[8,128,128]{2,1,0:T(8,128)S(1)} %collective-permute-done.10.pair_ref, f32[8,256,128]{2,1,0:T(8,128)S(1)} %all_to_all.20.spec_ref, ...), custom_call_target="tpu_custom_call" | custom-call | flops 1000000000 | bytes 2621440 | tf_op jit(solution)/shard_map/pallas_call | solution.py:332
  82.4 1.2 collective-permute-done.11.far_ref
  84.7 1.7 %shard_map.98.base_ref = f32[8,128,128]{2,1,0:T(8,128)S(1)} custom-call(f32[4]{0:T(128)S(1)} %copy-done.8, s32[1]{0:T(128)} %bitcast.core_ref, s32[8,7]{1,0:T(8,128)S(1)} %copy-done.7, f32[8,128,128]{2,1,0:T(8,128)S(1)} %shard_map.97.y_ref, f32[8,128,128]{2,1,0:T(8,128)S(1)} %collective-permute-done.4.pair_ref, f32[8,256,128]{2,1,0:T(8,128)S(1)} %all_to_all.20.spec_ref, ...), custom_call_target="tpu_custom_call" | custom-call | flops 1000000000 | bytes 2621440 | tf_op jit(solution)/shard_map/pallas_call | solution.py:332
  86.4 2.8 %collective-permute-done.5.far_ref = f32[8,128,128]{2,1,0:T(8,128)S(1)} collective-permute-done((f32[8,128,128]{2,1,0:T(8,128)S(1)}, f32[8,128,128]{2,1,0:T(8,128)S(1)}, u32[]{:S(2)}, u32[]{:S(2)}) %collective-permute-start.5) | collective-permute-done | bytes 524320 | tf_op jit(solution)/shard_map/ppermute | solution.py:331
  90.3 19.9 %all_to_all.21.y_ref = f32[8,256,128]{2,1,0:T(8,128)S(1)} all-to-all(f32[8,256,128]{2,1,0:T(8,128)S(1)} %shard_map.106), channel_id=1, replica_groups=mesh['tm'=8,'space'=16] {'tm'}, dimensions={0} | all-to-all | bytes 2097152 | tf_op jit(solution)/shard_map/all_to_all | solution.py:296
  111.1 21.2 %all_to_all.22 = f32[8,256,128]{2,1,0:T(8,128)S(1)} all-to-all(f32[8,256,128]{2,1,0:T(8,128)S(1)} %shard_map.107), channel_id=1, replica_groups=mesh['tm'=8,'space'=16] {'tm'}, dimensions={0} | all-to-all | bytes 2097152 | tf_op jit(solution)/shard_map/all_to_all | solution.py:296
  (42 shorter events, 14.0 us)
Async XLA Ops:
  0.0 25.3 %all-to-all-start = ((f32[8,256,128]{2,1,0:T(8,128)}), f32[8,256,128]{2,1,0:T(8,128)}, u32[]{:S(2)}, u32[]{:S(2)}) async-start(f32[8,256,128]{2,1,0:T(8,128)} %param.9), calls=%async_computation | async-start | bytes 2097152 | tf_op jit(solution)/shard_map/all_to_all | solution.py:296
  7.9 2.0 %copy-start.2 = (f32[8,7,128,128]{3,2,1,0:T(8,128)S(1)}, f32[8,7,128,128]{3,2,1,0:T(8,128)}, u32[]{:S(2)}) copy-start(f32[8,7,128,128]{3,2,1,0:T(8,128)} %blocks_ref.1) | copy-start | bytes 11010052
  11.0 0.8 copy-start
  25.3 1.2 copy-start.5
  26.5 1.2 copy-start.6
  27.7 22.3 %copy-start.8 = (f32[4]{0:T(128)S(1)}, f32[4]{0:T(128)}, u32[]{:S(2)}) copy-start(f32[4]{0:T(128)} %rates_ref.27) | copy-start | bytes 52
  30.1 23.3 %copy-start.7 = (s32[8,7]{1,0:T(8,128)S(1)}, s32[8,7]{1,0:T(8,128)}, u32[]{:S(2)}) copy-start(s32[8,7]{1,0:T(8,128)} %nb_ref.23) | copy-start | bytes 676
  50.6 2.7 %collective-permute-start.6 = (f32[8,128,128]{2,1,0:T(8,128)S(1)}, f32[8,128,128]{2,1,0:T(8,128)S(1)}, u32[]{:S(2)}, u32[]{:S(2)}) collective-permute-start(f32[8,128,128]{2,1,0:T(8,128)S(1)} %shard_map.99.y_ref), channel_id=1, source_target_pairs={{0,1},{1,0},{2,3},{3,2},{4,5},{5,4},{6,7},{7,6},{8,9},{9,8},{10,11... | collective-permute-start | bytes 1572872 | tf_op jit(solution)/shard_map/ppermute | solution.py:330
  50.7 8.7 %collective-permute-start.7 = (f32[8,128,128]{2,1,0:T(8,128)S(1)}, f32[8,128,128]{2,1,0:T(8,128)S(1)}, u32[]{:S(2)}, u32[]{:S(2)}) collective-permute-start(f32[8,128,128]{2,1,0:T(8,128)S(1)} %shard_map.99.y_ref), channel_id=1, source_target_pairs={{0,15},{1,2},{2,1},{3,4},{4,3},{5,6},{6,5},{7,8},{8,7},{9,10},{10,... | collective-permute-start | bytes 1572872 | tf_op jit(solution)/shard_map/ppermute | solution.py:331
  52.3 7.1 %copy-start.1 = (bf16[8,128,256]{2,1,0:T(8,128)(2,1)S(1)}, bf16[8,128,256]{2,1,0:T(8,128)(2,1)}, u32[]{:S(2)}) copy-start(bf16[8,128,256]{2,1,0:T(8,128)(2,1)} %copy-done) | copy-start | bytes 1572868
  52.3 10.8 %collective-permute-start = (f32[8,128,128]{2,1,0:T(8,128)S(1)}, f32[8,128,128]{2,1,0:T(8,128)S(1)}, u32[]{:S(2)}, u32[]{:S(2)}) collective-permute-start(f32[8,128,128]{2,1,0:T(8,128)S(1)} %shard_map.93.y_ref), channel_id=1, source_target_pairs={{0,1},{1,0},{2,3},{3,2},{4,5},{5,4},{6,7},{7,6},{8,9},{9,8},{10,11... | collective-permute-start | bytes 1572872 | tf_op jit(solution)/shard_map/ppermute | solution.py:330
  52.4 12.6 %collective-permute-start.1 = (f32[8,128,128]{2,1,0:T(8,128)S(1)}, f32[8,128,128]{2,1,0:T(8,128)S(1)}, u32[]{:S(2)}, u32[]{:S(2)}) collective-permute-start(f32[8,128,128]{2,1,0:T(8,128)S(1)} %shard_map.93.y_ref), channel_id=1, source_target_pairs={{0,15},{1,2},{2,1},{3,4},{4,3},{5,6},{6,5},{7,8},{8,7},{9,10},{10,... | collective-permute-start | bytes 1572872 | tf_op jit(solution)/shard_map/ppermute | solution.py:331
  60.5 8.2 %collective-permute-start.8 = (f32[8,128,128]{2,1,0:T(8,128)S(1)}, f32[8,128,128]{2,1,0:T(8,128)S(1)}, u32[]{:S(2)}, u32[]{:S(2)}) collective-permute-start(f32[8,128,128]{2,1,0:T(8,128)S(1)} %shard_map.101.y_ref), channel_id=1, source_target_pairs={{0,1},{1,0},{2,3},{3,2},{4,5},{5,4},{6,7},{7,6},{8,9},{9,8},{10,11... | collective-permute-start | bytes 1572872 | tf_op jit(solution)/shard_map/ppermute | solution.py:330
  63.1 8.6 %collective-permute-start.9 = (f32[8,128,128]{2,1,0:T(8,128)S(1)}, f32[8,128,128]{2,1,0:T(8,128)S(1)}, u32[]{:S(2)}, u32[]{:S(2)}) collective-permute-start(f32[8,128,128]{2,1,0:T(8,128)S(1)} %shard_map.101.y_ref), channel_id=1, source_target_pairs={{0,15},{1,2},{2,1},{3,4},{4,3},{5,6},{6,5},{7,8},{8,7},{9,10},{10,... | collective-permute-start | bytes 1572872 | tf_op jit(solution)/shard_map/ppermute | solution.py:331
  66.1 8.9 %collective-permute-start.2 = (f32[8,128,128]{2,1,0:T(8,128)S(1)}, f32[8,128,128]{2,1,0:T(8,128)S(1)}, u32[]{:S(2)}, u32[]{:S(2)}) collective-permute-start(f32[8,128,128]{2,1,0:T(8,128)S(1)} %shard_map.95.y_ref), channel_id=1, source_target_pairs={{0,1},{1,0},{2,3},{3,2},{4,5},{5,4},{6,7},{7,6},{8,9},{9,8},{10,11... | collective-permute-start | bytes 1572872 | tf_op jit(solution)/shard_map/ppermute | solution.py:330
  68.7 8.6 %collective-permute-start.3 = (f32[8,128,128]{2,1,0:T(8,128)S(1)}, f32[8,128,128]{2,1,0:T(8,128)S(1)}, u32[]{:S(2)}, u32[]{:S(2)}) collective-permute-start(f32[8,128,128]{2,1,0:T(8,128)S(1)} %shard_map.95.y_ref), channel_id=1, source_target_pairs={{0,15},{1,2},{2,1},{3,4},{4,3},{5,6},{6,5},{7,8},{8,7},{9,10},{10,... | collective-permute-start | bytes 1572872 | tf_op jit(solution)/shard_map/ppermute | solution.py:331
  72.7 7.9 %collective-permute-start.10 = (f32[8,128,128]{2,1,0:T(8,128)S(1)}, f32[8,128,128]{2,1,0:T(8,128)S(1)}, u32[]{:S(2)}, u32[]{:S(2)}) collective-permute-start(f32[8,128,128]{2,1,0:T(8,128)S(1)} %shard_map.103.y_ref), channel_id=1, source_target_pairs={{0,1},{1,0},{2,3},{3,2},{4,5},{5,4},{6,7},{7,6},{8,9},{9,8},{10,11... | collective-permute-start | bytes 1572872 | tf_op jit(solution)/shard_map/ppermute | solution.py:330
  75.0 8.6 %collective-permute-start.11 = (f32[8,128,128]{2,1,0:T(8,128)S(1)}, f32[8,128,128]{2,1,0:T(8,128)S(1)}, u32[]{:S(2)}, u32[]{:S(2)}) collective-permute-start(f32[8,128,128]{2,1,0:T(8,128)S(1)} %shard_map.103.y_ref), channel_id=1, source_target_pairs={{0,15},{1,2},{2,1},{3,4},{4,3},{5,6},{6,5},{7,8},{8,7},{9,10},{10,... | collective-permute-start | bytes 1572872 | tf_op jit(solution)/shard_map/ppermute | solution.py:331
  78.3 6.3 %collective-permute-start.4 = (f32[8,128,128]{2,1,0:T(8,128)S(1)}, f32[8,128,128]{2,1,0:T(8,128)S(1)}, u32[]{:S(2)}, u32[]{:S(2)}) collective-permute-start(f32[8,128,128]{2,1,0:T(8,128)S(1)} %shard_map.97.y_ref), channel_id=1, source_target_pairs={{0,1},{1,0},{2,3},{3,2},{4,5},{5,4},{6,7},{7,6},{8,9},{9,8},{10,11... | collective-permute-start | bytes 1572872 | tf_op jit(solution)/shard_map/ppermute | solution.py:330
  80.6 8.6 %collective-permute-start.5 = (f32[8,128,128]{2,1,0:T(8,128)S(1)}, f32[8,128,128]{2,1,0:T(8,128)S(1)}, u32[]{:S(2)}, u32[]{:S(2)}) collective-permute-start(f32[8,128,128]{2,1,0:T(8,128)S(1)} %shard_map.97.y_ref), channel_id=1, source_target_pairs={{0,15},{1,2},{2,1},{3,4},{4,3},{5,6},{6,5},{7,8},{8,7},{9,10},{10,... | collective-permute-start | bytes 1572872 | tf_op jit(solution)/shard_map/ppermute | solution.py:331
  86.4 23.7 %copy-start.3 = (bf16[8,256,256]{2,1,0:T(8,128)(2,1)S(1)}, bf16[8,256,256]{2,1,0:T(8,128)(2,1)}, u32[]{:S(2)}) copy-start(bf16[8,256,256]{2,1,0:T(8,128)(2,1)} %constant.39.clone.high_ref) | copy-start | bytes 3145732
  86.4 23.7 %copy-start.4 = (bf16[8,256,256]{2,1,0:T(8,128)(2,1)S(1)}, bf16[8,256,256]{2,1,0:T(8,128)(2,1)}, u32[]{:S(2)}) copy-start(bf16[8,256,256]{2,1,0:T(8,128)(2,1)} %constant.40.clone.low_ref) | copy-start | bytes 3145732

commit v4 on v3

--- a/solution.py
+++ b/solution.py
@@ -64,18 +64,17 @@
 
 def shift_table():
     root = math.exp(math.log(WRAP_WEIGHT) / LENGTH)
-    table = np.zeros((CLASSES, 3, HALF, NODES))
+    table = np.zeros((3, HALF, NODES))
     for c in range(CLASSES):
         angle = 2.0 * np.pi * slot_frequencies(c) / LENGTH
         real = 1.0 - root * np.cos(angle)
         second = real.copy()
         if c == 0:
             second[0] = 1.0 + root
-        table[c, 0] = real[:, None]
-        table[c, 1] = second[:, None]
-        table[c, 2] = (root * np.sin(angle))[:, None]
-    table = table.reshape(CLASSES, 3, PARTS, SLOTS, NODES).transpose(0, 2, 1, 3, 4)
-    return table.astype(np.float32)
+        table[0, :, c] = real
+        table[1, :, c] = second
+        table[2, :, c] = root * np.sin(angle)
+    return table.reshape(3, PARTS, SLOTS, NODES).transpose(1, 0, 2, 3).astype(np.float32)
 
 
 def split_host(matrix):
@@ -141,29 +140,29 @@
 CHUNK = 16
 
 
-def forward_kernel(x_ref, high_ref, low_ref, out_ref, z_ref):
+def steps_at(q, row):
+    return q // 2, pl.ds(q % 2 * HALF + row, CHUNK), slice(None)
+
+
+def table_product(high, low, value):
+    value_high, value_low = split(value)
+    both = dot(high, jnp.concatenate([value_high, value_low], 1))
+    return both[:, :NODES] + both[:, NODES:] + dot(low, value_high)
+
+
+def forward_kernel(x_ref, out_ref):
     @pl.loop(0, HALF // CHUNK)
     def _(step):
         row = pl.multiple_of(step * CHUNK, CHUNK)
-        series = [
-            x_ref[q // 2, pl.ds(q % 2 * HALF + row, CHUNK), :] * BLOCK_GROWTH[q] for q in range(16)
-        ]
-        for c, pair in enumerate(real_dft16(series)):
-            for part in range(2):
-                high, low = split(pair[part])
-                z_ref[c, pl.ds(part * HALF + row, CHUNK), :NODES] = high
-                z_ref[c, pl.ds(part * HALF + row, CHUNK), NODES:] = low
-
-    for c in range(CLASSES):
-        both = dot(high_ref[c], z_ref[c])
-        out_ref[c] = both[:, :NODES] + both[:, NODES:] + dot(low_ref[c], z_ref[c, :, :NODES])
+        series = [x_ref[steps_at(q, row)] * BLOCK_GROWTH[q] for q in range(16)]
+        for c, (real, imag) in enumerate(real_dft16(series)):
+            out_ref[c, pl.ds(row, CHUNK), :] = real
+            out_ref[c, pl.ds(HALF + row, CHUNK), :] = imag
 
 
 def inverse_kernel(y_ref, high_ref, low_ref, out_ref, v_ref):
     for c in range(CLASSES):
-        high, low = split(y_ref[c])
-        both = dot(high_ref[c], jnp.concatenate([high, low], 1))
-        v_ref[c] = both[:, :NODES] + both[:, NODES:] + dot(low_ref[c], high)
+        v_ref[c] = table_product(high_ref[c], low_ref[c], y_ref[c])
 
     @pl.loop(0, HALF // CHUNK)
     def _(step):
@@ -173,11 +172,11 @@
             for c in range(CLASSES)
         ]
         for q, value in enumerate(real_idft16(pairs)):
-            out_ref[q // 2, pl.ds(q % 2 * HALF + row, CHUNK), :] = value * (1.0 / BLOCK_GROWTH[q])
-
-
-def weights_kernel(core_ref, blocks_ref, near_ref, far_ref):
-    core = core_ref[0]
+            out_ref[steps_at(q, row)] = value * (1.0 / BLOCK_GROWTH[q])
+
+
+def weights_kernel(here_ref, blocks_ref, _, near_ref, far_ref):
+    core = here_ref[0] % 2
     for e in range(PLANE):
         for place, s in enumerate(OWN_SLOTS + (2 - core,)):
             high, low = split(blocks_ref[e, s].T)
@@ -188,12 +187,17 @@
         far_ref[e, :, NODES:] = low
 
 
-def solved(shift_ref, part, shift):
-    first = shift_ref[part, 0] + shift
-    second = shift_ref[part, 1] + shift
-    imaginary = shift_ref[part, 2]
+def solved(here_ref, shift_ref, part, shift):
+    mine = lax.broadcasted_iota(jnp.int32, (SLOTS, NODES), 1) == here_ref[0] // 2
+    real, second, imaginary = (
+        jnp.sum(jnp.where(mine, shift_ref[part, i], 0.0), 1, keepdims=True) for i in range(3)
+    )
+    first = real + shift
+    second = second + shift
     scale = 1.0 / (first * second + imaginary * imaginary)
-    a, b, c = second * scale, imaginary * scale, first * scale
+    a, b, c = (
+        jnp.broadcast_to(factor * scale, (SLOTS, NODES)) for factor in (second, imaginary, first)
+    )
 
     def apply(value):
         real, imag = value[:SLOTS], value[SLOTS:]
@@ -206,10 +210,14 @@
     return slice(part * ROWS, (part + 1) * ROWS)
 
 
-def first_kernel(part, rates_ref, spec_ref, shift_ref, out_ref):
-    apply = solved(shift_ref, part, STEP_SCALE * rates_ref[0])
+def first_kernel(part, rates_ref, here_ref, series_ref, high_ref, low_ref, shift_ref, spec_ref, out_ref):
+    apply = solved(here_ref, shift_ref, part, STEP_SCALE * rates_ref[0])
+    mine = here_ref[0] // 2
+    high, low = high_ref[mine, rows_of(part)], low_ref[mine, rows_of(part)]
     for e in range(PLANE):
-        out_ref[e] = apply(spec_ref[e, rows_of(part)])
+        spec = table_product(high, low, series_ref[e])
+        spec_ref[e] = spec
+        out_ref[e] = apply(spec)
 
 
 def folded(product):
@@ -219,9 +227,9 @@
 
 
 def near_kernel(
-    part, sweep, rates_ref, core_ref, nb_ref, y_ref, pair_ref, spec_ref, weights_ref, out_ref, split_ref
+    part, sweep, rates_ref, here_ref, nb_ref, y_ref, pair_ref, spec_ref, weights_ref, out_ref, split_ref
 ):
-    core = core_ref[0]
+    core = here_ref[0] % 2
     keep = STEP_SCALE * rates_ref[sweep] - STEP_SCALE * DIAG_WEIGHT
     for place, ref in enumerate((y_ref, pair_ref)):
         for e in range(PLANE):
@@ -232,15 +240,15 @@
         picked = [nb_ref[e, s] % PLANE for s in OWN_SLOTS] + [PLANE + nb_ref[e, 2 - core] % PLANE]
         product = dot(jnp.concatenate([split_ref[i] for i in picked], 1), weights_ref[e])
         out_ref[e] = (
-            spec_ref[e, rows_of(part)]
+            spec_ref[e]
             + keep * y_ref[e]
             - (STEP_SCALE * BLOCK_WEIGHT) * folded(product)
         )
 
 
-def far_kernel(part, sweep, rates_ref, core_ref, nb_ref, base_ref, far_ref, shift_ref, weights_ref, *rest):
-    core = core_ref[0]
-    apply = solved(shift_ref, part, STEP_SCALE * rates_ref[sweep])
+def far_kernel(part, sweep, rates_ref, here_ref, nb_ref, base_ref, far_ref, shift_ref, weights_ref, *rest):
+    core = here_ref[0] % 2
+    apply = solved(here_ref, shift_ref, part, STEP_SCALE * rates_ref[sweep])
     out_ref = rest[-1]
     for e in range(PLANE):
         product = dot(
@@ -284,10 +292,9 @@
     forward, inverse = transform_tables()
     forward_high, forward_low = (jnp.asarray(part) for part in split_host(forward))
     inverse_high, inverse_low = (jnp.asarray(part) for part in split_host(inverse))
-    shifts = lax.dynamic_index_in_dim(
-        jnp.asarray(shift_table()), lax.axis_index("tm"), 0, keepdims=False
-    )
-    core = (lax.axis_index("space") % 2).astype(jnp.int32).reshape(1)
+    shifts = jnp.asarray(shift_table())
+    here = (lax.axis_index("tm") * 2 + (lax.axis_index("space") & 1)).astype(jnp.int32).reshape(1)
+    right_side, here = lax.optimization_barrier((right_side, here))
     ring = lax.axis_size("space")
     on_chip = [(i, i ^ 1) for i in range(ring)]
     off_chip = [(i, (i + 1 if i % 2 else i - 1) % ring) for i in range(ring)]
@@ -295,35 +302,30 @@
     def exchange(value):
         return lax.all_to_all(value, "tm", 0, 0, tiled=True)
 
+    series = exchange(call(forward_kernel, STEPS, whole(1), 0, 2 * MIB)(exchange(right_side)))
+    spectrum, states = zip(
+        *(
+            call(
+                functools.partial(first_kernel, part),
+                (STATE, STATE),
+                scalars(2) + whole(4),
+                10**9 // PARTS,
+                4 * MIB // PARTS,
+            )(shift_rates, here, series, forward_high, forward_low, shifts)
+            for part in range(PARTS)
+        )
+    )
+    states = list(states)
     near_weights, far_weights = call(
         weights_kernel,
         (
             jax.ShapeDtypeStruct((PLANE, 6 * NODES, 2 * NODES), jnp.bfloat16),
             jax.ShapeDtypeStruct((PLANE, NODES, 2 * NODES), jnp.bfloat16),
         ),
-        scalars(1) + whole(1),
+        scalars(1) + whole(1) + [pl.BlockSpec(memory_space=pl.ANY)],
         0,
         8 * MIB,
-    )(core, blocks)
-    steps = exchange(right_side)
-    steps, near_weights, far_weights, shifts = lax.optimization_barrier(
-        (steps, near_weights, far_weights, shifts)
-    )
-    spectrum = call(
-        forward_kernel,
-        STEPS,
-        whole(3),
-        10**9,
-        4 * MIB,
-        [pltpu.VMEM((CLASSES, 256, 256), jnp.bfloat16)],
-    )(steps, forward_high, forward_low)
-    spectrum = exchange(spectrum)
-    states = [
-        call(functools.partial(first_kernel, part), STATE, scalars(1) + whole(2), 0, 2 * MIB // PARTS)(
-            shift_rates, spectrum, shifts
-        )
-        for part in range(PARTS)
-    ]
+    )(here, blocks, states[0])
     for sweep in range(1, SWEEPS):
         for part in range(PARTS):
             state = states[part]
@@ -336,7 +338,7 @@
                 2 * 10**9 // PARTS,
                 5 * MIB // PARTS,
                 [pltpu.VMEM((2 * PLANE, 2 * ROWS, NODES), jnp.bfloat16)],
-            )(shift_rates, core, neighbors, state, pair, spectrum, near_weights)
+            )(shift_rates, here, neighbors, state, pair, spectrum[part], near_weights)
             last = sweep == SWEEPS - 1 and part == PARTS - 1
             others = states[: PARTS - 1] if last else []
             states[part] = call(
@@ -345,14 +347,14 @@
                 scalars(3) + whole(4 + len(others)),
                 10**9 // PARTS,
                 3 * MIB // PARTS,
-            )(shift_rates, core, neighbors, base, far, shifts, far_weights, *others)
+            )(shift_rates, here, neighbors, base, far, shifts, far_weights, *others)
     steps = call(
         inverse_kernel,
         STEPS,
         whole(3),
         10**9,
         4 * MIB,
-        [pltpu.VMEM((CLASSES, 256, 128), jnp.float32)],
+        [pltpu.VMEM((CLASSES, 256, NODES), jnp.float32)],
     )(exchange(states[-1]), inverse_high, inverse_low)
     return exchange(steps)
 

time: 134 us -> 128 us (0.955)
  blocking collectives: 61 us -> 85 us
  waiting for transfers between devices: 22.9 us -> 8.85 us
  starting transfers between devices: 19.8 us -> 11.9 us
  local copies, waits for them, and re-layouts: 7.21 us -> 1.01 us
    all_to_all x3 -> x4, blocking collectives: 61 us -> 85 us  [exchange(): return lax.all_to_all(value, 'tm', 0, 0, tiled=True)]
    all_to_all x1 -> x0, waiting for transfers between devices: 12.5 us -> none  [exchange(): return lax.all_to_all(value, 'tm', 0, 0, tiled=True)]
    all_to_all x1 -> x0, starting transfers between devices: 7.94 us -> none  [exchange(): return lax.all_to_all(value, 'tm', 0, 0, tiled=True)]
    unnamed x19 -> x17, local copies, waits for them, and re-layouts: 6.27 us -> 1.01 us
    ppermute x6, waiting for transfers between devices: 10.3 us -> 8.84 us  [per_device(): far = lax.ppermute(state, 'space', off_chip)]
  transfers between devices with their start and end apart: 13 -> 12, of which waited for: 7 -> 6; matrix products, arithmetic and copies ran while one was open for 1% -> 0% of each run, Pallas kernels for 13% -> 14%
where the time goes in v4:
time: 128 us
  blocking collectives  85 us (66%)
  Pallas kernels  21 us (16%)
  starting transfers between devices  11.9 us (9%)
  waiting for transfers between devices  8.85 us (7%)
    all_to_all x4, blocking collectives, exchange(): return lax.all_to_all(value, 'tm', 0, 0, tiled=True)  85 us
    pallas_call x6, Pallas kernels, per_device(): call(functools.partial(near_kernel, part, sweep), STATE, scalars(3) + who...  10.5 us
    ppermute x6, starting transfers between devices, per_device(): pair = lax.ppermute(state, 'space', on_chip)  9.95 us
    ppermute x6, waiting for transfers between devices, per_device(): far = lax.ppermute(state, 'space', off_chip)  8.84 us
    pallas_call x6, Pallas kernels, per_device(): call(functools.partial(far_kernel, part, sweep), STEPS if last else STATE...  6.27 us
  transfers between devices with their start and end apart: 12, of which 6 were waited for; matrix products, arithmetic and copies ran while one was open for 0% of the time, Pallas kernels for 14%

profile of v4, /device:TPU:6, one launch (start us, length us, event | category | flops | bytes accessed | tf_op | source)
XLA Modules:
  0.0 128.0 jit_solution(12547411218155758117)
XLA Ops:
  0.0 25.3 %all_to_all.20.x_ref = f32[8,256,128]{2,1,0:T(8,128)S(1)} all-to-all(f32[8,256,128]{2,1,0:T(8,128)} %param.9), channel_id=1, replica_groups=mesh['tm'=8,'space'=16] {'tm'}, dimensions={0} | all-to-all | bytes 2097152 | tf_op jit(solution)/shard_map/all_to_all | solution.py:303
  25.6 18.7 %all_to_all.21.series_ref = f32[8,256,128]{2,1,0:T(8,128)S(1)} all-to-all(f32[8,256,128]{2,1,0:T(8,128)S(1)} %shard_map.91), channel_id=1, replica_groups=mesh['tm'=8,'space'=16] {'tm'}, dimensions={0} | all-to-all | bytes 2097152 | tf_op jit(solution)/shard_map/all_to_all | solution.py:303
  49.5 1.7 %shard_map.100.base_ref = f32[8,128,128]{2,1,0:T(8,128)S(1)} custom-call(f32[4]{0:T(128)S(1)} %copy-done.7, s32[1]{0:T(128)} %bitcast.here_ref, s32[8,7]{1,0:T(8,128)S(1)} %copy-done.6, f32[8,128,128]{2,1,0:T(8,128)S(1)} %get-tuple-element.17._.y_ref, f32[8,128,128]{2,1,0:T(8,128)S(1)} %collective-permute-done.6.pair_ref, ...), custom_call_target="tpu_custom_call" | custom-call | flops 1000000000 | bytes 2621440 | tf_op jit(solution)/shard_map/pallas_call | solution.py:334
  51.2 2.9 %collective-permute-done.7.far_ref = f32[8,128,128]{2,1,0:T(8,128)S(1)} collective-permute-done((f32[8,128,128]{2,1,0:T(8,128)S(1)}, f32[8,128,128]{2,1,0:T(8,128)S(1)}, u32[]{:S(2)}, u32[]{:S(2)}) %collective-permute-start.7) | collective-permute-done | bytes 524320 | tf_op jit(solution)/shard_map/ppermute | solution.py:333
  54.1 1.0 shard_map.101.y_ref
  55.2 2.6 %collective-permute-start.8 = (f32[8,128,128]{2,1,0:T(8,128)S(1)}, f32[8,128,128]{2,1,0:T(8,128)S(1)}, u32[]{:S(2)}, u32[]{:S(2)}) collective-permute-start(f32[8,128,128]{2,1,0:T(8,128)S(1)} %shard_map.101.y_ref), channel_id=1, source_target_pairs={{0,1},{1,0},{2,3},{3,2},{4,5},{5,4},{6,7},{7,6},{8,9},{9,8},{10,11... | collective-permute-start | bytes 1572872 | tf_op jit(solution)/shard_map/ppermute | solution.py:332
  57.8 1.7 %shard_map.95.base_ref = f32[8,128,128]{2,1,0:T(8,128)S(1)} custom-call(f32[4]{0:T(128)S(1)} %copy-done.7, s32[1]{0:T(128)} %bitcast.here_ref, s32[8,7]{1,0:T(8,128)S(1)} %copy-done.6, f32[8,128,128]{2,1,0:T(8,128)S(1)} %get-tuple-element.15.y_ref, f32[8,128,128]{2,1,0:T(8,128)S(1)} %collective-permute-done.pair_ref, ...), custom_call_target="tpu_custom_call" | custom-call | flops 1000000000 | bytes 2621440 | tf_op jit(solution)/shard_map/pallas_call | solution.py:334
  59.7 1.0 shard_map.96.y_ref
  60.8 2.6 %collective-permute-start.2 = (f32[8,128,128]{2,1,0:T(8,128)S(1)}, f32[8,128,128]{2,1,0:T(8,128)S(1)}, u32[]{:S(2)}, u32[]{:S(2)}) collective-permute-start(f32[8,128,128]{2,1,0:T(8,128)S(1)} %shard_map.96.y_ref), channel_id=1, source_target_pairs={{0,1},{1,0},{2,3},{3,2},{4,5},{5,4},{6,7},{7,6},{8,9},{9,8},{10,11... | collective-permute-start | bytes 1572872 | tf_op jit(solution)/shard_map/ppermute | solution.py:332
  63.4 1.8 %shard_map.102.base_ref = f32[8,128,128]{2,1,0:T(8,128)S(1)} custom-call(f32[4]{0:T(128)S(1)} %copy-done.7, s32[1]{0:T(128)} %bitcast.here_ref, s32[8,7]{1,0:T(8,128)S(1)} %copy-done.6, f32[8,128,128]{2,1,0:T(8,128)S(1)} %shard_map.101.y_ref, f32[8,128,128]{2,1,0:T(8,128)S(1)} %collective-permute-done.8.pair_ref, ...), custom_call_target="tpu_custom_call" | custom-call | flops 1000000000 | bytes 2621440 | tf_op jit(solution)/shard_map/pallas_call | solution.py:334
  65.2 1.2 collective-permute-done.9.far_ref
  66.4 1.0 shard_map.103.y_ref
  67.4 2.3 %collective-permute-start.10 = (f32[8,128,128]{2,1,0:T(8,128)S(1)}, f32[8,128,128]{2,1,0:T(8,128)S(1)}, u32[]{:S(2)}, u32[]{:S(2)}) collective-permute-start(f32[8,128,128]{2,1,0:T(8,128)S(1)} %shard_map.103.y_ref), channel_id=1, source_target_pairs={{0,1},{1,0},{2,3},{3,2},{4,5},{5,4},{6,7},{7,6},{8,9},{9,8},{10,11... | collective-permute-start | bytes 1572872 | tf_op jit(solution)/shard_map/ppermute | solution.py:332
  69.7 1.7 %shard_map.97.base_ref = f32[8,128,128]{2,1,0:T(8,128)S(1)} custom-call(f32[4]{0:T(128)S(1)} %copy-done.7, s32[1]{0:T(128)} %bitcast.here_ref, s32[8,7]{1,0:T(8,128)S(1)} %copy-done.6, f32[8,128,128]{2,1,0:T(8,128)S(1)} %shard_map.96.y_ref, f32[8,128,128]{2,1,0:T(8,128)S(1)} %collective-permute-done.2.pair_ref, ...), custom_call_target="tpu_custom_call" | custom-call | flops 1000000000 | bytes 2621440 | tf_op jit(solution)/shard_map/pallas_call | solution.py:334
  72.0 1.0 shard_map.98.y_ref
  73.1 2.3 %collective-permute-start.4 = (f32[8,128,128]{2,1,0:T(8,128)S(1)}, f32[8,128,128]{2,1,0:T(8,128)S(1)}, u32[]{:S(2)}, u32[]{:S(2)}) collective-permute-start(f32[8,128,128]{2,1,0:T(8,128)S(1)} %shard_map.98.y_ref), channel_id=1, source_target_pairs={{0,1},{1,0},{2,3},{3,2},{4,5},{5,4},{6,7},{7,6},{8,9},{9,8},{10,11... | collective-permute-start | bytes 1572872 | tf_op jit(solution)/shard_map/ppermute | solution.py:332
  75.3 1.8 %shard_map.104.base_ref = f32[8,128,128]{2,1,0:T(8,128)S(1)} custom-call(f32[4]{0:T(128)S(1)} %copy-done.7, s32[1]{0:T(128)} %bitcast.here_ref, s32[8,7]{1,0:T(8,128)S(1)} %copy-done.6, f32[8,128,128]{2,1,0:T(8,128)S(1)} %shard_map.103.y_ref, f32[8,128,128]{2,1,0:T(8,128)S(1)} %collective-permute-done.10.pair_ref, ...), custom_call_target="tpu_custom_call" | custom-call | flops 1000000000 | bytes 2621440 | tf_op jit(solution)/shard_map/pallas_call | solution.py:334
  77.1 1.2 collective-permute-done.11.far_ref
  78.3 1.0 shard_map.105.rest_0_
  79.4 1.7 %shard_map.99.base_ref = f32[8,128,128]{2,1,0:T(8,128)S(1)} custom-call(f32[4]{0:T(128)S(1)} %copy-done.7, s32[1]{0:T(128)} %bitcast.here_ref, s32[8,7]{1,0:T(8,128)S(1)} %copy-done.6, f32[8,128,128]{2,1,0:T(8,128)S(1)} %shard_map.98.y_ref, f32[8,128,128]{2,1,0:T(8,128)S(1)} %collective-permute-done.4.pair_ref, ...), custom_call_target="tpu_custom_call" | custom-call | flops 1000000000 | bytes 2621440 | tf_op jit(solution)/shard_map/pallas_call | solution.py:334
  81.2 2.8 %collective-permute-done.5.far_ref = f32[8,128,128]{2,1,0:T(8,128)S(1)} collective-permute-done((f32[8,128,128]{2,1,0:T(8,128)S(1)}, f32[8,128,128]{2,1,0:T(8,128)S(1)}, u32[]{:S(2)}, u32[]{:S(2)}) %collective-permute-start.5) | collective-permute-done | bytes 524320 | tf_op jit(solution)/shard_map/ppermute | solution.py:333
  84.0 1.1 shard_map.106
  85.0 19.8 %all_to_all.22.y_ref = f32[8,256,128]{2,1,0:T(8,128)S(1)} all-to-all(f32[8,256,128]{2,1,0:T(8,128)S(1)} %shard_map.106), channel_id=1, replica_groups=mesh['tm'=8,'space'=16] {'tm'}, dimensions={0} | all-to-all | bytes 2097152 | tf_op jit(solution)/shard_map/all_to_all | solution.py:303
  105.8 21.3 %all_to_all.23 = f32[8,256,128]{2,1,0:T(8,128)S(1)} all-to-all(f32[8,256,128]{2,1,0:T(8,128)S(1)} %shard_map.107), channel_id=1, replica_groups=mesh['tm'=8,'space'=16] {'tm'}, dimensions={0} | all-to-all | bytes 2097152 | tf_op jit(solution)/shard_map/all_to_all | solution.py:303
  (38 shorter events, 8.1 us)
Async XLA Ops:
  0.0 44.3 %copy-start.1 = (bf16[8,256,256]{2,1,0:T(8,128)(2,1)S(1)}, bf16[8,256,256]{2,1,0:T(8,128)(2,1)}, u32[]{:S(2)}) copy-start(bf16[8,256,256]{2,1,0:T(8,128)(2,1)} %constant.23.clone.high_ref) | copy-start | bytes 3145732
  0.0 44.3 %copy-start.2 = (bf16[8,256,256]{2,1,0:T(8,128)(2,1)S(1)}, bf16[8,256,256]{2,1,0:T(8,128)(2,1)}, u32[]{:S(2)}) copy-start(bf16[8,256,256]{2,1,0:T(8,128)(2,1)} %constant.24.clone.low_ref) | copy-start | bytes 3145732
  0.0 44.3 %copy-start = (f32[2,3,64,128]{3,2,1,0:T(8,128)S(1)}, f32[2,3,64,128]{3,2,1,0:T(8,128)}, u32[]{:S(2)}) copy-start(f32[2,3,64,128]{3,2,1,0:T(8,128)} %constant.27.clone.shift_ref) | copy-start | bytes 589828
  0.0 44.3 %copy-start.7 = (f32[4]{0:T(128)S(1)}, f32[4]{0:T(128)}, u32[]{:S(2)}) copy-start(f32[4]{0:T(128)} %rates_ref.27) | copy-start | bytes 52
  44.3 4.1 %copy-start.3 = (f32[8,7,128,128]{3,2,1,0:T(8,128)S(1)}, f32[8,7,128,128]{3,2,1,0:T(8,128)}, u32[]{:S(2)}) copy-start(f32[8,7,128,128]{3,2,1,0:T(8,128)} %blocks_ref.1) | copy-start | bytes 11010052
  45.3 4.1 %copy-start.6 = (s32[8,7]{1,0:T(8,128)S(1)}, s32[8,7]{1,0:T(8,128)}, u32[]{:S(2)}) copy-start(s32[8,7]{1,0:T(8,128)} %nb_ref.23) | copy-start | bytes 676
  45.3 4.1 %collective-permute-start.6 = (f32[8,128,128]{2,1,0:T(8,128)S(1)}, f32[8,128,128]{2,1,0:T(8,128)S(1)}, u32[]{:S(2)}, u32[]{:S(2)}) collective-permute-start(f32[8,128,128]{2,1,0:T(8,128)S(1)} %get-tuple-element.17._.y_ref), channel_id=1, source_target_pairs={{0,1},{1,0},{2,3},{3,2},{4,5},{5,4},{6,7},{7,6},{8,9},{9,8},{10,11... | collective-permute-start | bytes 1572872 | tf_op jit(solution)/shard_map/ppermute | solution.py:332
  45.4 8.7 %collective-permute-start.7 = (f32[8,128,128]{2,1,0:T(8,128)S(1)}, f32[8,128,128]{2,1,0:T(8,128)S(1)}, u32[]{:S(2)}, u32[]{:S(2)}) collective-permute-start(f32[8,128,128]{2,1,0:T(8,128)S(1)} %get-tuple-element.17._.y_ref), channel_id=1, source_target_pairs={{0,15},{1,2},{2,1},{3,4},{4,3},{5,6},{6,5},{7,8},{8,7},{9,10},{10,... | collective-permute-start | bytes 1572872 | tf_op jit(solution)/shard_map/ppermute | solution.py:333
  47.4 10.4 %collective-permute-start = (f32[8,128,128]{2,1,0:T(8,128)S(1)}, f32[8,128,128]{2,1,0:T(8,128)S(1)}, u32[]{:S(2)}, u32[]{:S(2)}) collective-permute-start(f32[8,128,128]{2,1,0:T(8,128)S(1)} %get-tuple-element.15.y_ref), channel_id=1, source_target_pairs={{0,1},{1,0},{2,3},{3,2},{4,5},{5,4},{6,7},{7,6},{8,9},{9,8},{10,11... | collective-permute-start | bytes 1572872 | tf_op jit(solution)/shard_map/ppermute | solution.py:332
  47.5 12.3 %collective-permute-start.1 = (f32[8,128,128]{2,1,0:T(8,128)S(1)}, f32[8,128,128]{2,1,0:T(8,128)S(1)}, u32[]{:S(2)}, u32[]{:S(2)}) collective-permute-start(f32[8,128,128]{2,1,0:T(8,128)S(1)} %get-tuple-element.15.y_ref), channel_id=1, source_target_pairs={{0,15},{1,2},{2,1},{3,4},{4,3},{5,6},{6,5},{7,8},{8,7},{9,10},{10,... | collective-permute-start | bytes 1572872 | tf_op jit(solution)/shard_map/ppermute | solution.py:333
  55.2 8.2 %collective-permute-start.8 = (f32[8,128,128]{2,1,0:T(8,128)S(1)}, f32[8,128,128]{2,1,0:T(8,128)S(1)}, u32[]{:S(2)}, u32[]{:S(2)}) collective-permute-start(f32[8,128,128]{2,1,0:T(8,128)S(1)} %shard_map.101.y_ref), channel_id=1, source_target_pairs={{0,1},{1,0},{2,3},{3,2},{4,5},{5,4},{6,7},{7,6},{8,9},{9,8},{10,11... | collective-permute-start | bytes 1572872 | tf_op jit(solution)/shard_map/ppermute | solution.py:332
  57.8 8.6 %collective-permute-start.9 = (f32[8,128,128]{2,1,0:T(8,128)S(1)}, f32[8,128,128]{2,1,0:T(8,128)S(1)}, u32[]{:S(2)}, u32[]{:S(2)}) collective-permute-start(f32[8,128,128]{2,1,0:T(8,128)S(1)} %shard_map.101.y_ref), channel_id=1, source_target_pairs={{0,15},{1,2},{2,1},{3,4},{4,3},{5,6},{6,5},{7,8},{8,7},{9,10},{10,... | collective-permute-start | bytes 1572872 | tf_op jit(solution)/shard_map/ppermute | solution.py:333
  60.8 8.9 %collective-permute-start.2 = (f32[8,128,128]{2,1,0:T(8,128)S(1)}, f32[8,128,128]{2,1,0:T(8,128)S(1)}, u32[]{:S(2)}, u32[]{:S(2)}) collective-permute-start(f32[8,128,128]{2,1,0:T(8,128)S(1)} %shard_map.96.y_ref), channel_id=1, source_target_pairs={{0,1},{1,0},{2,3},{3,2},{4,5},{5,4},{6,7},{7,6},{8,9},{9,8},{10,11... | collective-permute-start | bytes 1572872 | tf_op jit(solution)/shard_map/ppermute | solution.py:332
  63.4 8.6 %collective-permute-start.3 = (f32[8,128,128]{2,1,0:T(8,128)S(1)}, f32[8,128,128]{2,1,0:T(8,128)S(1)}, u32[]{:S(2)}, u32[]{:S(2)}) collective-permute-start(f32[8,128,128]{2,1,0:T(8,128)S(1)} %shard_map.96.y_ref), channel_id=1, source_target_pairs={{0,15},{1,2},{2,1},{3,4},{4,3},{5,6},{6,5},{7,8},{8,7},{9,10},{10,... | collective-permute-start | bytes 1572872 | tf_op jit(solution)/shard_map/ppermute | solution.py:333
  67.4 7.9 %collective-permute-start.10 = (f32[8,128,128]{2,1,0:T(8,128)S(1)}, f32[8,128,128]{2,1,0:T(8,128)S(1)}, u32[]{:S(2)}, u32[]{:S(2)}) collective-permute-start(f32[8,128,128]{2,1,0:T(8,128)S(1)} %shard_map.103.y_ref), channel_id=1, source_target_pairs={{0,1},{1,0},{2,3},{3,2},{4,5},{5,4},{6,7},{7,6},{8,9},{9,8},{10,11... | collective-permute-start | bytes 1572872 | tf_op jit(solution)/shard_map/ppermute | solution.py:332
  69.7 8.6 %collective-permute-start.11 = (f32[8,128,128]{2,1,0:T(8,128)S(1)}, f32[8,128,128]{2,1,0:T(8,128)S(1)}, u32[]{:S(2)}, u32[]{:S(2)}) collective-permute-start(f32[8,128,128]{2,1,0:T(8,128)S(1)} %shard_map.103.y_ref), channel_id=1, source_target_pairs={{0,15},{1,2},{2,1},{3,4},{4,3},{5,6},{6,5},{7,8},{8,7},{9,10},{10,... | collective-permute-start | bytes 1572872 | tf_op jit(solution)/shard_map/ppermute | solution.py:333
  73.1 6.3 %collective-permute-start.4 = (f32[8,128,128]{2,1,0:T(8,128)S(1)}, f32[8,128,128]{2,1,0:T(8,128)S(1)}, u32[]{:S(2)}, u32[]{:S(2)}) collective-permute-start(f32[8,128,128]{2,1,0:T(8,128)S(1)} %shard_map.98.y_ref), channel_id=1, source_target_pairs={{0,1},{1,0},{2,3},{3,2},{4,5},{5,4},{6,7},{7,6},{8,9},{9,8},{10,11... | collective-permute-start | bytes 1572872 | tf_op jit(solution)/shard_map/ppermute | solution.py:332
  75.3 8.6 %collective-permute-start.5 = (f32[8,128,128]{2,1,0:T(8,128)S(1)}, f32[8,128,128]{2,1,0:T(8,128)S(1)}, u32[]{:S(2)}, u32[]{:S(2)}) collective-permute-start(f32[8,128,128]{2,1,0:T(8,128)S(1)} %shard_map.98.y_ref), channel_id=1, source_target_pairs={{0,15},{1,2},{2,1},{3,4},{4,3},{5,6},{6,5},{7,8},{8,7},{9,10},{10,... | collective-permute-start | bytes 1572872 | tf_op jit(solution)/shard_map/ppermute | solution.py:333
  81.1 23.6 %copy-start.4 = (bf16[8,256,256]{2,1,0:T(8,128)(2,1)S(1)}, bf16[8,256,256]{2,1,0:T(8,128)(2,1)}, u32[]{:S(2)}) copy-start(bf16[8,256,256]{2,1,0:T(8,128)(2,1)} %constant.25.clone.high_ref) | copy-start | bytes 3145732
  81.2 23.6 %copy-start.5 = (bf16[8,256,256]{2,1,0:T(8,128)(2,1)S(1)}, bf16[8,256,256]{2,1,0:T(8,128)(2,1)}, u32[]{:S(2)}) copy-start(bf16[8,256,256]{2,1,0:T(8,128)(2,1)} %constant.26.clone.low_ref) | copy-start | bytes 3145732

commit v5 on v4

--- a/solution.py
+++ b/solution.py
@@ -237,7 +237,7 @@
             split_ref[place * PLANE + e, :ROWS] = high
             split_ref[place * PLANE + e, ROWS:] = low
     for e in range(PLANE):
-        picked = [nb_ref[e, s] % PLANE for s in OWN_SLOTS] + [PLANE + nb_ref[e, 2 - core] % PLANE]
+        picked = [nb_ref[e, s] % PLANE for s in OWN_SLOTS] + [PLANE + jnp.where(core == 0, nb_ref[e, 2], nb_ref[e, 1]) % PLANE]
         product = dot(jnp.concatenate([split_ref[i] for i in picked], 1), weights_ref[e])
         out_ref[e] = (
             spec_ref[e]
@@ -251,9 +251,8 @@
     apply = solved(here_ref, shift_ref, part, STEP_SCALE * rates_ref[sweep])
     out_ref = rest[-1]
     for e in range(PLANE):
-        product = dot(
-            jnp.concatenate(split(far_ref[nb_ref[e, 1 + core] % PLANE]), 0), weights_ref[e]
-        )
+        picked = jnp.where(core == 0, nb_ref[e, 1], nb_ref[e, 2]) % PLANE
+        product = dot(jnp.concatenate(split(far_ref[picked]), 0), weights_ref[e])
         result = apply(base_ref[e] - (STEP_SCALE * BLOCK_WEIGHT) * folded(product))
         if len(rest) == 1:
             out_ref[e] = result
@@ -265,10 +264,6 @@
 
 def whole(count):
     return [pl.BlockSpec(memory_space=pltpu.VMEM)] * count
-
-
-def scalars(count):
-    return [pl.BlockSpec(memory_space=pltpu.SMEM)] * count
 
 
 def call(kernel, outs, specs, flops, moved, scratch=()):
@@ -308,7 +303,7 @@
             call(
                 functools.partial(first_kernel, part),
                 (STATE, STATE),
-                scalars(2) + whole(4),
+                whole(6),
                 10**9 // PARTS,
                 4 * MIB // PARTS,
             )(shift_rates, here, series, forward_high, forward_low, shifts)
@@ -322,7 +317,7 @@
             jax.ShapeDtypeStruct((PLANE, 6 * NODES, 2 * NODES), jnp.bfloat16),
             jax.ShapeDtypeStruct((PLANE, NODES, 2 * NODES), jnp.bfloat16),
         ),
-        scalars(1) + whole(1) + [pl.BlockSpec(memory_space=pl.ANY)],
+        whole(2) + [pl.BlockSpec(memory_space=pl.ANY)],
         0,
         8 * MIB,
     )(here, blocks, states[0])
@@ -334,7 +329,7 @@
             base = call(
                 functools.partial(near_kernel, part, sweep),
                 STATE,
-                scalars(3) + whole(4),
+                whole(7),
                 2 * 10**9 // PARTS,
                 5 * MIB // PARTS,
                 [pltpu.VMEM((2 * PLANE, 2 * ROWS, NODES), jnp.bfloat16)],
@@ -344,7 +339,7 @@
             states[part] = call(
                 functools.partial(far_kernel, part, sweep),
                 STEPS if last else STATE,
-                scalars(3) + whole(4 + len(others)),
+                whole(7 + len(others)),
                 10**9 // PARTS,
                 3 * MIB // PARTS,
             )(shift_rates, here, neighbors, base, far, shifts, far_weights, *others)

time: 128 us -> 126 us (0.984)
  Pallas kernels: 21 us -> 13.6 us
  waiting for transfers between devices: 8.85 us -> 14.3 us
    ppermute x6, waiting for transfers between devices: 8.84 us -> 14.2 us  [per_device(): far = lax.ppermute(state, 'space', off_chip)]
    pallas_call x8, Pallas kernels: 12.5 us -> 8.06 us  [the longest x6 7.08 us: per_device(): call(functools.partial(near_kernel, part, sweep), STATE, whole(7), 2 * 10...]
    pallas_call x6, Pallas kernels: 6.27 us -> 3.27 us  [per_device(): call(functools.partial(far_kernel, part, sweep), STEPS if last else STATE...]
  transfers between devices with their start and end apart: 12 -> 12, of which waited for: 6 -> 6; matrix products, arithmetic and copies ran while one was open for 0% -> 0% of each run, Pallas kernels for 14% -> 9%
where the time goes in v5:
time: 126 us
  blocking collectives  85 us (67%)
  waiting for transfers between devices  14.3 us (11%)
  Pallas kernels  13.6 us (11%)
  starting transfers between devices  11.9 us (9%)
    all_to_all x4, blocking collectives, exchange(): return lax.all_to_all(value, 'tm', 0, 0, tiled=True)  85 us
    ppermute x6, waiting for transfers between devices, per_device(): far = lax.ppermute(state, 'space', off_chip)  14.2 us
    ppermute x6, starting transfers between devices, per_device(): pair = lax.ppermute(state, 'space', on_chip)  9.95 us
    pallas_call x6, Pallas kernels, per_device(): call(functools.partial(near_kernel, part, sweep), STATE, whole(7), 2 * 10...  7.08 us
    pallas_call x6, Pallas kernels, per_device(): call(functools.partial(far_kernel, part, sweep), STEPS if last else STATE...  3.27 us
  transfers between devices with their start and end apart: 12, of which 6 were waited for; matrix products, arithmetic and copies ran while one was open for 0% of the time, Pallas kernels for 9%

profile of v5, /device:TPU:6, one launch (start us, length us, event | category | flops | bytes accessed | tf_op | source)
XLA Modules:
  0.0 126.0 jit_solution(490887712595126872)
XLA Ops:
  0.0 25.3 %all_to_all.20.x_ref = f32[8,256,128]{2,1,0:T(8,128)S(1)} all-to-all(f32[8,256,128]{2,1,0:T(8,128)} %param.9), channel_id=1, replica_groups=mesh['tm'=8,'space'=16] {'tm'}, dimensions={0} | all-to-all | bytes 2097152 | tf_op jit(solution)/shard_map/all_to_all | solution.py:298
  25.6 18.7 %all_to_all.21.series_ref = f32[8,256,128]{2,1,0:T(8,128)S(1)} all-to-all(f32[8,256,128]{2,1,0:T(8,128)S(1)} %shard_map.91), channel_id=1, replica_groups=mesh['tm'=8,'space'=16] {'tm'}, dimensions={0} | all-to-all | bytes 2097152 | tf_op jit(solution)/shard_map/all_to_all | solution.py:298
  46.5 1.0 collective-permute-start.1
  47.4 1.0 shard_map.94
  48.5 1.2 shard_map.100.base_ref
  49.7 4.0 %collective-permute-done.7.far_ref = f32[8,128,128]{2,1,0:T(8,128)S(1)} collective-permute-done((f32[8,128,128]{2,1,0:T(8,128)S(1)}, f32[8,128,128]{2,1,0:T(8,128)S(1)}, u32[]{:S(2)}, u32[]{:S(2)}) %collective-permute-start.7) | collective-permute-done | bytes 524320 | tf_op jit(solution)/shard_map/ppermute | solution.py:328
  54.2 2.6 %collective-permute-start.8 = (f32[8,128,128]{2,1,0:T(8,128)S(1)}, f32[8,128,128]{2,1,0:T(8,128)S(1)}, u32[]{:S(2)}, u32[]{:S(2)}) collective-permute-start(f32[8,128,128]{2,1,0:T(8,128)S(1)} %shard_map.101.y_ref), channel_id=1, source_target_pairs={{0,1},{1,0},{2,3},{3,2},{4,5},{5,4},{6,7},{7,6},{8,9},{9,8},{10,11... | collective-permute-start | bytes 1572872 | tf_op jit(solution)/shard_map/ppermute | solution.py:327
  56.8 1.2 shard_map.95.base_ref
  58.0 1.3 %collective-permute-done.1.far_ref = f32[8,128,128]{2,1,0:T(8,128)S(1)} collective-permute-done((f32[8,128,128]{2,1,0:T(8,128)S(1)}, f32[8,128,128]{2,1,0:T(8,128)S(1)}, u32[]{:S(2)}, u32[]{:S(2)}) %collective-permute-start.1) | collective-permute-done | bytes 524320 | tf_op jit(solution)/shard_map/ppermute | solution.py:328
  59.8 2.6 %collective-permute-start.2 = (f32[8,128,128]{2,1,0:T(8,128)S(1)}, f32[8,128,128]{2,1,0:T(8,128)S(1)}, u32[]{:S(2)}, u32[]{:S(2)}) collective-permute-start(f32[8,128,128]{2,1,0:T(8,128)S(1)} %shard_map.96.y_ref), channel_id=1, source_target_pairs={{0,1},{1,0},{2,3},{3,2},{4,5},{5,4},{6,7},{7,6},{8,9},{9,8},{10,11... | collective-permute-start | bytes 1572872 | tf_op jit(solution)/shard_map/ppermute | solution.py:327
  62.4 1.2 shard_map.102.base_ref
  63.6 1.8 %collective-permute-done.9.far_ref = f32[8,128,128]{2,1,0:T(8,128)S(1)} collective-permute-done((f32[8,128,128]{2,1,0:T(8,128)S(1)}, f32[8,128,128]{2,1,0:T(8,128)S(1)}, u32[]{:S(2)}, u32[]{:S(2)}) %collective-permute-start.9) | collective-permute-done | bytes 524320 | tf_op jit(solution)/shard_map/ppermute | solution.py:328
  65.9 2.3 %collective-permute-start.10 = (f32[8,128,128]{2,1,0:T(8,128)S(1)}, f32[8,128,128]{2,1,0:T(8,128)S(1)}, u32[]{:S(2)}, u32[]{:S(2)}) collective-permute-start(f32[8,128,128]{2,1,0:T(8,128)S(1)} %shard_map.103.y_ref), channel_id=1, source_target_pairs={{0,1},{1,0},{2,3},{3,2},{4,5},{5,4},{6,7},{7,6},{8,9},{9,8},{10,11... | collective-permute-start | bytes 1572872 | tf_op jit(solution)/shard_map/ppermute | solution.py:327
  68.2 1.2 shard_map.97.base_ref
  69.4 1.6 %collective-permute-done.3.far_ref = f32[8,128,128]{2,1,0:T(8,128)S(1)} collective-permute-done((f32[8,128,128]{2,1,0:T(8,128)S(1)}, f32[8,128,128]{2,1,0:T(8,128)S(1)}, u32[]{:S(2)}, u32[]{:S(2)}) %collective-permute-start.3) | collective-permute-done | bytes 524320 | tf_op jit(solution)/shard_map/ppermute | solution.py:328
  71.6 2.3 %collective-permute-start.4 = (f32[8,128,128]{2,1,0:T(8,128)S(1)}, f32[8,128,128]{2,1,0:T(8,128)S(1)}, u32[]{:S(2)}, u32[]{:S(2)}) collective-permute-start(f32[8,128,128]{2,1,0:T(8,128)S(1)} %shard_map.98.y_ref), channel_id=1, source_target_pairs={{0,1},{1,0},{2,3},{3,2},{4,5},{5,4},{6,7},{7,6},{8,9},{9,8},{10,11... | collective-permute-start | bytes 1572872 | tf_op jit(solution)/shard_map/ppermute | solution.py:327
  73.8 1.2 shard_map.104.base_ref
  75.0 1.8 %collective-permute-done.11.far_ref = f32[8,128,128]{2,1,0:T(8,128)S(1)} collective-permute-done((f32[8,128,128]{2,1,0:T(8,128)S(1)}, f32[8,128,128]{2,1,0:T(8,128)S(1)}, u32[]{:S(2)}, u32[]{:S(2)}) %collective-permute-start.11) | collective-permute-done | bytes 524320 | tf_op jit(solution)/shard_map/ppermute | solution.py:328
  77.4 1.2 shard_map.99.base_ref
  78.6 3.8 %collective-permute-done.5.far_ref = f32[8,128,128]{2,1,0:T(8,128)S(1)} collective-permute-done((f32[8,128,128]{2,1,0:T(8,128)S(1)}, f32[8,128,128]{2,1,0:T(8,128)S(1)}, u32[]{:S(2)}, u32[]{:S(2)}) %collective-permute-start.5) | collective-permute-done | bytes 524320 | tf_op jit(solution)/shard_map/ppermute | solution.py:328
  83.0 19.8 %all_to_all.22.y_ref = f32[8,256,128]{2,1,0:T(8,128)S(1)} all-to-all(f32[8,256,128]{2,1,0:T(8,128)S(1)} %shard_map.106), channel_id=1, replica_groups=mesh['tm'=8,'space'=16] {'tm'}, dimensions={0} | all-to-all | bytes 2097152 | tf_op jit(solution)/shard_map/all_to_all | solution.py:298
  102.8 1.0 shard_map.107
  103.8 21.3 %all_to_all.23 = f32[8,256,128]{2,1,0:T(8,128)S(1)} all-to-all(f32[8,256,128]{2,1,0:T(8,128)S(1)} %shard_map.107), channel_id=1, replica_groups=mesh['tm'=8,'space'=16] {'tm'}, dimensions={0} | all-to-all | bytes 2097152 | tf_op jit(solution)/shard_map/all_to_all | solution.py:298
  125.1 1.0 copy.11
  (38 shorter events, 5.7 us)
Async XLA Ops:
  0.0 44.3 %copy-start.1 = (bf16[8,256,256]{2,1,0:T(8,128)(2,1)S(1)}, bf16[8,256,256]{2,1,0:T(8,128)(2,1)}, u32[]{:S(2)}) copy-start(bf16[8,256,256]{2,1,0:T(8,128)(2,1)} %constant.23.clone.high_ref) | copy-start | bytes 3145732
  0.0 44.3 %copy-start.2 = (bf16[8,256,256]{2,1,0:T(8,128)(2,1)S(1)}, bf16[8,256,256]{2,1,0:T(8,128)(2,1)}, u32[]{:S(2)}) copy-start(bf16[8,256,256]{2,1,0:T(8,128)(2,1)} %constant.24.clone.low_ref) | copy-start | bytes 3145732
  0.0 44.3 %copy-start = (f32[2,3,64,128]{3,2,1,0:T(8,128)S(1)}, f32[2,3,64,128]{3,2,1,0:T(8,128)}, u32[]{:S(2)}) copy-start(f32[2,3,64,128]{3,2,1,0:T(8,128)} %constant.27.clone.shift_ref) | copy-start | bytes 589828
  0.0 44.3 %copy-start.7 = (f32[4]{0:T(128)S(1)}, f32[4]{0:T(128)}, u32[]{:S(2)}) copy-start(f32[4]{0:T(128)} %rates_ref.27) | copy-start | bytes 52
  44.3 3.1 %copy-start.3 = (f32[8,7,128,128]{3,2,1,0:T(8,128)S(1)}, f32[8,7,128,128]{3,2,1,0:T(8,128)}, u32[]{:S(2)}) copy-start(f32[8,7,128,128]{3,2,1,0:T(8,128)} %blocks_ref.1) | copy-start | bytes 11010052
  44.8 3.6 %copy-start.6 = (s32[8,7]{1,0:T(8,128)S(1)}, s32[8,7]{1,0:T(8,128)}, u32[]{:S(2)}) copy-start(s32[8,7]{1,0:T(8,128)} %nb_ref.23) | copy-start | bytes 676
  44.8 3.6 %collective-permute-start.6 = (f32[8,128,128]{2,1,0:T(8,128)S(1)}, f32[8,128,128]{2,1,0:T(8,128)S(1)}, u32[]{:S(2)}, u32[]{:S(2)}) collective-permute-start(f32[8,128,128]{2,1,0:T(8,128)S(1)} %get-tuple-element.17._.y_ref), channel_id=1, source_target_pairs={{0,1},{1,0},{2,3},{3,2},{4,5},{5,4},{6,7},{7,6},{8,9},{9,8},{10,11... | collective-permute-start | bytes 1572872 | tf_op jit(solution)/shard_map/ppermute | solution.py:327
  44.9 8.7 %collective-permute-start.7 = (f32[8,128,128]{2,1,0:T(8,128)S(1)}, f32[8,128,128]{2,1,0:T(8,128)S(1)}, u32[]{:S(2)}, u32[]{:S(2)}) collective-permute-start(f32[8,128,128]{2,1,0:T(8,128)S(1)} %get-tuple-element.17._.y_ref), channel_id=1, source_target_pairs={{0,15},{1,2},{2,1},{3,4},{4,3},{5,6},{6,5},{7,8},{8,7},{9,10},{10,... | collective-permute-start | bytes 1572872 | tf_op jit(solution)/shard_map/ppermute | solution.py:328
  46.4 10.4 %collective-permute-start = (f32[8,128,128]{2,1,0:T(8,128)S(1)}, f32[8,128,128]{2,1,0:T(8,128)S(1)}, u32[]{:S(2)}, u32[]{:S(2)}) collective-permute-start(f32[8,128,128]{2,1,0:T(8,128)S(1)} %get-tuple-element.15.y_ref), channel_id=1, source_target_pairs={{0,1},{1,0},{2,3},{3,2},{4,5},{5,4},{6,7},{7,6},{8,9},{9,8},{10,11... | collective-permute-start | bytes 1572872 | tf_op jit(solution)/shard_map/ppermute | solution.py:327
  46.5 12.8 %collective-permute-start.1 = (f32[8,128,128]{2,1,0:T(8,128)S(1)}, f32[8,128,128]{2,1,0:T(8,128)S(1)}, u32[]{:S(2)}, u32[]{:S(2)}) collective-permute-start(f32[8,128,128]{2,1,0:T(8,128)S(1)} %get-tuple-element.15.y_ref), channel_id=1, source_target_pairs={{0,15},{1,2},{2,1},{3,4},{4,3},{5,6},{6,5},{7,8},{8,7},{9,10},{10,... | collective-permute-start | bytes 1572872 | tf_op jit(solution)/shard_map/ppermute | solution.py:328
  54.2 8.2 %collective-permute-start.8 = (f32[8,128,128]{2,1,0:T(8,128)S(1)}, f32[8,128,128]{2,1,0:T(8,128)S(1)}, u32[]{:S(2)}, u32[]{:S(2)}) collective-permute-start(f32[8,128,128]{2,1,0:T(8,128)S(1)} %shard_map.101.y_ref), channel_id=1, source_target_pairs={{0,1},{1,0},{2,3},{3,2},{4,5},{5,4},{6,7},{7,6},{8,9},{9,8},{10,11... | collective-permute-start | bytes 1572872 | tf_op jit(solution)/shard_map/ppermute | solution.py:327
  56.8 8.6 %collective-permute-start.9 = (f32[8,128,128]{2,1,0:T(8,128)S(1)}, f32[8,128,128]{2,1,0:T(8,128)S(1)}, u32[]{:S(2)}, u32[]{:S(2)}) collective-permute-start(f32[8,128,128]{2,1,0:T(8,128)S(1)} %shard_map.101.y_ref), channel_id=1, source_target_pairs={{0,15},{1,2},{2,1},{3,4},{4,3},{5,6},{6,5},{7,8},{8,7},{9,10},{10,... | collective-permute-start | bytes 1572872 | tf_op jit(solution)/shard_map/ppermute | solution.py:328
  59.8 8.4 %collective-permute-start.2 = (f32[8,128,128]{2,1,0:T(8,128)S(1)}, f32[8,128,128]{2,1,0:T(8,128)S(1)}, u32[]{:S(2)}, u32[]{:S(2)}) collective-permute-start(f32[8,128,128]{2,1,0:T(8,128)S(1)} %shard_map.96.y_ref), channel_id=1, source_target_pairs={{0,1},{1,0},{2,3},{3,2},{4,5},{5,4},{6,7},{7,6},{8,9},{9,8},{10,11... | collective-permute-start | bytes 1572872 | tf_op jit(solution)/shard_map/ppermute | solution.py:327
  62.4 8.6 %collective-permute-start.3 = (f32[8,128,128]{2,1,0:T(8,128)S(1)}, f32[8,128,128]{2,1,0:T(8,128)S(1)}, u32[]{:S(2)}, u32[]{:S(2)}) collective-permute-start(f32[8,128,128]{2,1,0:T(8,128)S(1)} %shard_map.96.y_ref), channel_id=1, source_target_pairs={{0,15},{1,2},{2,1},{3,4},{4,3},{5,6},{6,5},{7,8},{8,7},{9,10},{10,... | collective-permute-start | bytes 1572872 | tf_op jit(solution)/shard_map/ppermute | solution.py:328
  65.9 7.9 %collective-permute-start.10 = (f32[8,128,128]{2,1,0:T(8,128)S(1)}, f32[8,128,128]{2,1,0:T(8,128)S(1)}, u32[]{:S(2)}, u32[]{:S(2)}) collective-permute-start(f32[8,128,128]{2,1,0:T(8,128)S(1)} %shard_map.103.y_ref), channel_id=1, source_target_pairs={{0,1},{1,0},{2,3},{3,2},{4,5},{5,4},{6,7},{7,6},{8,9},{9,8},{10,11... | collective-permute-start | bytes 1572872 | tf_op jit(solution)/shard_map/ppermute | solution.py:327
  68.2 8.6 %collective-permute-start.11 = (f32[8,128,128]{2,1,0:T(8,128)S(1)}, f32[8,128,128]{2,1,0:T(8,128)S(1)}, u32[]{:S(2)}, u32[]{:S(2)}) collective-permute-start(f32[8,128,128]{2,1,0:T(8,128)S(1)} %shard_map.103.y_ref), channel_id=1, source_target_pairs={{0,15},{1,2},{2,1},{3,4},{4,3},{5,6},{6,5},{7,8},{8,7},{9,10},{10,... | collective-permute-start | bytes 1572872 | tf_op jit(solution)/shard_map/ppermute | solution.py:328
  71.6 5.8 %collective-permute-start.4 = (f32[8,128,128]{2,1,0:T(8,128)S(1)}, f32[8,128,128]{2,1,0:T(8,128)S(1)}, u32[]{:S(2)}, u32[]{:S(2)}) collective-permute-start(f32[8,128,128]{2,1,0:T(8,128)S(1)} %shard_map.98.y_ref), channel_id=1, source_target_pairs={{0,1},{1,0},{2,3},{3,2},{4,5},{5,4},{6,7},{7,6},{8,9},{9,8},{10,11... | collective-permute-start | bytes 1572872 | tf_op jit(solution)/shard_map/ppermute | solution.py:327
  73.8 8.6 %collective-permute-start.5 = (f32[8,128,128]{2,1,0:T(8,128)S(1)}, f32[8,128,128]{2,1,0:T(8,128)S(1)}, u32[]{:S(2)}, u32[]{:S(2)}) collective-permute-start(f32[8,128,128]{2,1,0:T(8,128)S(1)} %shard_map.98.y_ref), channel_id=1, source_target_pairs={{0,15},{1,2},{2,1},{3,4},{4,3},{5,6},{6,5},{7,8},{8,7},{9,10},{10,... | collective-permute-start | bytes 1572872 | tf_op jit(solution)/shard_map/ppermute | solution.py:328
  78.6 24.2 %copy-start.4 = (bf16[8,256,256]{2,1,0:T(8,128)(2,1)S(1)}, bf16[8,256,256]{2,1,0:T(8,128)(2,1)}, u32[]{:S(2)}) copy-start(bf16[8,256,256]{2,1,0:T(8,128)(2,1)} %constant.25.clone.high_ref) | copy-start | bytes 3145732
  78.6 24.2 %copy-start.5 = (bf16[8,256,256]{2,1,0:T(8,128)(2,1)S(1)}, bf16[8,256,256]{2,1,0:T(8,128)(2,1)}, u32[]{:S(2)}) copy-start(bf16[8,256,256]{2,1,0:T(8,128)(2,1)} %constant.26.clone.low_ref) | copy-start | bytes 3145732

commit v6 on v5

--- a/solution.py
+++ b/solution.py
@@ -138,10 +138,17 @@
 
 
 CHUNK = 16
-
-
-def steps_at(q, row):
-    return q // 2, pl.ds(q % 2 * HALF + row, CHUNK), slice(None)
+ORDERS = ((0, 4, 2, 6, 3, 7, 1, 5), (5, 1, 7, 3, 6, 2, 4, 0))
+
+
+def places_of(here_ref):
+    return [
+        jnp.where(here_ref[0] % 2 == 0, ORDERS[0].index(p), ORDERS[1].index(p)) for p in range(8)
+    ]
+
+
+def steps_at(places, q, row):
+    return places[q // 2], pl.ds(q % 2 * HALF + row, CHUNK), slice(None)
 
 
 def table_product(high, low, value):
@@ -150,19 +157,22 @@
     return both[:, :NODES] + both[:, NODES:] + dot(low, value_high)
 
 
-def forward_kernel(x_ref, out_ref):
+def forward_kernel(here_ref, x_ref, out_ref):
+    places = places_of(here_ref)
+
     @pl.loop(0, HALF // CHUNK)
     def _(step):
         row = pl.multiple_of(step * CHUNK, CHUNK)
-        series = [x_ref[steps_at(q, row)] * BLOCK_GROWTH[q] for q in range(16)]
+        series = [x_ref[steps_at(places, q, row)] * BLOCK_GROWTH[q] for q in range(16)]
         for c, (real, imag) in enumerate(real_dft16(series)):
-            out_ref[c, pl.ds(row, CHUNK), :] = real
-            out_ref[c, pl.ds(HALF + row, CHUNK), :] = imag
-
-
-def inverse_kernel(y_ref, high_ref, low_ref, out_ref, v_ref):
+            out_ref[places[c], pl.ds(row, CHUNK), :] = real
+            out_ref[places[c], pl.ds(HALF + row, CHUNK), :] = imag
+
+
+def inverse_kernel(here_ref, y_ref, high_ref, low_ref, out_ref, v_ref):
+    places = places_of(here_ref)
     for c in range(CLASSES):
-        v_ref[c] = table_product(high_ref[c], low_ref[c], y_ref[c])
+        v_ref[c] = table_product(high_ref[c], low_ref[c], y_ref[places[c]])
 
     @pl.loop(0, HALF // CHUNK)
     def _(step):
@@ -172,7 +182,7 @@
             for c in range(CLASSES)
         ]
         for q, value in enumerate(real_idft16(pairs)):
-            out_ref[steps_at(q, row)] = value * (1.0 / BLOCK_GROWTH[q])
+            out_ref[steps_at(places, q, row)] = value * (1.0 / BLOCK_GROWTH[q])
 
 
 def weights_kernel(here_ref, blocks_ref, _, near_ref, far_ref):
@@ -292,12 +302,15 @@
     right_side, here = lax.optimization_barrier((right_side, here))
     ring = lax.axis_size("space")
     on_chip = [(i, i ^ 1) for i in range(ring)]
+    groups = [[p * ring + place for p in ORDERS[place % 2]] for place in range(ring)]
     off_chip = [(i, (i + 1 if i % 2 else i - 1) % ring) for i in range(ring)]
 
     def exchange(value):
-        return lax.all_to_all(value, "tm", 0, 0, tiled=True)
-
-    series = exchange(call(forward_kernel, STEPS, whole(1), 0, 2 * MIB)(exchange(right_side)))
+        return lax.all_to_all(
+            value, ("tm", "space"), 0, 0, tiled=True, axis_index_groups=groups
+        )
+
+    series = exchange(call(forward_kernel, STEPS, whole(2), 0, 2 * MIB)(here, exchange(right_side)))
     spectrum, states = zip(
         *(
             call(
@@ -346,11 +359,11 @@
     steps = call(
         inverse_kernel,
         STEPS,
-        whole(3),
+        whole(4),
         10**9,
         4 * MIB,
         [pltpu.VMEM((CLASSES, 256, NODES), jnp.float32)],
-    )(exchange(states[-1]), inverse_high, inverse_low)
+    )(here, exchange(states[-1]), inverse_high, inverse_low)
     return exchange(steps)
 
 

time: 126 us -> 123 us (0.976)
  blocking collectives: 85 us -> 82 us
    all_to_all x4, blocking collectives: 85 us -> 82 us  [exchange(): lax.all_to_all(value, ('tm', 'space'), 0, 0, tiled=True, axis_index_group...]
where the time goes in v6:
time: 123 us
  blocking collectives  82 us (67%)
  waiting for transfers between devices  14.3 us (12%)
  Pallas kernels  13.8 us (11%)
  starting transfers between devices  11.9 us (10%)
    all_to_all x4, blocking collectives, exchange(): lax.all_to_all(value, ('tm', 'space'), 0, 0, tiled=True, axis_index_group...  82 us
    ppermute x6, waiting for transfers between devices, per_device(): far = lax.ppermute(state, 'space', off_chip)  14.2 us
    ppermute x6, starting transfers between devices, per_device(): pair = lax.ppermute(state, 'space', on_chip)  9.95 us
    pallas_call x6, Pallas kernels, per_device(): call(functools.partial(near_kernel, part, sweep), STATE, whole(7), 2 * 10...  7.08 us
    pallas_call x6, Pallas kernels, per_device(): call(functools.partial(far_kernel, part, sweep), STEPS if last else STATE...  3.27 us
  transfers between devices with their start and end apart: 12, of which 6 were waited for; matrix products, arithmetic and copies ran while one was open for 0% of the time, Pallas kernels for 9%

profile of v6, /device:TPU:6, one launch (start us, length us, event | category | flops | bytes accessed | tf_op | source)
XLA Modules:
  0.0 123.2 jit_solution(8886166871884593140)
XLA Ops:
  0.0 22.3 %all_to_all.20.x_ref = f32[8,256,128]{2,1,0:T(8,128)S(1)} all-to-all(f32[8,256,128]{2,1,0:T(8,128)} %param.9), channel_id=1, replica_groups={{0,64,32,96,48,112,16,80},{81,17,113,49,97,33,65,1},{2,66,34,98,50,114,..., dimensions={0} | all-to-all | bytes 2097152 | tf_op jit(solution)/shard_map/all_to_all | solution.py:309
  22.7 18.9 %all_to_all.21.series_ref = f32[8,256,128]{2,1,0:T(8,128)S(1)} all-to-all(f32[8,256,128]{2,1,0:T(8,128)S(1)} %shard_map.91), channel_id=1, replica_groups={{0,64,32,96,48,112,16,80},{81,17,113,49,97,33,65,1},{2,66,34,98,50,114,..., dimensions={0} | all-to-all | bytes 2097152 | tf_op jit(solution)/shard_map/all_to_all | solution.py:309
  43.7 1.0 collective-permute-start.1
  44.7 1.0 shard_map.94
  45.8 1.2 shard_map.100.base_ref
  47.0 4.0 %collective-permute-done.7.far_ref = f32[8,128,128]{2,1,0:T(8,128)S(1)} collective-permute-done((f32[8,128,128]{2,1,0:T(8,128)S(1)}, f32[8,128,128]{2,1,0:T(8,128)S(1)}, u32[]{:S(2)}, u32[]{:S(2)}) %collective-permute-start.7) | collective-permute-done | bytes 524320 | tf_op jit(solution)/shard_map/ppermute | solution.py:341
  51.5 2.6 %collective-permute-start.8 = (f32[8,128,128]{2,1,0:T(8,128)S(1)}, f32[8,128,128]{2,1,0:T(8,128)S(1)}, u32[]{:S(2)}, u32[]{:S(2)}) collective-permute-start(f32[8,128,128]{2,1,0:T(8,128)S(1)} %shard_map.101.y_ref), channel_id=1, source_target_pairs={{0,1},{1,0},{2,3},{3,2},{4,5},{5,4},{6,7},{7,6},{8,9},{9,8},{10,11... | collective-permute-start | bytes 1572872 | tf_op jit(solution)/shard_map/ppermute | solution.py:340
  54.1 1.2 shard_map.95.base_ref
  55.3 1.3 %collective-permute-done.1.far_ref = f32[8,128,128]{2,1,0:T(8,128)S(1)} collective-permute-done((f32[8,128,128]{2,1,0:T(8,128)S(1)}, f32[8,128,128]{2,1,0:T(8,128)S(1)}, u32[]{:S(2)}, u32[]{:S(2)}) %collective-permute-start.1) | collective-permute-done | bytes 524320 | tf_op jit(solution)/shard_map/ppermute | solution.py:341
  57.1 2.6 %collective-permute-start.2 = (f32[8,128,128]{2,1,0:T(8,128)S(1)}, f32[8,128,128]{2,1,0:T(8,128)S(1)}, u32[]{:S(2)}, u32[]{:S(2)}) collective-permute-start(f32[8,128,128]{2,1,0:T(8,128)S(1)} %shard_map.96.y_ref), channel_id=1, source_target_pairs={{0,1},{1,0},{2,3},{3,2},{4,5},{5,4},{6,7},{7,6},{8,9},{9,8},{10,11... | collective-permute-start | bytes 1572872 | tf_op jit(solution)/shard_map/ppermute | solution.py:340
  59.7 1.2 shard_map.102.base_ref
  60.9 1.8 %collective-permute-done.9.far_ref = f32[8,128,128]{2,1,0:T(8,128)S(1)} collective-permute-done((f32[8,128,128]{2,1,0:T(8,128)S(1)}, f32[8,128,128]{2,1,0:T(8,128)S(1)}, u32[]{:S(2)}, u32[]{:S(2)}) %collective-permute-start.9) | collective-permute-done | bytes 524320 | tf_op jit(solution)/shard_map/ppermute | solution.py:341
  63.2 2.3 %collective-permute-start.10 = (f32[8,128,128]{2,1,0:T(8,128)S(1)}, f32[8,128,128]{2,1,0:T(8,128)S(1)}, u32[]{:S(2)}, u32[]{:S(2)}) collective-permute-start(f32[8,128,128]{2,1,0:T(8,128)S(1)} %shard_map.103.y_ref), channel_id=1, source_target_pairs={{0,1},{1,0},{2,3},{3,2},{4,5},{5,4},{6,7},{7,6},{8,9},{9,8},{10,11... | collective-permute-start | bytes 1572872 | tf_op jit(solution)/shard_map/ppermute | solution.py:340
  65.5 1.2 shard_map.97.base_ref
  66.7 1.6 %collective-permute-done.3.far_ref = f32[8,128,128]{2,1,0:T(8,128)S(1)} collective-permute-done((f32[8,128,128]{2,1,0:T(8,128)S(1)}, f32[8,128,128]{2,1,0:T(8,128)S(1)}, u32[]{:S(2)}, u32[]{:S(2)}) %collective-permute-start.3) | collective-permute-done | bytes 524320 | tf_op jit(solution)/shard_map/ppermute | solution.py:341
  68.9 2.3 %collective-permute-start.4 = (f32[8,128,128]{2,1,0:T(8,128)S(1)}, f32[8,128,128]{2,1,0:T(8,128)S(1)}, u32[]{:S(2)}, u32[]{:S(2)}) collective-permute-start(f32[8,128,128]{2,1,0:T(8,128)S(1)} %shard_map.98.y_ref), channel_id=1, source_target_pairs={{0,1},{1,0},{2,3},{3,2},{4,5},{5,4},{6,7},{7,6},{8,9},{9,8},{10,11... | collective-permute-start | bytes 1572872 | tf_op jit(solution)/shard_map/ppermute | solution.py:340
  71.1 1.2 shard_map.104.base_ref
  72.3 1.8 %collective-permute-done.11.far_ref = f32[8,128,128]{2,1,0:T(8,128)S(1)} collective-permute-done((f32[8,128,128]{2,1,0:T(8,128)S(1)}, f32[8,128,128]{2,1,0:T(8,128)S(1)}, u32[]{:S(2)}, u32[]{:S(2)}) %collective-permute-start.11) | collective-permute-done | bytes 524320 | tf_op jit(solution)/shard_map/ppermute | solution.py:341
  74.7 1.2 shard_map.99.base_ref
  75.9 3.8 %collective-permute-done.5.far_ref = f32[8,128,128]{2,1,0:T(8,128)S(1)} collective-permute-done((f32[8,128,128]{2,1,0:T(8,128)S(1)}, f32[8,128,128]{2,1,0:T(8,128)S(1)}, u32[]{:S(2)}, u32[]{:S(2)}) %collective-permute-start.5) | collective-permute-done | bytes 524320 | tf_op jit(solution)/shard_map/ppermute | solution.py:341
  80.3 21.7 %all_to_all.22.y_ref = f32[8,256,128]{2,1,0:T(8,128)S(1)} all-to-all(f32[8,256,128]{2,1,0:T(8,128)S(1)} %shard_map.106), channel_id=1, replica_groups={{0,64,32,96,48,112,16,80},{81,17,113,49,97,33,65,1},{2,66,34,98,50,114,..., dimensions={0} | all-to-all | bytes 2097152 | tf_op jit(solution)/shard_map/all_to_all | solution.py:309
  102.0 1.1 shard_map.107
  103.1 19.1 %all_to_all.23 = f32[8,256,128]{2,1,0:T(8,128)S(1)} all-to-all(f32[8,256,128]{2,1,0:T(8,128)S(1)} %shard_map.107), channel_id=1, replica_groups={{0,64,32,96,48,112,16,80},{81,17,113,49,97,33,65,1},{2,66,34,98,50,114,..., dimensions={0} | all-to-all | bytes 2097152 | tf_op jit(solution)/shard_map/all_to_all | solution.py:309
  122.2 1.0 copy.11
  (38 shorter events, 5.8 us)
Async XLA Ops:
  0.0 41.6 %copy-start.1 = (bf16[8,256,256]{2,1,0:T(8,128)(2,1)S(1)}, bf16[8,256,256]{2,1,0:T(8,128)(2,1)}, u32[]{:S(2)}) copy-start(bf16[8,256,256]{2,1,0:T(8,128)(2,1)} %constant.23.clone.high_ref) | copy-start | bytes 3145732
  0.0 41.6 %copy-start.2 = (bf16[8,256,256]{2,1,0:T(8,128)(2,1)S(1)}, bf16[8,256,256]{2,1,0:T(8,128)(2,1)}, u32[]{:S(2)}) copy-start(bf16[8,256,256]{2,1,0:T(8,128)(2,1)} %constant.24.clone.low_ref) | copy-start | bytes 3145732
  0.0 41.6 %copy-start = (f32[2,3,64,128]{3,2,1,0:T(8,128)S(1)}, f32[2,3,64,128]{3,2,1,0:T(8,128)}, u32[]{:S(2)}) copy-start(f32[2,3,64,128]{3,2,1,0:T(8,128)} %constant.27.clone.shift_ref) | copy-start | bytes 589828
  0.0 41.6 %copy-start.7 = (f32[4]{0:T(128)S(1)}, f32[4]{0:T(128)}, u32[]{:S(2)}) copy-start(f32[4]{0:T(128)} %rates_ref.27) | copy-start | bytes 52
  41.6 3.1 %copy-start.3 = (f32[8,7,128,128]{3,2,1,0:T(8,128)S(1)}, f32[8,7,128,128]{3,2,1,0:T(8,128)}, u32[]{:S(2)}) copy-start(f32[8,7,128,128]{3,2,1,0:T(8,128)} %blocks_ref.1) | copy-start | bytes 11010052
  42.1 3.6 %copy-start.6 = (s32[8,7]{1,0:T(8,128)S(1)}, s32[8,7]{1,0:T(8,128)}, u32[]{:S(2)}) copy-start(s32[8,7]{1,0:T(8,128)} %nb_ref.23) | copy-start | bytes 676
  42.1 3.6 %collective-permute-start.6 = (f32[8,128,128]{2,1,0:T(8,128)S(1)}, f32[8,128,128]{2,1,0:T(8,128)S(1)}, u32[]{:S(2)}, u32[]{:S(2)}) collective-permute-start(f32[8,128,128]{2,1,0:T(8,128)S(1)} %get-tuple-element.17._.y_ref), channel_id=1, source_target_pairs={{0,1},{1,0},{2,3},{3,2},{4,5},{5,4},{6,7},{7,6},{8,9},{9,8},{10,11... | collective-permute-start | bytes 1572872 | tf_op jit(solution)/shard_map/ppermute | solution.py:340
  42.2 8.7 %collective-permute-start.7 = (f32[8,128,128]{2,1,0:T(8,128)S(1)}, f32[8,128,128]{2,1,0:T(8,128)S(1)}, u32[]{:S(2)}, u32[]{:S(2)}) collective-permute-start(f32[8,128,128]{2,1,0:T(8,128)S(1)} %get-tuple-element.17._.y_ref), channel_id=1, source_target_pairs={{0,15},{1,2},{2,1},{3,4},{4,3},{5,6},{6,5},{7,8},{8,7},{9,10},{10,... | collective-permute-start | bytes 1572872 | tf_op jit(solution)/shard_map/ppermute | solution.py:341
  43.7 10.4 %collective-permute-start = (f32[8,128,128]{2,1,0:T(8,128)S(1)}, f32[8,128,128]{2,1,0:T(8,128)S(1)}, u32[]{:S(2)}, u32[]{:S(2)}) collective-permute-start(f32[8,128,128]{2,1,0:T(8,128)S(1)} %get-tuple-element.15.y_ref), channel_id=1, source_target_pairs={{0,1},{1,0},{2,3},{3,2},{4,5},{5,4},{6,7},{7,6},{8,9},{9,8},{10,11... | collective-permute-start | bytes 1572872 | tf_op jit(solution)/shard_map/ppermute | solution.py:340
  43.7 12.8 %collective-permute-start.1 = (f32[8,128,128]{2,1,0:T(8,128)S(1)}, f32[8,128,128]{2,1,0:T(8,128)S(1)}, u32[]{:S(2)}, u32[]{:S(2)}) collective-permute-start(f32[8,128,128]{2,1,0:T(8,128)S(1)} %get-tuple-element.15.y_ref), channel_id=1, source_target_pairs={{0,15},{1,2},{2,1},{3,4},{4,3},{5,6},{6,5},{7,8},{8,7},{9,10},{10,... | collective-permute-start | bytes 1572872 | tf_op jit(solution)/shard_map/ppermute | solution.py:341
  51.5 8.2 %collective-permute-start.8 = (f32[8,128,128]{2,1,0:T(8,128)S(1)}, f32[8,128,128]{2,1,0:T(8,128)S(1)}, u32[]{:S(2)}, u32[]{:S(2)}) collective-permute-start(f32[8,128,128]{2,1,0:T(8,128)S(1)} %shard_map.101.y_ref), channel_id=1, source_target_pairs={{0,1},{1,0},{2,3},{3,2},{4,5},{5,4},{6,7},{7,6},{8,9},{9,8},{10,11... | collective-permute-start | bytes 1572872 | tf_op jit(solution)/shard_map/ppermute | solution.py:340
  54.1 8.6 %collective-permute-start.9 = (f32[8,128,128]{2,1,0:T(8,128)S(1)}, f32[8,128,128]{2,1,0:T(8,128)S(1)}, u32[]{:S(2)}, u32[]{:S(2)}) collective-permute-start(f32[8,128,128]{2,1,0:T(8,128)S(1)} %shard_map.101.y_ref), channel_id=1, source_target_pairs={{0,15},{1,2},{2,1},{3,4},{4,3},{5,6},{6,5},{7,8},{8,7},{9,10},{10,... | collective-permute-start | bytes 1572872 | tf_op jit(solution)/shard_map/ppermute | solution.py:341
  57.1 8.4 %collective-permute-start.2 = (f32[8,128,128]{2,1,0:T(8,128)S(1)}, f32[8,128,128]{2,1,0:T(8,128)S(1)}, u32[]{:S(2)}, u32[]{:S(2)}) collective-permute-start(f32[8,128,128]{2,1,0:T(8,128)S(1)} %shard_map.96.y_ref), channel_id=1, source_target_pairs={{0,1},{1,0},{2,3},{3,2},{4,5},{5,4},{6,7},{7,6},{8,9},{9,8},{10,11... | collective-permute-start | bytes 1572872 | tf_op jit(solution)/shard_map/ppermute | solution.py:340
  59.7 8.6 %collective-permute-start.3 = (f32[8,128,128]{2,1,0:T(8,128)S(1)}, f32[8,128,128]{2,1,0:T(8,128)S(1)}, u32[]{:S(2)}, u32[]{:S(2)}) collective-permute-start(f32[8,128,128]{2,1,0:T(8,128)S(1)} %shard_map.96.y_ref), channel_id=1, source_target_pairs={{0,15},{1,2},{2,1},{3,4},{4,3},{5,6},{6,5},{7,8},{8,7},{9,10},{10,... | collective-permute-start | bytes 1572872 | tf_op jit(solution)/shard_map/ppermute | solution.py:341
  63.2 7.9 %collective-permute-start.10 = (f32[8,128,128]{2,1,0:T(8,128)S(1)}, f32[8,128,128]{2,1,0:T(8,128)S(1)}, u32[]{:S(2)}, u32[]{:S(2)}) collective-permute-start(f32[8,128,128]{2,1,0:T(8,128)S(1)} %shard_map.103.y_ref), channel_id=1, source_target_pairs={{0,1},{1,0},{2,3},{3,2},{4,5},{5,4},{6,7},{7,6},{8,9},{9,8},{10,11... | collective-permute-start | bytes 1572872 | tf_op jit(solution)/shard_map/ppermute | solution.py:340
  65.5 8.6 %collective-permute-start.11 = (f32[8,128,128]{2,1,0:T(8,128)S(1)}, f32[8,128,128]{2,1,0:T(8,128)S(1)}, u32[]{:S(2)}, u32[]{:S(2)}) collective-permute-start(f32[8,128,128]{2,1,0:T(8,128)S(1)} %shard_map.103.y_ref), channel_id=1, source_target_pairs={{0,15},{1,2},{2,1},{3,4},{4,3},{5,6},{6,5},{7,8},{8,7},{9,10},{10,... | collective-permute-start | bytes 1572872 | tf_op jit(solution)/shard_map/ppermute | solution.py:341
  68.9 5.8 %collective-permute-start.4 = (f32[8,128,128]{2,1,0:T(8,128)S(1)}, f32[8,128,128]{2,1,0:T(8,128)S(1)}, u32[]{:S(2)}, u32[]{:S(2)}) collective-permute-start(f32[8,128,128]{2,1,0:T(8,128)S(1)} %shard_map.98.y_ref), channel_id=1, source_target_pairs={{0,1},{1,0},{2,3},{3,2},{4,5},{5,4},{6,7},{7,6},{8,9},{9,8},{10,11... | collective-permute-start | bytes 1572872 | tf_op jit(solution)/shard_map/ppermute | solution.py:340
  71.1 8.6 %collective-permute-start.5 = (f32[8,128,128]{2,1,0:T(8,128)S(1)}, f32[8,128,128]{2,1,0:T(8,128)S(1)}, u32[]{:S(2)}, u32[]{:S(2)}) collective-permute-start(f32[8,128,128]{2,1,0:T(8,128)S(1)} %shard_map.98.y_ref), channel_id=1, source_target_pairs={{0,15},{1,2},{2,1},{3,4},{4,3},{5,6},{6,5},{7,8},{8,7},{9,10},{10,... | collective-permute-start | bytes 1572872 | tf_op jit(solution)/shard_map/ppermute | solution.py:341
  75.9 26.1 %copy-start.4 = (bf16[8,256,256]{2,1,0:T(8,128)(2,1)S(1)}, bf16[8,256,256]{2,1,0:T(8,128)(2,1)}, u32[]{:S(2)}) copy-start(bf16[8,256,256]{2,1,0:T(8,128)(2,1)} %constant.25.clone.high_ref) | copy-start | bytes 3145732
  75.9 26.1 %copy-start.5 = (bf16[8,256,256]{2,1,0:T(8,128)(2,1)S(1)}, bf16[8,256,256]{2,1,0:T(8,128)(2,1)}, u32[]{:S(2)}) copy-start(bf16[8,256,256]{2,1,0:T(8,128)(2,1)} %constant.26.clone.low_ref) | copy-start | bytes 3145732

commit v7 on v6

--- a/solution.py
+++ b/solution.py
@@ -160,7 +160,7 @@
 def forward_kernel(here_ref, x_ref, out_ref):
     places = places_of(here_ref)
 
-    @pl.loop(0, HALF // CHUNK)
+    @pl.loop(0, HALF // CHUNK, unroll=True)
     def _(step):
         row = pl.multiple_of(step * CHUNK, CHUNK)
         series = [x_ref[steps_at(places, q, row)] * BLOCK_GROWTH[q] for q in range(16)]
@@ -174,7 +174,7 @@
     for c in range(CLASSES):
         v_ref[c] = table_product(high_ref[c], low_ref[c], y_ref[places[c]])
 
-    @pl.loop(0, HALF // CHUNK)
+    @pl.loop(0, HALF // CHUNK, unroll=True)
     def _(step):
         row = pl.multiple_of(step * CHUNK, CHUNK)
         pairs = [

time: 123 us -> 123 us (level)
  no operation moved by 1% of the time
where the time goes in v7:
time: 123 us
  blocking collectives  82 us (67%)
  waiting for transfers between devices  14.3 us (12%)
  Pallas kernels  13.6 us (11%)
  starting transfers between devices  11.9 us (10%)
    all_to_all x4, blocking collectives, exchange(): lax.all_to_all(value, ('tm', 'space'), 0, 0, tiled=True, axis_index_group...  82 us
    ppermute x6, waiting for transfers between devices, per_device(): far = lax.ppermute(state, 'space', off_chip)  14.2 us
    ppermute x6, starting transfers between devices, per_device(): pair = lax.ppermute(state, 'space', on_chip)  9.95 us
    pallas_call x6, Pallas kernels, per_device(): call(functools.partial(near_kernel, part, sweep), STATE, whole(7), 2 * 10...  7.09 us
    pallas_call x6, Pallas kernels, per_device(): call(functools.partial(far_kernel, part, sweep), STEPS if last else STATE...  3.27 us
  transfers between devices with their start and end apart: 12, of which 6 were waited for; matrix products, arithmetic and copies ran while one was open for 0% of the time, Pallas kernels for 9%

profile of v7, /device:TPU:6, one launch (start us, length us, event | category | flops | bytes accessed | tf_op | source)
XLA Modules:
  0.0 122.9 jit_solution(1938045103986815898)
XLA Ops:
  0.0 22.3 %all_to_all.20.x_ref = f32[8,256,128]{2,1,0:T(8,128)S(1)} all-to-all(f32[8,256,128]{2,1,0:T(8,128)} %param.9), channel_id=1, replica_groups={{0,64,32,96,48,112,16,80},{81,17,113,49,97,33,65,1},{2,66,34,98,50,114,..., dimensions={0} | all-to-all | bytes 2097152 | tf_op jit(solution)/shard_map/all_to_all | solution.py:309
  22.6 18.9 %all_to_all.21.series_ref = f32[8,256,128]{2,1,0:T(8,128)S(1)} all-to-all(f32[8,256,128]{2,1,0:T(8,128)S(1)} %shard_map.91), channel_id=1, replica_groups={{0,64,32,96,48,112,16,80},{81,17,113,49,97,33,65,1},{2,66,34,98,50,114,..., dimensions={0} | all-to-all | bytes 2097152 | tf_op jit(solution)/shard_map/all_to_all | solution.py:309
  42.1 0.9 collective-permute-start.7
  43.7 1.0 collective-permute-start.1
  44.6 1.0 shard_map.94
  45.7 1.2 shard_map.100.base_ref
  46.9 4.0 %collective-permute-done.7.far_ref = f32[8,128,128]{2,1,0:T(8,128)S(1)} collective-permute-done((f32[8,128,128]{2,1,0:T(8,128)S(1)}, f32[8,128,128]{2,1,0:T(8,128)S(1)}, u32[]{:S(2)}, u32[]{:S(2)}) %collective-permute-start.7) | collective-permute-done | bytes 524320 | tf_op jit(solution)/shard_map/ppermute | solution.py:341
  51.4 2.6 %collective-permute-start.8 = (f32[8,128,128]{2,1,0:T(8,128)S(1)}, f32[8,128,128]{2,1,0:T(8,128)S(1)}, u32[]{:S(2)}, u32[]{:S(2)}) collective-permute-start(f32[8,128,128]{2,1,0:T(8,128)S(1)} %shard_map.101.y_ref), channel_id=1, source_target_pairs={{0,1},{1,0},{2,3},{3,2},{4,5},{5,4},{6,7},{7,6},{8,9},{9,8},{10,11... | collective-permute-start | bytes 1572872 | tf_op jit(solution)/shard_map/ppermute | solution.py:340
  54.0 1.2 shard_map.95.base_ref
  55.2 1.3 %collective-permute-done.1.far_ref = f32[8,128,128]{2,1,0:T(8,128)S(1)} collective-permute-done((f32[8,128,128]{2,1,0:T(8,128)S(1)}, f32[8,128,128]{2,1,0:T(8,128)S(1)}, u32[]{:S(2)}, u32[]{:S(2)}) %collective-permute-start.1) | collective-permute-done | bytes 524320 | tf_op jit(solution)/shard_map/ppermute | solution.py:341
  57.0 2.6 %collective-permute-start.2 = (f32[8,128,128]{2,1,0:T(8,128)S(1)}, f32[8,128,128]{2,1,0:T(8,128)S(1)}, u32[]{:S(2)}, u32[]{:S(2)}) collective-permute-start(f32[8,128,128]{2,1,0:T(8,128)S(1)} %shard_map.96.y_ref), channel_id=1, source_target_pairs={{0,1},{1,0},{2,3},{3,2},{4,5},{5,4},{6,7},{7,6},{8,9},{9,8},{10,11... | collective-permute-start | bytes 1572872 | tf_op jit(solution)/shard_map/ppermute | solution.py:340
  59.6 1.2 shard_map.102.base_ref
  60.8 1.8 %collective-permute-done.9.far_ref = f32[8,128,128]{2,1,0:T(8,128)S(1)} collective-permute-done((f32[8,128,128]{2,1,0:T(8,128)S(1)}, f32[8,128,128]{2,1,0:T(8,128)S(1)}, u32[]{:S(2)}, u32[]{:S(2)}) %collective-permute-start.9) | collective-permute-done | bytes 524320 | tf_op jit(solution)/shard_map/ppermute | solution.py:341
  63.2 2.3 %collective-permute-start.10 = (f32[8,128,128]{2,1,0:T(8,128)S(1)}, f32[8,128,128]{2,1,0:T(8,128)S(1)}, u32[]{:S(2)}, u32[]{:S(2)}) collective-permute-start(f32[8,128,128]{2,1,0:T(8,128)S(1)} %shard_map.103.y_ref), channel_id=1, source_target_pairs={{0,1},{1,0},{2,3},{3,2},{4,5},{5,4},{6,7},{7,6},{8,9},{9,8},{10,11... | collective-permute-start | bytes 1572872 | tf_op jit(solution)/shard_map/ppermute | solution.py:340
  65.4 1.2 shard_map.97.base_ref
  66.6 1.6 %collective-permute-done.3.far_ref = f32[8,128,128]{2,1,0:T(8,128)S(1)} collective-permute-done((f32[8,128,128]{2,1,0:T(8,128)S(1)}, f32[8,128,128]{2,1,0:T(8,128)S(1)}, u32[]{:S(2)}, u32[]{:S(2)}) %collective-permute-start.3) | collective-permute-done | bytes 524320 | tf_op jit(solution)/shard_map/ppermute | solution.py:341
  68.8 2.3 %collective-permute-start.4 = (f32[8,128,128]{2,1,0:T(8,128)S(1)}, f32[8,128,128]{2,1,0:T(8,128)S(1)}, u32[]{:S(2)}, u32[]{:S(2)}) collective-permute-start(f32[8,128,128]{2,1,0:T(8,128)S(1)} %shard_map.98.y_ref), channel_id=1, source_target_pairs={{0,1},{1,0},{2,3},{3,2},{4,5},{5,4},{6,7},{7,6},{8,9},{9,8},{10,11... | collective-permute-start | bytes 1572872 | tf_op jit(solution)/shard_map/ppermute | solution.py:340
  71.1 1.2 shard_map.104.base_ref
  72.3 1.8 %collective-permute-done.11.far_ref = f32[8,128,128]{2,1,0:T(8,128)S(1)} collective-permute-done((f32[8,128,128]{2,1,0:T(8,128)S(1)}, f32[8,128,128]{2,1,0:T(8,128)S(1)}, u32[]{:S(2)}, u32[]{:S(2)}) %collective-permute-start.11) | collective-permute-done | bytes 524320 | tf_op jit(solution)/shard_map/ppermute | solution.py:341
  74.6 1.2 shard_map.99.base_ref
  75.8 3.8 %collective-permute-done.5.far_ref = f32[8,128,128]{2,1,0:T(8,128)S(1)} collective-permute-done((f32[8,128,128]{2,1,0:T(8,128)S(1)}, f32[8,128,128]{2,1,0:T(8,128)S(1)}, u32[]{:S(2)}, u32[]{:S(2)}) %collective-permute-start.5) | collective-permute-done | bytes 524320 | tf_op jit(solution)/shard_map/ppermute | solution.py:341
  80.2 21.7 %all_to_all.22.y_ref = f32[8,256,128]{2,1,0:T(8,128)S(1)} all-to-all(f32[8,256,128]{2,1,0:T(8,128)S(1)} %shard_map.106), channel_id=1, replica_groups={{0,64,32,96,48,112,16,80},{81,17,113,49,97,33,65,1},{2,66,34,98,50,114,..., dimensions={0} | all-to-all | bytes 2097152 | tf_op jit(solution)/shard_map/all_to_all | solution.py:309
  102.9 19.1 %all_to_all.23 = f32[8,256,128]{2,1,0:T(8,128)S(1)} all-to-all(f32[8,256,128]{2,1,0:T(8,128)S(1)} %shard_map.107), channel_id=1, replica_groups={{0,64,32,96,48,112,16,80},{81,17,113,49,97,33,65,1},{2,66,34,98,50,114,..., dimensions={0} | all-to-all | bytes 2097152 | tf_op jit(solution)/shard_map/all_to_all | solution.py:309
  122.0 1.0 copy.11
  (38 shorter events, 5.7 us)
Async XLA Ops:
  0.0 41.5 %copy-start.1 = (bf16[8,256,256]{2,1,0:T(8,128)(2,1)S(1)}, bf16[8,256,256]{2,1,0:T(8,128)(2,1)}, u32[]{:S(2)}) copy-start(bf16[8,256,256]{2,1,0:T(8,128)(2,1)} %constant.23.clone.high_ref) | copy-start | bytes 3145732
  0.0 41.5 %copy-start.2 = (bf16[8,256,256]{2,1,0:T(8,128)(2,1)S(1)}, bf16[8,256,256]{2,1,0:T(8,128)(2,1)}, u32[]{:S(2)}) copy-start(bf16[8,256,256]{2,1,0:T(8,128)(2,1)} %constant.24.clone.low_ref) | copy-start | bytes 3145732
  0.0 41.5 %copy-start = (f32[2,3,64,128]{3,2,1,0:T(8,128)S(1)}, f32[2,3,64,128]{3,2,1,0:T(8,128)}, u32[]{:S(2)}) copy-start(f32[2,3,64,128]{3,2,1,0:T(8,128)} %constant.27.clone.shift_ref) | copy-start | bytes 589828
  0.0 41.5 %copy-start.7 = (f32[4]{0:T(128)S(1)}, f32[4]{0:T(128)}, u32[]{:S(2)}) copy-start(f32[4]{0:T(128)} %rates_ref.27) | copy-start | bytes 52
  41.5 3.1 %copy-start.3 = (f32[8,7,128,128]{3,2,1,0:T(8,128)S(1)}, f32[8,7,128,128]{3,2,1,0:T(8,128)}, u32[]{:S(2)}) copy-start(f32[8,7,128,128]{3,2,1,0:T(8,128)} %blocks_ref.1) | copy-start | bytes 11010052
  42.0 3.6 %copy-start.6 = (s32[8,7]{1,0:T(8,128)S(1)}, s32[8,7]{1,0:T(8,128)}, u32[]{:S(2)}) copy-start(s32[8,7]{1,0:T(8,128)} %nb_ref.23) | copy-start | bytes 676
  42.1 3.6 %collective-permute-start.6 = (f32[8,128,128]{2,1,0:T(8,128)S(1)}, f32[8,128,128]{2,1,0:T(8,128)S(1)}, u32[]{:S(2)}, u32[]{:S(2)}) collective-permute-start(f32[8,128,128]{2,1,0:T(8,128)S(1)} %get-tuple-element.17._.y_ref), channel_id=1, source_target_pairs={{0,1},{1,0},{2,3},{3,2},{4,5},{5,4},{6,7},{7,6},{8,9},{9,8},{10,11... | collective-permute-start | bytes 1572872 | tf_op jit(solution)/shard_map/ppermute | solution.py:340
  42.1 8.7 %collective-permute-start.7 = (f32[8,128,128]{2,1,0:T(8,128)S(1)}, f32[8,128,128]{2,1,0:T(8,128)S(1)}, u32[]{:S(2)}, u32[]{:S(2)}) collective-permute-start(f32[8,128,128]{2,1,0:T(8,128)S(1)} %get-tuple-element.17._.y_ref), channel_id=1, source_target_pairs={{0,15},{1,2},{2,1},{3,4},{4,3},{5,6},{6,5},{7,8},{8,7},{9,10},{10,... | collective-permute-start | bytes 1572872 | tf_op jit(solution)/shard_map/ppermute | solution.py:341
  43.6 10.4 %collective-permute-start = (f32[8,128,128]{2,1,0:T(8,128)S(1)}, f32[8,128,128]{2,1,0:T(8,128)S(1)}, u32[]{:S(2)}, u32[]{:S(2)}) collective-permute-start(f32[8,128,128]{2,1,0:T(8,128)S(1)} %get-tuple-element.15.y_ref), channel_id=1, source_target_pairs={{0,1},{1,0},{2,3},{3,2},{4,5},{5,4},{6,7},{7,6},{8,9},{9,8},{10,11... | collective-permute-start | bytes 1572872 | tf_op jit(solution)/shard_map/ppermute | solution.py:340
  43.7 12.8 %collective-permute-start.1 = (f32[8,128,128]{2,1,0:T(8,128)S(1)}, f32[8,128,128]{2,1,0:T(8,128)S(1)}, u32[]{:S(2)}, u32[]{:S(2)}) collective-permute-start(f32[8,128,128]{2,1,0:T(8,128)S(1)} %get-tuple-element.15.y_ref), channel_id=1, source_target_pairs={{0,15},{1,2},{2,1},{3,4},{4,3},{5,6},{6,5},{7,8},{8,7},{9,10},{10,... | collective-permute-start | bytes 1572872 | tf_op jit(solution)/shard_map/ppermute | solution.py:341
  51.4 8.2 %collective-permute-start.8 = (f32[8,128,128]{2,1,0:T(8,128)S(1)}, f32[8,128,128]{2,1,0:T(8,128)S(1)}, u32[]{:S(2)}, u32[]{:S(2)}) collective-permute-start(f32[8,128,128]{2,1,0:T(8,128)S(1)} %shard_map.101.y_ref), channel_id=1, source_target_pairs={{0,1},{1,0},{2,3},{3,2},{4,5},{5,4},{6,7},{7,6},{8,9},{9,8},{10,11... | collective-permute-start | bytes 1572872 | tf_op jit(solution)/shard_map/ppermute | solution.py:340
  54.0 8.6 %collective-permute-start.9 = (f32[8,128,128]{2,1,0:T(8,128)S(1)}, f32[8,128,128]{2,1,0:T(8,128)S(1)}, u32[]{:S(2)}, u32[]{:S(2)}) collective-permute-start(f32[8,128,128]{2,1,0:T(8,128)S(1)} %shard_map.101.y_ref), channel_id=1, source_target_pairs={{0,15},{1,2},{2,1},{3,4},{4,3},{5,6},{6,5},{7,8},{8,7},{9,10},{10,... | collective-permute-start | bytes 1572872 | tf_op jit(solution)/shard_map/ppermute | solution.py:341
  57.0 8.4 %collective-permute-start.2 = (f32[8,128,128]{2,1,0:T(8,128)S(1)}, f32[8,128,128]{2,1,0:T(8,128)S(1)}, u32[]{:S(2)}, u32[]{:S(2)}) collective-permute-start(f32[8,128,128]{2,1,0:T(8,128)S(1)} %shard_map.96.y_ref), channel_id=1, source_target_pairs={{0,1},{1,0},{2,3},{3,2},{4,5},{5,4},{6,7},{7,6},{8,9},{9,8},{10,11... | collective-permute-start | bytes 1572872 | tf_op jit(solution)/shard_map/ppermute | solution.py:340
  59.6 8.6 %collective-permute-start.3 = (f32[8,128,128]{2,1,0:T(8,128)S(1)}, f32[8,128,128]{2,1,0:T(8,128)S(1)}, u32[]{:S(2)}, u32[]{:S(2)}) collective-permute-start(f32[8,128,128]{2,1,0:T(8,128)S(1)} %shard_map.96.y_ref), channel_id=1, source_target_pairs={{0,15},{1,2},{2,1},{3,4},{4,3},{5,6},{6,5},{7,8},{8,7},{9,10},{10,... | collective-permute-start | bytes 1572872 | tf_op jit(solution)/shard_map/ppermute | solution.py:341
  63.2 7.9 %collective-permute-start.10 = (f32[8,128,128]{2,1,0:T(8,128)S(1)}, f32[8,128,128]{2,1,0:T(8,128)S(1)}, u32[]{:S(2)}, u32[]{:S(2)}) collective-permute-start(f32[8,128,128]{2,1,0:T(8,128)S(1)} %shard_map.103.y_ref), channel_id=1, source_target_pairs={{0,1},{1,0},{2,3},{3,2},{4,5},{5,4},{6,7},{7,6},{8,9},{9,8},{10,11... | collective-permute-start | bytes 1572872 | tf_op jit(solution)/shard_map/ppermute | solution.py:340
  65.4 8.6 %collective-permute-start.11 = (f32[8,128,128]{2,1,0:T(8,128)S(1)}, f32[8,128,128]{2,1,0:T(8,128)S(1)}, u32[]{:S(2)}, u32[]{:S(2)}) collective-permute-start(f32[8,128,128]{2,1,0:T(8,128)S(1)} %shard_map.103.y_ref), channel_id=1, source_target_pairs={{0,15},{1,2},{2,1},{3,4},{4,3},{5,6},{6,5},{7,8},{8,7},{9,10},{10,... | collective-permute-start | bytes 1572872 | tf_op jit(solution)/shard_map/ppermute | solution.py:341
  68.8 5.8 %collective-permute-start.4 = (f32[8,128,128]{2,1,0:T(8,128)S(1)}, f32[8,128,128]{2,1,0:T(8,128)S(1)}, u32[]{:S(2)}, u32[]{:S(2)}) collective-permute-start(f32[8,128,128]{2,1,0:T(8,128)S(1)} %shard_map.98.y_ref), channel_id=1, source_target_pairs={{0,1},{1,0},{2,3},{3,2},{4,5},{5,4},{6,7},{7,6},{8,9},{9,8},{10,11... | collective-permute-start | bytes 1572872 | tf_op jit(solution)/shard_map/ppermute | solution.py:340
  71.1 8.6 %collective-permute-start.5 = (f32[8,128,128]{2,1,0:T(8,128)S(1)}, f32[8,128,128]{2,1,0:T(8,128)S(1)}, u32[]{:S(2)}, u32[]{:S(2)}) collective-permute-start(f32[8,128,128]{2,1,0:T(8,128)S(1)} %shard_map.98.y_ref), channel_id=1, source_target_pairs={{0,15},{1,2},{2,1},{3,4},{4,3},{5,6},{6,5},{7,8},{8,7},{9,10},{10,... | collective-permute-start | bytes 1572872 | tf_op jit(solution)/shard_map/ppermute | solution.py:341
  75.8 26.1 %copy-start.4 = (bf16[8,256,256]{2,1,0:T(8,128)(2,1)S(1)}, bf16[8,256,256]{2,1,0:T(8,128)(2,1)}, u32[]{:S(2)}) copy-start(bf16[8,256,256]{2,1,0:T(8,128)(2,1)} %constant.25.clone.high_ref) | copy-start | bytes 3145732
  75.8 26.1 %copy-start.5 = (bf16[8,256,256]{2,1,0:T(8,128)(2,1)S(1)}, bf16[8,256,256]{2,1,0:T(8,128)(2,1)}, u32[]{:S(2)}) copy-start(bf16[8,256,256]{2,1,0:T(8,128)(2,1)} %constant.26.clone.low_ref) | copy-start | bytes 3145732
